TPU v7x, 32 devices: a whole 2x2x4 slice. The times are simulated.
32 devices in a mesh: fsdp: 16 (over z, y, core), tensor: 2 (over x).
Axes of the slice: x: 2, y: 2, z: 4, core: 2. Of those that a mesh axis runs over, the one named last changes fastest.
Arguments:
- tokens: bfloat16 [2048, 8192], P('fsdp'), may hold values from -6 to 6
- cotangent: bfloat16 [2048, 8192], P('fsdp'), may hold values from -1.5 to 1.5
- gate_blocks: bfloat16 [2, 32, 128, 128], P('tensor', 'fsdp'), may hold values from -0.75 to 0.75
- up_blocks: bfloat16 [2, 32, 128, 128], P('tensor', 'fsdp'), may hold values from -0.75 to 0.75
- down_blocks: bfloat16 [2, 32, 128, 128], P('tensor', 'fsdp'), may hold values from -0.75 to 0.75
- gate_where: int32 [2, 32], P('tensor'), may hold values from 0 to 3583, as said below
- up_where: int32 [2, 32], P('tensor'), may hold values from 0 to 3583, as said below
- down_where: int32 [2, 32], P('tensor'), may hold values from 0 to 3583, as said below
- block_counts: int32 [3, 2], P(None, 'tensor'), may hold values from 16 to 32, as said below
Outputs:
- outputs: bfloat16 [2048, 8192], P('fsdp', 'tensor')
- input_grads: bfloat16 [2048, 8192], P('fsdp', 'tensor')
- gate_grads: bfloat16 [2, 32, 128, 128], P('tensor', 'fsdp')
- up_grads: bfloat16 [2, 32, 128, 128], P('tensor', 'fsdp')
- down_grads: bfloat16 [2, 32, 128, 128], P('tensor', 'fsdp')
Inputs may be any that keep to these rules, and one draw needn't show every extreme that they name: Within one group of hidden units the 32 positions of gate_where are distinct. Within one group of hidden units the 32 positions of up_where are distinct. Within one group of hidden units the 32 positions of down_where are distinct. `block_counts`: for each matrix some group has all 32 slots live.
All inputs are finite; a program needn't handle non-finite values.
Results may differ from a plain program's by a relative error of at most 0.015.
Values may be sent and summed in bfloat16 or wider, within the bound.
No kernel may reach another device: no remote copies, remote signals or barrier semaphores. Data moves between devices by JAX's collectives and lax.ppermute only.
A program may use at most 128 MiB of HBM per device.

v0:
```python
import jax
import jax.numpy as jnp
from jax import lax
from jax.sharding import PartitionSpec as P

FF = 14336


def blockwise(pattern, left_side, right_side):
    return jnp.einsum(pattern, left_side, right_side, preferred_element_type=jnp.float32)


def collect(block_terms, segment_ids, segments):
    return jax.ops.segment_sum(block_terms, segment_ids, num_segments=segments)


def shards(
    tokens,
    cotangent,
    gate_blocks,
    up_blocks,
    down_blocks,
    gate_where,
    up_where,
    down_where,
    block_counts,
):
    tok_rows, tok_width = tokens.shape
    row_blocks = tok_width // 128
    col_blocks = FF // (128 * lax.axis_size("tensor"))
    slot_count = gate_where.shape[1]
    rows_blocked = tokens.reshape(tok_rows, row_blocks, 128).transpose(1, 0, 2)
    grad_blocked = cotangent.reshape(tok_rows, row_blocks, 128).transpose(1, 0, 2)
    live_slots = lax.broadcasted_iota(jnp.int32, (3, slot_count), 1) < block_counts
    live_blocks = live_slots.astype(jnp.bfloat16)[:, :, None, None]
    live_parts = live_slots.astype(jnp.float32)[:, :, None, None]
    gate_all, up_all, down_all = (
        lax.all_gather(gate_blocks, "fsdp", axis=1, tiled=True),
        lax.all_gather(up_blocks, "fsdp", axis=1, tiled=True),
        lax.all_gather(down_blocks, "fsdp", axis=1, tiled=True),
    )
    gate_eff = gate_all[0] * live_blocks[0]
    up_eff = up_all[0] * live_blocks[1]
    gate_row = gate_where[0] // col_blocks
    gate_col = gate_where[0] % col_blocks
    up_row = up_where[0] // col_blocks
    up_col = up_where[0] % col_blocks
    down_ff = down_where[0] // row_blocks
    down_d = down_where[0] % row_blocks
    rows_gate = jnp.take(rows_blocked, gate_row, axis=0)
    rows_up = jnp.take(rows_blocked, up_row, axis=0)
    gate_val = collect(blockwise("ntk,nkj->ntj", rows_gate, gate_eff), gate_col, col_blocks)
    up_val = collect(blockwise("ntk,nkj->ntj", rows_up, up_eff), up_col, col_blocks)
    down_eff = down_all[0] * live_blocks[2]
    gate_sig = jax.nn.sigmoid(gate_val)
    silu_gate = gate_val * gate_sig
    hidden = (silu_gate * up_val).astype(jnp.bfloat16)
    hidden_sel = jnp.take(hidden, down_ff, axis=0)
    grad_sel = jnp.take(grad_blocked, down_d, axis=0)
    output_term = collect(blockwise("ntk,nkj->ntj", hidden_sel, down_eff), down_d, row_blocks)
    output_sum = lax.psum_scatter(
        output_term.astype(jnp.bfloat16), "tensor", scatter_dimension=0, tiled=True
    ).astype(jnp.float32)
    hidden_grad = collect(blockwise("ntj,nkj->ntk", grad_sel, down_eff), down_ff, col_blocks)
    down_part = blockwise("ntk,ntj->nkj", hidden_sel, grad_sel) * live_parts[2]
    gate_delta = (hidden_grad * up_val * gate_sig * (1.0 + gate_val * (1.0 - gate_sig))).astype(
        jnp.bfloat16
    )
    up_delta = (hidden_grad * silu_gate).astype(jnp.bfloat16)
    delta_gate = jnp.take(gate_delta, gate_col, axis=0)
    delta_up = jnp.take(up_delta, up_col, axis=0)
    input_term = collect(blockwise("ntj,nkj->ntk", delta_gate, gate_eff), gate_row, row_blocks)
    input_term = input_term + collect(
        blockwise("ntj,nkj->ntk", delta_up, up_eff), up_row, row_blocks
    )
    gate_part = blockwise("ntk,ntj->nkj", rows_gate, delta_gate) * live_parts[0]
    up_part = blockwise("ntk,ntj->nkj", rows_up, delta_up) * live_parts[1]
    gate_sum, up_sum, down_sum = (
        lax.psum_scatter(
            gate_part[None].astype(jnp.bfloat16), "fsdp", scatter_dimension=1, tiled=True
        ).astype(jnp.float32),
        lax.psum_scatter(
            up_part[None].astype(jnp.bfloat16), "fsdp", scatter_dimension=1, tiled=True
        ).astype(jnp.float32),
        lax.psum_scatter(
            down_part[None].astype(jnp.bfloat16), "fsdp", scatter_dimension=1, tiled=True
        ).astype(jnp.float32),
    )
    input_sum = lax.psum_scatter(
        input_term.astype(jnp.bfloat16), "tensor", scatter_dimension=0, tiled=True
    ).astype(jnp.float32)
    outputs = output_sum.transpose(1, 0, 2).reshape(tok_rows, -1).astype(jnp.bfloat16)
    input_grads = input_sum.transpose(1, 0, 2).reshape(tok_rows, -1).astype(jnp.bfloat16)
    return (
        outputs,
        input_grads,
        gate_sum.astype(jnp.bfloat16),
        up_sum.astype(jnp.bfloat16),
        down_sum.astype(jnp.bfloat16),
    )


def solution(mesh):
    placed = (
        P("fsdp", None),
        P("fsdp", None),
        P("tensor", "fsdp", None, None),
        P("tensor", "fsdp", None, None),
        P("tensor", "fsdp", None, None),
        P("tensor", None),
        P("tensor", None),
        P("tensor", None),
        P(None, "tensor"),
    )
    return jax.shard_map(
        shards,
        mesh=mesh,
        in_specs=placed,
        out_specs=(
            P("fsdp", "tensor"),
            P("fsdp", "tensor"),
            P("tensor", "fsdp", None, None),
            P("tensor", "fsdp", None, None),
            P("tensor", "fsdp", None, None),
        ),
        check_vma=False,
    )
```

profile of v0, /device:TPU:0, one launch (start us, length us, event | category | flops | bytes accessed | tf_op | source)
XLA Modules:
  0.0 416.9 jit_solution(4692210032180908116)
XLA Ops:
  7.2 0.0 all-gather.4.cloned.1.call-start
  7.2 0.7 all-gather.4.cloned.1.call-update
  7.9 0.0 all-gather.8.cloned.1.call-start
  7.9 0.7 all-gather.8.cloned.1.call-update
  8.6 0.0 all-gather.6.cloned.1.call-start
  8.7 0.7 all-gather.6.cloned.1.call-update
  9.4 0.0 reduce-scatter.6.cloned.1.call-start
  9.4 0.7 fusion.26
  10.1 0.7 fusion.27
  10.8 0.7 compare_and_fusion
  11.5 4.1 copy.31
  15.5 3.2 copy.32
  18.8 1.7 gather_fusion.1
  20.4 1.7 gather_fusion
  22.1 3.2 copy.37
  25.3 2.9 copy.38
  28.3 2.3 gather_fusion.3
  30.7 0.1 fusion.16
  30.8 20.1 %all-gather.4.cloned.1.call-done = bf16[1,32,128,128]{3,2,0,1:T(8,128)(2,1)} async-done(((bf16[1,2,128,128]{3,2,0,1:T(8,128)(2,1)}), bf16[1,32,128,128]{3,2,0,1:T(8,128)(2,1)}) %all-gather.4.cloned.1.call-update) | async-done | bytes 1048592 | tf_op jit(solution)/shard_map/all_gather | solution.py:38
  50.8 2.0 fusion.5
  52.9 2.3 broadcast.235.clone.1
  55.2 6.2 %scatter_fusion = f32[56,128,128]{2,1,0:T(8,128)} fusion(f32[56,128,128]{2,1,0:T(8,128)} %broadcast.235.clone.1, s32[32]{0:T(128)S(1)} %get-tuple-element.52, f32[32,128,128]{2,1,0:T(8,128)S(1)} %fusion.5), kind=kCustom, calls=%fused_computation.6 | custom fusion | flops 524288 | bytes 6291584 | tf_op jit(solution)/shard_map/scatter-add | solution.py:14
  61.4 28.5 %all-gather.8.cloned.1.call-done = bf16[1,32,128,128]{3,2,0,1:T(8,128)(2,1)} async-done(((bf16[1,2,128,128]{3,2,0,1:T(8,128)(2,1)}), bf16[1,32,128,128]{3,2,0,1:T(8,128)(2,1)}) %all-gather.8.cloned.1.call-update) | async-done | bytes 1048592 | tf_op jit(solution)/shard_map/all_gather | solution.py:40
  89.9 2.1 fusion.8
  92.0 2.2 broadcast.235.clone
  94.3 6.3 %scatter_fusion.3 = f32[56,128,128]{2,1,0:T(8,128)} fusion(f32[56,128,128]{2,1,0:T(8,128)} %broadcast.235.clone, s32[32]{0:T(128)S(1)} %get-tuple-element.50, f32[32,128,128]{2,1,0:T(8,128)S(1)} %fusion.8), kind=kCustom, calls=%fused_computation.9 | custom fusion | flops 524288 | bytes 6291584 | tf_op jit(solution)/shard_map/scatter-add | solution.py:14
  100.6 28.4 %all-gather.6.cloned.1.call-done = bf16[1,32,128,128]{3,2,0,1:T(8,128)(2,1)} async-done(((bf16[1,2,128,128]{3,2,0,1:T(8,128)(2,1)}), bf16[1,32,128,128]{3,2,0,1:T(8,128)(2,1)}) %all-gather.6.cloned.1.call-update) | async-done | bytes 1048592 | tf_op jit(solution)/shard_map/all_gather | solution.py:39
  128.9 1.7 fusion.7
  130.7 2.2 broadcast.235.clone.2
  132.9 6.2 %scatter_fusion.1 = f32[56,128,128]{2,1,0:T(8,128)} fusion(f32[56,128,128]{2,1,0:T(8,128)} %broadcast.235.clone.2, s32[32]{0:T(128)S(1)} %get-tuple-element.53, f32[32,128,128]{2,1,0:T(8,128)S(1)} %fusion.7), kind=kCustom, calls=%fused_computation.7 | custom fusion | flops 524288 | bytes 6291584 | tf_op jit(solution)/shard_map/scatter-add | solution.py:14
  139.2 6.8 %multiply_convert_fusion = (bf16[56,128,128]{2,1,0:T(8,128)(2,1)}, bf16[56,128,128]{2,1,0:T(8,128)(2,1)}, bf16[56,128,128]{2,1,0:T(8,128)(2,1)S(1)}) fusion(f32[56,128,128]{2,1,0:T(8,128)} %scatter_fusion.3, f32[56,128,128]{2,1,0:T(8,128)} %scatter_fusion, f32[56,128,128]{2,1,0:T(8,128)} %scatter_fusion.1), kind=kLoop, calls=%fused_computation.13 | loop fusion | flops 13762560 | bytes 16515072 | tf_op jit(solution)/shard_map/convert_element_type | solution.py:69
  145.9 1.7 gather_fusion.2
  147.6 1.7 fusion.9
  149.3 2.4 broadcast.233.clone
  151.8 6.2 %scatter_fusion.2 = f32[64,128,128]{2,1,0:T(8,128)} fusion(f32[64,128,128]{2,1,0:T(8,128)} %broadcast.233.clone, s32[32]{0:T(128)S(1)} %get-tuple-element.51, f32[32,128,128]{2,1,0:T(8,128)S(1)} %fusion.9), kind=kCustom, calls=%fused_computation.8 | custom fusion | flops 524288 | bytes 6291584 | tf_op jit(solution)/shard_map/scatter-add | solution.py:14
  157.9 3.9 convert_element_type.63
  161.9 0.0 reduce-scatter.6.cloned.1.call-update
  161.9 0.2 reduce-scatter.8.cloned.1.call-start
  162.1 3.4 gather_fusion.5
  165.5 1.7 gather_fusion.4
  167.2 2.2 fusion.4
  169.5 2.6 broadcast.233.clone.1
  172.1 6.3 %scatter_fusion.4 = f32[64,128,128]{2,1,0:T(8,128)} fusion(f32[64,128,128]{2,1,0:T(8,128)} %broadcast.233.clone.1, s32[32]{0:T(128)S(1)} %get-tuple-element.25, f32[32,128,128]{2,1,0:T(8,128)S(1)} %fusion.4), kind=kCustom, calls=%fused_computation.10 | custom fusion | flops 524288 | bytes 6291584 | tf_op jit(solution)/shard_map/scatter-add | solution.py:14
  178.4 2.1 fusion.6
  180.5 2.5 broadcast.233.clone.2
  183.0 6.3 %scatter_fusion.5 = f32[64,128,128]{2,1,0:T(8,128)} fusion(f32[64,128,128]{2,1,0:T(8,128)} %broadcast.233.clone.2, s32[32]{0:T(128)S(1)} %get-tuple-element.19, f32[32,128,128]{2,1,0:T(8,128)S(1)} %fusion.6), kind=kCustom, calls=%fused_computation.11 | custom fusion | flops 524288 | bytes 6291584 | tf_op jit(solution)/shard_map/scatter-add | solution.py:14
  189.3 5.7 %add_convert_fusion = bf16[64,128,128]{2,1,0:T(8,128)(2,1)} fusion(f32[64,128,128]{2,1,0:T(8,128)} %scatter_fusion.4, f32[64,128,128]{2,1,0:T(8,128)} %scatter_fusion.5), kind=kLoop, calls=%fused_computation.12 | loop fusion | flops 2097152 | bytes 10485760 | tf_op jit(solution)/shard_map/convert_element_type | solution.py:90
  195.0 0.0 reduce-scatter.12.cloned.1.call-start
  195.1 1.1 copy-done.8
  196.2 0.3 copy-done.10
  196.5 1.6 fusion.2
  198.2 0.0 reduce-scatter.10.cloned.1.call-start
  198.3 3.1 fusion.1
  201.4 0.0 reduce-scatter.14.cloned.1.call-start
  201.5 1.6 fusion.3
  203.1 0.0 reduce-scatter.6.cloned.1.call-done
  203.2 1.6 copy.36
  204.8 1.3 copy.43
  206.1 20.8 %reduce-scatter.8.cloned.1.call-done = bf16[32,128,128]{2,1,0:T(8,128)(2,1)} async-done(((bf16[64,128,128]{2,1,0:T(8,128)(2,1)}), bf16[32,128,128]{2,1,0:T(8,128)(2,1)}) %reduce-scatter.8.cloned.1.call-update) | async-done | bytes 1048592 | tf_op jit(solution)/shard_map/reduce_scatter | solution.py:89
  226.9 1.6 copy.39
  228.5 1.3 copy.44
  229.8 58.6 %reduce-scatter.12.cloned.1.call-done = bf16[1,2,128,128]{3,2,1,0:T(8,128)(2,1)} async-done(((bf16[1,32,128,128]{3,2,1,0:T(8,128)(2,1)}), bf16[1,2,128,128]{3,2,1,0:T(8,128)(2,1)}) %reduce-scatter.12.cloned.1.call-update) | async-done | bytes 65552 | tf_op jit(solution)/shard_map/reduce_scatter | solution.py:82
  288.4 61.1 %reduce-scatter.10.cloned.1.call-done = bf16[1,2,128,128]{3,2,1,0:T(8,128)(2,1)} async-done(((bf16[1,32,128,128]{3,2,1,0:T(8,128)(2,1)}), bf16[1,2,128,128]{3,2,1,0:T(8,128)(2,1)}) %reduce-scatter.10.cloned.1.call-update) | async-done | bytes 65552 | tf_op jit(solution)/shard_map/reduce_scatter | solution.py:79
  349.4 60.6 %reduce-scatter.14.cloned.1.call-done = bf16[1,2,128,128]{3,2,1,0:T(8,128)(2,1)} async-done(((bf16[1,32,128,128]{3,2,1,0:T(8,128)(2,1)}), bf16[1,2,128,128]{3,2,1,0:T(8,128)(2,1)}) %reduce-scatter.14.cloned.1.call-update) | async-done | bytes 65552 | tf_op jit(solution)/shard_map/reduce_scatter | solution.py:85
  (38 shorter events, 0.2 us)
Async XLA Ops:
  7.2 43.7 %all-gather.4.cloned.1.call-start = ((), (), s32[]{:S(2)}) async-start(), calls=%async_computation.5 | async-start | bytes 1114112 | tf_op jit(solution)/shard_map/all_gather | solution.py:38
  7.9 82.0 %all-gather.8.cloned.1.call-start = ((), (), s32[]{:S(2)}) async-start(), calls=%async_computation.7 | async-start | bytes 1114112 | tf_op jit(solution)/shard_map/all_gather | solution.py:40
  8.6 120.3 %all-gather.6.cloned.1.call-start = ((), (), s32[]{:S(2)}) async-start(), calls=%async_computation.6 | async-start | bytes 1114112 | tf_op jit(solution)/shard_map/all_gather | solution.py:39
  9.4 193.8 %reduce-scatter.6.cloned.1.call-start = ((), (), s32[]{:S(2)}) async-start(), calls=%async_computation.8 | async-start | bytes 3145728 | tf_op jit(solution)/shard_map/reduce_scatter | solution.py:61
  18.7 1.7 copy-start.11
  25.3 2.9 copy-start.12
  28.3 2.4 copy-start.13
  30.6 59.2 %copy-start.4 = (bf16[32,128,128]{2,1,0:T(8,128)(2,1)}, bf16[32,128,128]{2,1,0:T(8,128)(2,1)S(1)}, u32[]{:S(2)}) copy-start(bf16[32,128,128]{2,1,0:T(8,128)(2,1)S(1)} %gather_fusion.3) | copy-start | bytes 3145732
  94.3 34.7 %copy-start.7 = (bf16[32,128,128]{2,1,0:T(8,128)(2,1)S(1)}, bf16[32,128,128]{2,1,0:T(8,128)(2,1)}, u32[]{:S(2)}) copy-start(bf16[32,128,128]{2,1,0:T(8,128)(2,1)} %gather_fusion.1) | copy-start | bytes 3145732
  145.9 1.7 copy-start.3
  161.9 3.6 copy-start
  161.9 65.0 %reduce-scatter.8.cloned.1.call-start = ((), (), s32[]{:S(2)}) async-start(), calls=%async_computation.9 | async-start | bytes 3145728 | tf_op jit(solution)/shard_map/reduce_scatter | solution.py:89
  162.1 5.1 %copy-start.1 = (bf16[1,32,128,128]{3,2,0,1:T(8,128)(2,1)S(1)}, bf16[1,32,128,128]{3,2,0,1:T(8,128)(2,1)}, u32[]{:S(2)}) copy-start(bf16[1,32,128,128]{3,2,0,1:T(8,128)(2,1)} %all-gather.4.cloned.1.call-done) | copy-start | bytes 3145732
  172.1 6.3 %copy-start.2 = (bf16[1,32,128,128]{3,2,0,1:T(8,128)(2,1)S(1)}, bf16[1,32,128,128]{3,2,0,1:T(8,128)(2,1)}, u32[]{:S(2)}) copy-start(bf16[1,32,128,128]{3,2,0,1:T(8,128)(2,1)} %all-gather.6.cloned.1.call-done) | copy-start | bytes 3145732
  195.0 1.2 copy-start.8
  195.0 1.5 copy-start.10
  195.0 93.3 %reduce-scatter.12.cloned.1.call-start = ((), (), s32[]{:S(2)}) async-start(), calls=%async_computation.11 | async-start | bytes 1114112 | tf_op jit(solution)/shard_map/reduce_scatter | solution.py:82
  196.5 1.7 copy-start.6
  198.2 151.2 %reduce-scatter.10.cloned.1.call-start = ((), (), s32[]{:S(2)}) async-start(), calls=%async_computation.10 | async-start | bytes 1114112 | tf_op jit(solution)/shard_map/reduce_scatter | solution.py:79
  198.3 3.2 copy-start.5
  198.3 3.2 copy-start.9
  201.4 208.6 %reduce-scatter.14.cloned.1.call-start = ((), (), s32[]{:S(2)}) async-start(), calls=%async_computation.12 | async-start | bytes 1114112 | tf_op jit(solution)/shard_map/reduce_scatter | solution.py:85
Sparse Core Ops, SparseCore 0:
  10.2 40.6 all-gather.3
  53.0 36.8 all-gather.7
  92.1 36.8 all-gather.5
  162.0 30.7 reduce-scatter.5
  195.1 31.6 reduce-scatter.7
  230.9 57.3 reduce-scatter.11
  293.0 56.3 reduce-scatter.9
  353.6 56.3 reduce-scatter.13
where the time goes:
time: 418 us; the launch traced here: 417 us
  waiting for transfers between devices  280 us (67%)
  other arithmetic  56.1 us (13%)
  local copies, waits for them, and re-layouts  47.5 us (11%)
  matrix products  18.4 us (4%)
  between operations  14.4 us (3%)
    reduce_scatter x1, waiting for transfers between devices, shards(): lax.psum_scatter(gate_part[None].astype(jnp.bfloat16), 'fsdp', scatter_di...  61.1 us
    reduce_scatter x1, waiting for transfers between devices, shards(): lax.psum_scatter(down_part[None].astype(jnp.bfloat16), 'fsdp', scatter_di...  60.6 us
    reduce_scatter x1, waiting for transfers between devices, shards(): lax.psum_scatter(up_part[None].astype(jnp.bfloat16), 'fsdp', scatter_dime...  58.6 us
    scatter-add x6, other arithmetic, collect(): return jax.ops.segment_sum(block_terms, segment_ids, num_segments=segments)  37.6 us
    all_gather x1, waiting for transfers between devices, shards(): lax.all_gather(down_blocks, 'fsdp', axis=1, tiled=True)  28.5 us
    all_gather x1, waiting for transfers between devices, shards(): lax.all_gather(up_blocks, 'fsdp', axis=1, tiled=True)  28.4 us
    reduce_scatter x1, waiting for transfers between devices, shards(): lax.psum_scatter(input_term.astype(jnp.bfloat16), 'tensor', scatter_dimen...  20.8 us
    all_gather x1, waiting for transfers between devices, shards(): lax.all_gather(gate_blocks, 'fsdp', axis=1, tiled=True)  20.1 us
  transfers between devices with their start and end apart: 8, of which 7 were waited for; matrix products, arithmetic and copies ran while one was open for 21% of the time, Pallas kernels for 0%

commit v1 on v0

v1 whole, which is shorter than its diff:
```python
import functools

import jax
import jax.numpy as jnp
from jax import lax
from jax.experimental import pallas as pl
from jax.experimental.pallas import tpu as pltpu
from jax.sharding import PartitionSpec as P

FF = 14336
BLK = 128
GROUP = 4
FIRST_SEND = 20
FIRST_GRADS = 4
COL, ROW, LIVE, OWNER, BASE, SHIFT, LOCAL, MINE, WAT = range(9)
TABLE_ROWS = 16
PLACE, PART, STRIP, CIDX, CWAS, OIDX, OWAS = range(7)
FIELDS = 7
COLS_ROW = 3 * FIELDS
HEAD_ROW = COLS_ROW + 1
MINE_ROW = COLS_ROW + 2
LISTS_ROW = COLS_ROW + 3
HEAD_COLS, HEAD_OVER, HEAD_LISTS = 3, 4, 8


class Sizes:
    def __init__(self, tokens, gate_blocks, slots, n_fsdp, n_tensor):
        self.tok, self.width = tokens.shape
        self.n_fsdp, self.n_tensor = n_fsdp, n_tensor
        self.rb = self.width // BLK
        self.cb = FF // (BLK * n_tensor)
        self.slots = slots
        self.all = 3 * slots
        self.lanes = -(-(self.all + GROUP) // 128) * 128
        self.nb = gate_blocks.shape[1]
        self.chunk = 3 * self.nb
        self.ring = n_fsdp // 2
        self.top = self.ring // 2
        self.rbt = self.rb // n_tensor
        self.order = [self.top]
        for d in range(1, self.top):
            self.order += [self.top + d, self.top - d]
        self.order.append(0)
        self.far = min(4, self.ring - 1)
        sparse = slots < self.cb
        self.keep = min(FIRST_GRADS, self.chunk) if sparse else self.chunk
        self.more = self.chunk - self.keep
        self.send_all = 2 * self.rbt
        self.first = min(FIRST_SEND, self.send_all) if sparse else self.send_all
        self.rest = self.send_all - self.first
        self.blocks = 2 * self.ring * self.chunk
        self.main = 2 * self.ring * self.keep
        self.plan_rows = -(-(LISTS_ROW + 2 * n_tensor) // 8) * 8
        self.recv_rows = -(-n_tensor // 8) * 8
        self.room = slots + GROUP


def permutations(sz):
    seq = list(range(0, sz.ring, 2)) + list(range(sz.ring - 1, 0, -2))
    ahead, behind, swap = [], [], []
    for i, q in enumerate(seq):
        up, down = seq[(i + 1) % sz.ring], seq[i - 1]
        ahead += [(q * 2, up * 2), (q * 2 + 1, down * 2 + 1)]
        behind += [(q * 2, down * 2), (q * 2 + 1, up * 2 + 1)]
        swap += [(q * 2, q * 2 + 1), (q * 2 + 1, q * 2)]
    return ahead, behind, swap


def group_table(sz, where, counts, f, rank):
    S, R, top = sz.slots, sz.ring, sz.top
    lane = lax.iota(jnp.int32, sz.lanes)
    kind = (lane >= S).astype(jnp.int32) + (lane >= 2 * S).astype(jnp.int32)
    n = lane - kind * S
    pad = sz.lanes - sz.all
    w = jnp.pad(where, (0, pad))
    limit = jnp.pad(jnp.repeat(counts, S, total_repeat_length=sz.all), (0, pad))
    live = (n < limit) & (lane < sz.all)
    down = kind == 2
    row = jnp.where(down, w % sz.rb, w // sz.cb)
    col = jnp.where(down, w // sz.rb, w % sz.cb)
    owner = n // sz.nb

    def position(chip):
        return jnp.where(chip % 2 == 0, chip // 2, R - 1 - chip // 2)

    away = position(owner // 2) - position(f // 2)
    away = jnp.where(owner % 2 == 0, away, -away)
    rel = (away + R) % R
    j = jnp.where(rel > top, 2 * (rel - top) - 1, 2 * (top - rel))
    j = jnp.where(rel == 0, R - 1, j)
    base = jnp.where(owner % 2 == f % 2, 0, R) + j
    shift = (row // sz.rbt - rank + sz.n_tensor) % sz.n_tensor
    local = jnp.where(down, 0, sz.rbt) + row % sz.rbt
    mine = (lane // sz.nb) * S + f * sz.nb + lane % sz.nb
    at = kind * sz.nb + n % sz.nb
    rows = [col, row, live.astype(jnp.int32), owner, base, shift, local, mine, at]
    table = jnp.stack([r.astype(jnp.float32) for r in rows])
    return jnp.pad(table, ((0, TABLE_ROWS - len(rows)), (0, 0)))


class Marks:
    def __init__(self, sz, table):
        N, L, S = sz.all, sz.lanes, sz.slots
        f32 = jnp.float32
        self.sub = lax.broadcasted_iota(jnp.int32, (N, L), 0)
        self.lane = lax.broadcasted_iota(jnp.int32, (N, L), 1)
        same = self.sub == self.lane
        self.row = lambda i: table[i:i + 1, :]
        self.col = lambda i: jnp.sum(jnp.where(same, table[i:i + 1, :], 0.0), axis=1, keepdims=True)
        sub_c = self.sub[:, :1]
        lane_r = self.lane[:1, :]

        def kind(x):
            return (x >= S).astype(f32) + (x >= 2 * S).astype(f32)

        self.kind_c, self.kind_r = kind(sub_c), kind(lane_r)
        live_c, live_r = self.col(LIVE), self.row(LIVE)
        self.same_col = (self.col(COL) == self.row(COL)).astype(f32)
        act_c, act_r = live_c, live_r
        for k in range(3):
            lanes = self.same_col * (live_r * (self.kind_r == k).astype(f32))
            act_c = act_c * jnp.max(lanes, axis=1, keepdims=True)
            subs = self.same_col * (live_c * (self.kind_c == k).astype(f32))
            act_r = act_r * jnp.max(subs, axis=0, keepdims=True)
        self.act_c, self.act_r = act_c, act_r
        out_c = jnp.where(self.kind_c == 2, 0.0, f32(sz.rb)) + self.col(ROW)
        out_r = jnp.where(self.kind_r == 2, 0.0, f32(sz.rb)) + self.row(ROW)
        self.same_out = (out_c == out_r).astype(f32)
        self.before = (self.lane < self.sub).astype(f32)
        self.after = (self.sub < self.lane).astype(f32)
        self.owas_c = jnp.max(self.same_out * self.before * act_r, axis=1, keepdims=True)
        self.owas_r = jnp.max(self.same_out * self.after * act_c, axis=0, keepdims=True)
        self.lead_c = act_c * (1.0 - self.owas_c)
        self.lead_r = act_r * (1.0 - self.owas_r)

    def ranks(self, chosen_r):
        return jnp.sum(self.before * chosen_r, axis=1, keepdims=True)

    def listed(self, chosen_c, rank_c, value_c, lo=0, hi=None):
        at = rank_c[lo:hi] == self.lane[lo:hi].astype(jnp.float32)
        return jnp.sum(jnp.where(at, chosen_c[lo:hi] * value_c[lo:hi], 0.0), axis=0, keepdims=True)

    def most_owned(self):
        owned = (self.col(OWNER) == self.row(OWNER)).astype(jnp.float32)
        return jnp.max(jnp.sum(owned * self.act_r, axis=1, keepdims=True), axis=0, keepdims=True)


def total(x):
    return jnp.sum(x, axis=0, keepdims=True)


def head_row(sz, entries):
    lane = lax.broadcasted_iota(jnp.int32, (1, sz.lanes), 1)
    row = jnp.zeros((1, sz.lanes), jnp.float32)
    for i, value in entries:
        row = jnp.where(lane == i, value, row)
    return row


def plan_kernel(sz, table_ref, plan):
    S, N = sz.slots, sz.all
    m = Marks(sz, table_ref)
    f32 = jnp.float32
    lane_r = m.lane[:1, :].astype(f32)
    same_kind = (m.kind_c == m.kind_r).astype(f32)
    rank_c = jnp.sum(m.before * same_kind * m.act_r, axis=1, keepdims=True)
    cwas_c = jnp.max(m.before * same_kind * m.same_col * m.act_r, axis=1, keepdims=True)
    cwas_r = jnp.max(m.after * same_kind * m.same_col * m.act_c, axis=0, keepdims=True)
    big = f32(4 * N)
    lanes_f = m.lane.astype(f32)
    gates_r = m.act_r * (m.kind_r == 0).astype(f32)
    cidx_c = jnp.min(jnp.where(m.same_col * gates_r > 0, lanes_f, big), axis=1, keepdims=True)
    oidx_c = jnp.min(jnp.where(m.same_out * m.act_r > 0, lanes_f, big), axis=1, keepdims=True)
    owned = (m.col(OWNER) == m.row(OWNER)).astype(f32)
    pos_c = jnp.sum(m.before * owned * m.act_r, axis=1, keepdims=True)
    base_c = m.col(BASE)
    place_c = base_c * sz.chunk + m.col(WAT)
    part_c = jnp.where(
        pos_c < sz.keep, base_c * sz.keep + pos_c, sz.main + base_c * sz.more + pos_c - sz.keep)
    fields = [
        (place_c, sz.blocks), (part_c, sz.blocks), (m.col(ROW), 0), (cidx_c, S), (cwas_c, 0), (oidx_c, N), (m.owas_c, 0)]
    rows = []
    head = []
    for k in range(3):
        lo, hi = k * S, (k + 1) * S
        n_k = total(m.act_c[lo:hi])
        head.append((k, n_k))
        for value, spare in fields:
            row = m.listed(m.act_c, rank_c, value, lo, hi)
            rows.append(jnp.where(lane_r < n_k, row, f32(spare)))
    sub_c = m.sub[:, :1].astype(f32)
    leader_c = m.act_c * (1.0 - cwas_c) * (m.kind_c == 0).astype(f32)
    leader_r = m.act_r * (1.0 - cwas_r) * (m.kind_r == 0).astype(f32)
    rows.append(m.listed(leader_c, m.ranks(leader_r), sub_c, 0, S))
    head.append((HEAD_COLS, total(leader_c)))
    over = (m.most_owned() > sz.keep).astype(f32)
    lists = []
    shift_c, shift_r = m.col(SHIFT), m.row(SHIFT)
    for s in range(sz.n_tensor):
        chosen_c = m.lead_c * (shift_c == s).astype(f32)
        chosen_r = m.lead_r * (shift_r == s).astype(f32)
        rank = m.ranks(chosen_r)
        lists.append(m.listed(chosen_c, rank, sub_c))
        lists.append(m.listed(chosen_c, rank, m.col(LOCAL)))
        n = total(chosen_c)
        head.append((HEAD_LISTS + s, n))
        over = jnp.maximum(over, (n > sz.first).astype(f32))
    head.append((HEAD_OVER, over))
    rows.append(head_row(sz, head))
    mine = m.sub.astype(f32) == m.row(MINE)
    rows.append(jnp.sum(jnp.where(mine, m.act_c * (pos_c + 1.0), 0.0), axis=0, keepdims=True))
    rows += lists
    for i, row in enumerate(rows):
        plan[i:i + 1, :] = row.astype(jnp.int32)


def recv_kernel(sz, *refs):
    tables, recv = refs[:-1], refs[-1]
    f32 = jnp.float32
    head = []
    over = jnp.zeros((1, 1), f32)
    for s, table in enumerate(tables, 1):
        m = Marks(sz, table)
        shift_c, shift_r = m.col(SHIFT), m.row(SHIFT)
        chosen_c = m.lead_c * (shift_c == 0).astype(f32)
        chosen_r = m.lead_r * (shift_r == 0).astype(f32)
        recv[s:s + 1, :] = m.listed(chosen_c, m.ranks(chosen_r), m.col(LOCAL)).astype(jnp.int32)
        head.append((HEAD_LISTS + s, total(chosen_c)))
        over = jnp.maximum(over, (m.most_owned() > sz.keep).astype(f32))
        for d in range(sz.n_tensor):
            n = total(m.lead_c * (shift_c == d).astype(f32))
            over = jnp.maximum(over, (n > sz.first).astype(f32))
    head.append((HEAD_OVER, over))
    recv[0:1, :] = head_row(sz, head).astype(jnp.int32)


def dot(a, b, ca, cb):
    return lax.dot_general(a, b, (((ca,), (cb,)), ((), ())), preferred_element_type=jnp.float32)


def compute_kernel(sz, *refs):
    plan, tokens, cot = refs[:3]
    n_chunks = 2 * sz.ring
    chunks = refs[3:3 + n_chunks]
    refs = refs[3 + n_chunks:]
    T = sz.n_tensor
    same, far, near, extra = refs[:4]
    firsts, rests = refs[4:4 + T], refs[4 + T:4 + 2 * T]
    (xs, wbuf, parts, gate_acc, up_acc, hg_acc, hid, gate_d, up_d, out_acc, stage, strip_sems, sems, rest_sems) = refs[4 + 2 * T:]

    def field(k, j, e):
        return plan[k * FIELDS + j, e]

    def steps(k):
        return (plan[HEAD_ROW, k] + (GROUP - 1)) // GROUP

    def strip_copy(k, e):
        src = cot if k == 2 else tokens
        cols = pl.ds(pl.multiple_of(field(k, STRIP, e) * BLK, BLK), BLK)
        return pltpu.make_async_copy(src.at[:, cols], xs.at[k * sz.room + e], strip_sems.at[k * sz.room + e])

    for k in range(3):
        lax.fori_loop(0, steps(k) * GROUP, lambda e, _, k=k: strip_copy(k, e).start(), None)
    loads = [
        pltpu.make_async_copy(chunk, wbuf.at[pl.ds(i * sz.chunk, sz.chunk)], sems.at[i])
        for i, chunk in enumerate(chunks)
    ]
    for c in loads:
        c.start()
    for k in range(3):
        lax.fori_loop(0, steps(k) * GROUP, lambda e, _, k=k: strip_copy(k, e).wait(), None)
    for c in loads:
        c.wait()

    def walk(k, body):
        lax.fori_loop(0, steps(k), lambda p, _: body(p * GROUP), None)

    def forward(k, acc, w_dim):
        def body(e0):
            prods = [
                dot(xs[k * sz.room + e0 + u], wbuf[field(k, PLACE, e0 + u)], 1, w_dim) for u in range(GROUP)]
            for u in range(GROUP):
                c = field(k, CIDX, e0 + u)
                acc[c] = prods[u] + jnp.where(field(k, CWAS, e0 + u) == 0, 0.0, acc[c])

        walk(k, body)

    forward(0, gate_acc, 0)
    forward(1, up_acc, 0)
    forward(2, hg_acc, 1)

    def column(i, _):
        c = plan[COLS_ROW, i]
        g, u, h = gate_acc[c], up_acc[c], hg_acc[c]
        s = lax.logistic(g)
        silu = g * s
        hid[c] = (silu * u).astype(jnp.bfloat16)
        gate_d[c] = (h * u * s * (1.0 + g * (1.0 - s))).astype(jnp.bfloat16)
        up_d[c] = (h * silu).astype(jnp.bfloat16)

    lax.fori_loop(0, plan[HEAD_ROW, HEAD_COLS], column, None)

    def backward(k, act, w_dim):
        def body(e0):
            terms, grads = [], []
            for u in range(GROUP):
                a = act[field(k, CIDX, e0 + u)]
                x = xs[k * sz.room + e0 + u]
                terms.append(dot(a, wbuf[field(k, PLACE, e0 + u)], 1, w_dim))
                grads.append(dot(a, x, 0, 0) if k == 2 else dot(x, a, 0, 0))
            for u in range(GROUP):
                parts[field(k, PART, e0 + u)] = grads[u].astype(jnp.bfloat16)
            for u in range(GROUP):
                at = field(k, OIDX, e0 + u)
                out_acc[at] = terms[u] + jnp.where(field(k, OWAS, e0 + u) == 0, 0.0, out_acc[at])

        walk(k, body)

    backward(2, hid, 0)
    backward(0, gate_d, 1)
    backward(1, up_d, 1)

    split = sz.ring * sz.keep
    cut = split + sz.far * sz.keep
    outs = [
        pltpu.make_async_copy(parts.at[pl.ds(split, cut - split)], far, sems.at[0]),
        pltpu.make_async_copy(parts.at[pl.ds(0, split)], same, sems.at[1]),
        pltpu.make_async_copy(parts.at[pl.ds(cut, sz.main - cut)], near, sems.at[2]),
    ]
    for c in outs:
        c.start()

    for s in range(T):
        def staged(i, _, s=s):
            stage[s * sz.send_all + i] = out_acc[plan[LISTS_ROW + 2 * s, i]].astype(jnp.bfloat16)

        lax.fori_loop(0, plan[HEAD_ROW, HEAD_LISTS + s], staged, None)
        first = pltpu.make_async_copy(stage.at[pl.ds(s * sz.send_all, sz.first)], firsts[s], sems.at[3 + s])
        first.start()
        outs.append(first)

    if sz.rest + sz.more > 0:
        @pl.when(plan[HEAD_ROW, HEAD_OVER] > 0)
        def _():
            copies = []
            if sz.rest > 0:
                copies += [
                    pltpu.make_async_copy(
                        stage.at[pl.ds(s * sz.send_all + sz.first, sz.rest)], rests[s], rest_sems.at[s])
                    for s in range(T)
                ]
            if sz.more > 0:
                copies.append(pltpu.make_async_copy(
                    parts.at[pl.ds(sz.main, sz.blocks - sz.main)], extra, rest_sems.at[T]))
            for c in copies:
                c.start()
            for c in copies:
                c.wait()
    for c in outs:
        c.wait()


def join_kernel(sz, *refs):
    T = sz.n_tensor
    plan, recv = refs[:2]
    firsts, rests = refs[2:2 + T], refs[2 + T:2 + 2 * T]
    outputs, input_grads, spare, sem = refs[-4:]
    outputs[...] = jnp.zeros_like(outputs)
    input_grads[...] = jnp.zeros_like(input_grads)

    def add(at, value):
        def into(ref, w):
            cols = pl.ds(pl.multiple_of(w * BLK, BLK), BLK)
            ref[:, cols] = (ref[:, cols].astype(jnp.float32) + value.astype(jnp.float32)).astype(jnp.bfloat16)

        @pl.when(at < sz.rbt)
        def _():
            into(outputs, at)

        @pl.when(at >= sz.rbt)
        def _():
            into(input_grads, at - sz.rbt)

    for s in range(T):
        n = (recv[0, HEAD_LISTS + s] if s else plan[HEAD_ROW, HEAD_LISTS])

        def where_to(i, s=s):
            return recv[s, i] if s else plan[LISTS_ROW + 1, i]

        def early(i, _, s=s):
            add(where_to(i), firsts[s][i])

        lax.fori_loop(0, jnp.minimum(n, sz.first), early, None)
        if sz.rest > 0:
            def late(i, _, s=s):
                copy = pltpu.make_async_copy(rests[s].at[i - sz.first], spare, sem)
                copy.start()
                copy.wait()
                add(where_to(i), spare[...])

            lax.fori_loop(jnp.minimum(n, sz.first), n, late, None)


def spec(space):
    return pl.BlockSpec(memory_space=space)


ANY, VMEM, SMEM = pl.ANY, pltpu.VMEM, pltpu.SMEM


def cost(flops, moved):
    return pl.CostEstimate(flops=flops, bytes_accessed=moved, transcendentals=0)


def call_plan(sz, table):
    return pl.pallas_call(
        functools.partial(plan_kernel, sz),
        out_shape=jax.ShapeDtypeStruct((sz.plan_rows, sz.lanes), jnp.int32),
        in_specs=[spec(VMEM)],
        out_specs=spec(VMEM),
        cost_estimate=cost(1_000_000, 4_000_000),
        name="plan",
    )(table)


def call_recv(sz, tables):
    return pl.pallas_call(
        functools.partial(recv_kernel, sz),
        out_shape=jax.ShapeDtypeStruct((sz.recv_rows, sz.lanes), jnp.int32),
        in_specs=[spec(VMEM)] * len(tables),
        out_specs=spec(VMEM),
        cost_estimate=cost(1_000_000, 4_000_000),
        name="recv",
    )(*tables)


def call_compute(sz, plan, tokens, cot, chunks):
    T = sz.n_tensor
    bf, f32 = jnp.bfloat16, jnp.float32

    def blocks(n):
        return jax.ShapeDtypeStruct((max(n, 1), BLK, BLK), bf)

    out_shape = [
        blocks(sz.ring * sz.keep),
        blocks(sz.far * sz.keep),
        blocks((sz.ring - sz.far) * sz.keep),
        blocks(sz.blocks - sz.main),
    ]
    out_shape += [blocks(sz.first)] * T + [blocks(sz.rest)] * T
    scratch = [
        ((3 * sz.room, sz.tok, BLK), bf),
        ((sz.blocks + 1, BLK, BLK), bf),
        ((sz.blocks + 1, BLK, BLK), bf),
        ((sz.slots + 1, sz.tok, BLK), f32),
        ((sz.slots + 1, sz.tok, BLK), f32),
        ((sz.slots + 1, sz.tok, BLK), f32),
        ((sz.slots + 1, sz.tok, BLK), bf),
        ((sz.slots + 1, sz.tok, BLK), bf),
        ((sz.slots + 1, sz.tok, BLK), bf),
        ((sz.all + 1, sz.tok, BLK), f32),
        ((T * sz.send_all, sz.tok, BLK), bf),
    ]
    held = sum(s[0] * s[1] * s[2] * jnp.dtype(t).itemsize for s, t in scratch)
    return pl.pallas_call(
        functools.partial(compute_kernel, sz),
        out_shape=out_shape,
        in_specs=[spec(SMEM)] + [spec(ANY)] * (2 + len(chunks)),
        out_specs=[spec(ANY)] * len(out_shape),
        scratch_shapes=[pltpu.VMEM(s, t) for s, t in scratch] + [
            pltpu.SemaphoreType.DMA((3 * sz.room,)),
            pltpu.SemaphoreType.DMA((max(len(chunks), 3 + T),)),
            pltpu.SemaphoreType.DMA((T + 1,)),
        ],
        compiler_params=pltpu.CompilerParams(vmem_limit_bytes=held + 2 * 1024 * 1024),
        cost_estimate=cost(1_000_000_000, 20_000_000),
        name="compute",
    )(plan, tokens, cot, *chunks)


def call_join(sz, plan, recv, firsts, rests):
    half = jax.ShapeDtypeStruct((sz.tok, sz.width // sz.n_tensor), jnp.bfloat16)
    return pl.pallas_call(
        functools.partial(join_kernel, sz),
        out_shape=[half, half],
        in_specs=[spec(SMEM)] * 2 + [spec(VMEM)] * len(firsts) + [spec(ANY)] * len(rests),
        out_specs=[spec(VMEM), spec(VMEM)],
        scratch_shapes=[pltpu.VMEM((sz.tok, BLK), jnp.bfloat16), pltpu.SemaphoreType.DMA],
        compiler_params=pltpu.CompilerParams(vmem_limit_bytes=16 * 1024 * 1024),
        cost_estimate=cost(1_000_000, 6_000_000),
        name="join",
    )(plan, recv, *firsts, *rests)


def gather_chunks(sz, chunk, plan_of):
    ahead, behind, swap = permutations(sz)
    same = {0: chunk}
    a = b = chunk
    for s in range(1, sz.top + 1):
        if s == 2:
            (a, b), plan = lax.optimization_barrier(((a, b), plan_of()))
        a = lax.ppermute(a, "fsdp", ahead)
        same[sz.ring - s] = a
        if s < sz.top:
            b = lax.ppermute(b, "fsdp", behind)
            same[s] = b
    other = {d: lax.ppermute(same[d], "fsdp", swap) for d in same}
    return [side[d] for side in (same, other) for d in sz.order], plan


def reduce_parts(sz, per, same, pair):
    ahead, behind, _ = permutations(sz)

    def term(d, *more):
        j = sz.order.index(d)
        out = same[j * per:(j + 1) * per].astype(jnp.float32) + pair(j).astype(jnp.float32)
        for m in more:
            out = out + m.astype(jnp.float32)
        return out.astype(jnp.bfloat16)

    a, b = term(sz.top), term(sz.top + 1) if sz.top > 1 else None
    for s in range(1, sz.top + 1):
        if b is not None and s < sz.top:
            a, b = lax.optimization_barrier((a, b))
        a = lax.ppermute(a, "fsdp", ahead)
        if s < sz.top:
            b = lax.ppermute(b, "fsdp", behind)
            a = term(sz.top - s, a)
            if s + 1 < sz.top:
                b = term(sz.top + 1 + s, b)
    return term(0, a, b) if b is not None else term(0, a)


def shards(
    tokens,
    cotangent,
    gate_blocks,
    up_blocks,
    down_blocks,
    gate_where,
    up_where,
    down_where,
    block_counts,
):
    n_fsdp, T = lax.axis_size("fsdp"), lax.axis_size("tensor")
    sz = Sizes(tokens, gate_blocks, gate_where.shape[1], n_fsdp, T)
    f, rank = lax.axis_index("fsdp"), lax.axis_index("tensor")
    _, _, swap = permutations(sz)

    chunk = jnp.concatenate([gate_blocks[0], up_blocks[0], down_blocks[0]])
    where = jnp.concatenate([gate_where[0], up_where[0], down_where[0], block_counts[:, 0]])

    def table_of(raw):
        return group_table(sz, raw[:sz.all], raw[sz.all:], f, rank)

    chunks, plan = gather_chunks(sz, chunk, lambda: call_plan(sz, table_of(where)))
    theirs = [
        lax.ppermute(where, "tensor", [(i, (i + s) % T) for i in range(T)]) for s in range(1, T)]
    recv = call_recv(sz, [table_of(raw) for raw in theirs])

    outs = call_compute(sz, plan, tokens, cotangent, chunks)
    same, far, near, extra = outs[:4]
    firsts, rests = outs[4:4 + T], outs[4 + T:]

    def exchange(arrays):
        return [arrays[0]] + [
            lax.ppermute(arrays[s], "tensor", [(i, (i + s) % T) for i in range(T)]) for s in range(1, T)]

    far, near = lax.ppermute(far, "fsdp", swap), lax.ppermute(near, "fsdp", swap)
    firsts = exchange(firsts)

    def pair(j):
        at = j * sz.keep
        return far[at:at + sz.keep] if j < sz.far else near[at - sz.far * sz.keep:][:sz.keep]

    grads = reduce_parts(sz, sz.keep, same, pair)

    if sz.rest + sz.more > 0:
        def spill(rests, extra):
            moved = exchange(rests)
            if sz.more == 0:
                return moved, extra
            n = sz.ring * sz.more
            other = lax.ppermute(extra[n:], "fsdp", swap)
            late = reduce_parts(sz, sz.more, extra[:n], lambda j: other[j * sz.more:(j + 1) * sz.more])
            return moved, late

        def none(rests, extra):
            return list(rests), extra[:max(sz.more, 1)]

        over = plan[HEAD_ROW, HEAD_OVER] + recv[0, HEAD_OVER]
        rests, late = lax.cond(over > 0, spill, none, list(rests), extra)
        if sz.more > 0:
            grads = jnp.concatenate([grads, late])
    outputs, input_grads = call_join(sz, plan, recv, firsts, rests)

    def owned(i):
        at = plan[MINE_ROW, i]
        out = jnp.zeros((BLK, BLK), jnp.bfloat16)
        for p in range(sz.chunk):
            out = jnp.where(at == p + 1, grads[p], out)
        return out

    mine = [
        jnp.stack([owned(k * sz.nb + a) for a in range(sz.nb)])[None] for k in range(3)]
    return outputs, input_grads, *mine


def solution(mesh):
    placed = (
        P("fsdp", None),
        P("fsdp", None),
        P("tensor", "fsdp", None, None),
        P("tensor", "fsdp", None, None),
        P("tensor", "fsdp", None, None),
        P("tensor", None),
        P("tensor", None),
        P("tensor", None),
        P(None, "tensor"),
    )
    return jax.shard_map(
        shards,
        mesh=mesh,
        in_specs=placed,
        out_specs=(
            P("fsdp", "tensor"),
            P("fsdp", "tensor"),
            P("tensor", "fsdp", None, None),
            P("tensor", "fsdp", None, None),
            P("tensor", "fsdp", None, None),
        ),
        check_vma=False,
    )
```

time: 418 us -> 114 us (0.27)
  waiting for transfers between devices: 280 us -> 25.3 us
  other arithmetic: 56.1 us -> 13.7 us
  local copies, waits for them, and re-layouts: 47.5 us -> 13 us
  Pallas kernels: 0 us -> 19.8 us
  matrix products: 18.4 us -> 0 us
  starting transfers between devices: 0.5 us -> 17.4 us
  between operations: 14.4 us -> 24.7 us
    reduce_scatter x5 -> x0, waiting for transfers between devices: 201 us -> none  [the longest x1 61.1 us: shards(): lax.psum_scatter(gate_part[None].astype(jnp.bfloat16), 'fsdp', scatter_di...]
    all_gather x3 -> x0, waiting for transfers between devices: 76.9 us -> none  [the longest x1 28.5 us: shards(): lax.all_gather(down_blocks, 'fsdp', axis=1, tiled=True)]
    scatter-add x6 -> x0, other arithmetic: 37.6 us -> none  [collect(): return jax.ops.segment_sum(block_terms, segment_ids, num_segments=segments)]
    ppermute x0 -> x26, waiting for transfers between devices: none -> 25.3 us  [the longest x4 11.8 us: gather_chunks(): a = lax.ppermute(a, 'fsdp', ahead)]
    pallas_call x0 -> x4, Pallas kernels: none -> 19.8 us  [the longest x1 13.3 us: call_compute(): pl.pallas_call(functools.partial(compute_kernel, sz), out_shape=out_shape...]
    dot_general x9 -> x0, matrix products: 18.4 us -> none  [blockwise(): jnp.einsum(pattern, left_side, right_side, preferred_element_type=jnp.flo...]
    ppermute x0 -> x26, starting transfers between devices: none -> 17.4 us  [the longest x4 5.16 us: gather_chunks(): a = lax.ppermute(a, 'fsdp', ahead)]
    another operation x6 -> x2, local copies, waits for them, and re-layouts: 14.3 us -> 0.08 us  [group_table(): table = jnp.stack([r.astype(jnp.float32) for r in rows])]
  transfers between devices with their start and end apart: 8 -> 26, of which waited for: 7 -> 10; matrix products, arithmetic and copies ran while one was open for 21% -> 15% of each run, Pallas kernels for 0% -> 4%
where the time goes in v1:
time: 114 us
  waiting for transfers between devices  25.3 us (22%)
  between operations  24.7 us (22%)
  Pallas kernels  19.8 us (17%)
  starting transfers between devices  17.4 us (15%)
  other arithmetic  13.7 us (12%)
  local copies, waits for them, and re-layouts  13 us (11%)
    pallas_call x1, Pallas kernels, call_compute(): pl.pallas_call(functools.partial(compute_kernel, sz), out_shape=out_shape...  13.3 us
    ppermute x4, waiting for transfers between devices, gather_chunks(): a = lax.ppermute(a, 'fsdp', ahead)  11.8 us
    ppermute x3, waiting for transfers between devices, reduce_parts(): b = lax.ppermute(b, 'fsdp', behind)  6.54 us
    unnamed x26, local copies, waits for them, and re-layouts  5.54 us
    ppermute x4, starting transfers between devices, gather_chunks(): a = lax.ppermute(a, 'fsdp', ahead)  5.16 us
    ppermute x3, starting transfers between devices, reduce_parts(): b = lax.ppermute(b, 'fsdp', behind)  4.9 us
    gather x1, other arithmetic, group_table(): limit = jnp.pad(jnp.repeat(counts, S, total_repeat_length=sz.all), (0, pad))  4.51 us
    pallas_call x1, Pallas kernels, call_join(): pl.pallas_call(functools.partial(join_kernel, sz), out_shape=[half, half]...  3.2 us
  transfers between devices with their start and end apart: 26, of which 10 were waited for; matrix products, arithmetic and copies ran while one was open for 15% of the time, Pallas kernels for 4%

profile of v1, /device:TPU:0, one launch (start us, length us, event | category | flops | bytes accessed | tf_op | source)
XLA Modules:
  0.0 114.0 jit_solution(2944349119101991869)
XLA Ops:
  0.6 0.9 pad_maximum_fusion.refs_10_
  1.6 3.1 %collective-permute-start.9 = (bf16[6,128,128]{2,1,0:T(8,128)(2,1)S(1)}, bf16[6,128,128]{2,1,0:T(8,128)(2,1)S(1)}, u32[]{:S(2)}, u32[]{:S(2)}) collective-permute-start(bf16[6,128,128]{2,1,0:T(8,128)(2,1)S(1)} %pad_maximum_fusion.refs_10_), channel_id=1, source_target_pairs={{0,8},{2,6},{8,16},{10,2},{16,24},{18,10},{24,28},{26,18},{28,20},... | collective-permute-start | bytes 589832 | tf_op jit(solution)/shard_map/ppermute | solution.py:502
  4.6 0.0 collective-permute-start.10
  4.6 0.8 pad_add_fusion.1
  5.4 1.9 %collective-permute-start.11 = (s32[99]{0:T(128)S(1)}, s32[99]{0:T(128)S(1)}, u32[]{:S(2)}, u32[]{:S(2)}) collective-permute-start(s32[99]{0:T(128)S(1)} %pad_add_fusion.1), channel_id=1, source_target_pairs={{0,1},{1,0},{2,3},{3,2},{4,5},{5,4},{6,7},{7,6},{8,9},{9,8},{10,11... | collective-permute-start | bytes 1196 | tf_op jit(solution)/shard_map/ppermute | solution.py:558
  7.4 0.8 pad_add_fusion
  8.1 1.4 %fusion.30 = (s32[1]{0:T(128)}, s32[1]{0:T(128)}, s32[1]{0:T(128)}) fusion(s32[3]{0:T(128)} %bitcast.81), kind=kLoop, calls=%fused_computation.133 | loop fusion | bytes 24 | tf_op jit(solution)/shard_map/jit(_take)/gather | solution.py:76
  9.7 0.1 fusion.8
  9.7 0.6 convert_bitcast_fusion
  10.3 0.6 fusion.29
  10.9 4.5 %select_select_fusion.6 = (s32[96]{0:T(128)S(1)}, s32[96]{0:T(128)S(1)}) fusion(pred[96]{0:T(512)(128)(4,1)} %constant.435, pred[96]{0:T(512)(128)(4,1)} %constant.436, s32[]{:T(128)} %bitcast.19, s32[]{:T(128)} %bitcast.18, s32[]{:T(128)} %bitcast.17, s32[]{:T(128)} %bitcast.11, s32[]{:T(128)} %bitcast.10, s32[]{:T(128)} %bitcast.9), kind=kLoop, calls=%fused_computation.114 | loop fusion | flops 384 | bytes 984 | tf_op jit(solution)/shard_map/jit(_take)/gather | solution.py:76
  15.4 0.5 convert_bitcast_fusion.1
  16.0 0.6 fusion.15
  16.6 0.6 pad.26.table_ref
  17.2 1.8 %plan.1.refs_0_ = s32[32,128]{1,0:T(8,128)} custom-call(f32[16,128]{1,0:T(8,128)} %pad.26.table_ref), custom_call_target="tpu_custom_call" | custom-call | flops 1000000 | bytes 4000000 | tf_op jit(solution)/shard_map/plan/pallas_call | solution.py:416
  18.9 1.6 %collective-permute-start.12 = (bf16[6,128,128]{2,1,0:T(8,128)(2,1)S(1)}, bf16[6,128,128]{2,1,0:T(8,128)(2,1)S(1)}, u32[]{:S(2)}, u32[]{:S(2)}) collective-permute-start(bf16[6,128,128]{2,1,0:T(8,128)(2,1)S(1)} %collective-permute-done.9.refs_8_), channel_id=1, source_target_pairs={{0,8},{2,6},{8,16},{10,2},{16,24},{18,10},{24,28},{26,18},{28,20},... | collective-permute-start | bytes 589832 | tf_op jit(solution)/shard_map/ppermute | solution.py:502
  20.5 0.4 collective-permute-start.15
  21.0 5.0 %collective-permute-done.12.refs_6_ = bf16[6,128,128]{2,1,0:T(8,128)(2,1)S(1)} collective-permute-done((bf16[6,128,128]{2,1,0:T(8,128)(2,1)S(1)}, bf16[6,128,128]{2,1,0:T(8,128)(2,1)S(1)}, u32[]{:S(2)}, u32[]{:S(2)}) %collective-permute-start.12) | collective-permute-done | bytes 196640 | tf_op jit(solution)/shard_map/ppermute | solution.py:502
  26.0 0.5 collective-permute-start.13
  26.5 0.5 collective-permute-start.22
  27.0 0.7 copy-done.2
  27.7 1.5 %collective-permute-start.16 = (bf16[6,128,128]{2,1,0:T(8,128)(2,1)S(1)}, bf16[6,128,128]{2,1,0:T(8,128)(2,1)S(1)}, u32[]{:S(2)}, u32[]{:S(2)}) collective-permute-start(bf16[6,128,128]{2,1,0:T(8,128)(2,1)S(1)} %collective-permute-done.15.refs_7_), channel_id=1, source_target_pairs={{0,4},{2,10},{8,0},{10,18},{16,8},{18,26},{24,16},{26,30},{28,24},... | collective-permute-start | bytes 589832 | tf_op jit(solution)/shard_map/ppermute | solution.py:505
  29.2 3.3 %collective-permute-done.13.refs_4_ = bf16[6,128,128]{2,1,0:T(8,128)(2,1)S(1)} collective-permute-done((bf16[6,128,128]{2,1,0:T(8,128)(2,1)S(1)}, bf16[6,128,128]{2,1,0:T(8,128)(2,1)S(1)}, u32[]{:S(2)}, u32[]{:S(2)}) %collective-permute-start.13) | collective-permute-done | bytes 196640 | tf_op jit(solution)/shard_map/ppermute | solution.py:502
  32.5 0.5 collective-permute-start.21
  33.0 0.1 collective-permute-start.18
  33.1 1.6 %collective-permute-done.16.refs_5_ = bf16[6,128,128]{2,1,0:T(8,128)(2,1)S(1)} collective-permute-done((bf16[6,128,128]{2,1,0:T(8,128)(2,1)S(1)}, bf16[6,128,128]{2,1,0:T(8,128)(2,1)S(1)}, u32[]{:S(2)}, u32[]{:S(2)}) %collective-permute-start.16) | collective-permute-done | bytes 196640 | tf_op jit(solution)/shard_map/ppermute | solution.py:505
  34.7 3.5 %collective-permute-done.14.refs_3_ = bf16[6,128,128]{2,1,0:T(8,128)(2,1)S(1)} collective-permute-done((bf16[6,128,128]{2,1,0:T(8,128)(2,1)S(1)}, bf16[6,128,128]{2,1,0:T(8,128)(2,1)S(1)}, u32[]{:S(2)}, u32[]{:S(2)}) %collective-permute-start.14) | collective-permute-done | bytes 196640 | tf_op jit(solution)/shard_map/ppermute | solution.py:502
  38.2 1.4 %collective-permute-done.17.refs_11_ = bf16[6,128,128]{2,1,0:T(8,128)(2,1)S(1)} collective-permute-done((bf16[6,128,128]{2,1,0:T(8,128)(2,1)S(1)}, bf16[6,128,128]{2,1,0:T(8,128)(2,1)S(1)}, u32[]{:S(2)}, u32[]{:S(2)}) %collective-permute-start.17) | collective-permute-done | bytes 196640 | tf_op jit(solution)/shard_map/ppermute | solution.py:507
  39.6 1.6 %copy-done = bf16[128,8192]{1,0:T(8,128)(2,1)S(1)} copy-done((bf16[128,8192]{1,0:T(8,128)(2,1)S(1)}, bf16[128,8192]{1,0:T(8,128)(2,1)}, u32[]{:S(2)}) %copy-start) | copy-done | bytes 2097176
  41.2 1.6 %copy-done.1 = bf16[128,8192]{1,0:T(8,128)(2,1)S(1)} copy-done((bf16[128,8192]{1,0:T(8,128)(2,1)S(1)}, bf16[128,8192]{1,0:T(8,128)(2,1)}, u32[]{:S(2)}) %copy-start.1) | copy-done | bytes 2097176
  42.8 0.9 copy-done.3
  43.7 0.7 copy-done.4
  44.4 13.3 %compute.1 = (bf16[32,128,128]{2,1,0:T(8,128)(2,1)S(1)}, bf16[16,128,128]{2,1,0:T(8,128)(2,1)S(1)}, bf16[16,128,128]{2,1,0:T(8,128)(2,1)S(1)}, bf16[32,128,128]{...) custom-call(s32[32,128]{1,0:T(8,128)S(1)} %copy-done.4, ...), custom_call_target="tpu_custom_call" | custom-call | flops 1000000000 | bytes 20000000 | tf_op jit(solution)/shard_map/compute/pallas_call | solution.py:465
  57.7 0.2 collective-permute-start.27
  57.9 0.4 collective-permute-start.26
  58.3 1.4 %collective-permute-done.27 = bf16[16,128,128]{2,1,0:T(8,128)(2,1)S(1)} collective-permute-done((bf16[16,128,128]{2,1,0:T(8,128)(2,1)S(1)}, bf16[16,128,128]{2,1,0:T(8,128)(2,1)S(1)}, u32[]{:S(2)}, u32[]{:S(2)}) %collective-permute-start.27) | collective-permute-done | bytes 524320 | tf_op jit(solution)/shard_map/ppermute | solution.py:569
  59.7 0.1 add_convert_fusion.14
  59.8 1.7 %collective-permute-start.29 = (bf16[4,128,128]{2,1,0:T(8,128)(2,1)S(1)}, bf16[4,128,128]{2,1,0:T(8,128)(2,1)S(1)}, u32[]{:S(2)}, u32[]{:S(2)}) collective-permute-start(bf16[4,128,128]{2,1,0:T(8,128)(2,1)S(1)} %get-tuple-element.85), channel_id=1, source_target_pairs={{0,4},{2,10},{8,0},{10,18},{16,8},{18,26},{24,16},{26,30},{28,24},... | collective-permute-start | bytes 393224 | tf_op jit(solution)/shard_map/ppermute | solution.py:527
  61.5 0.4 collective-permute-start.28
  61.9 3.6 %collective-permute-done.29 = bf16[4,128,128]{2,1,0:T(8,128)(2,1)S(1)} collective-permute-done((bf16[4,128,128]{2,1,0:T(8,128)(2,1)S(1)}, bf16[4,128,128]{2,1,0:T(8,128)(2,1)S(1)}, u32[]{:S(2)}, u32[]{:S(2)}) %collective-permute-start.29) | collective-permute-done | bytes 131104 | tf_op jit(solution)/shard_map/ppermute | solution.py:527
  65.5 1.0 collective-permute-done.28
  66.5 0.1 add_convert_fusion.12
  66.6 1.6 %collective-permute-start.31 = (bf16[4,128,128]{2,1,0:T(8,128)(2,1)S(1)}, bf16[4,128,128]{2,1,0:T(8,128)(2,1)S(1)}, u32[]{:S(2)}, u32[]{:S(2)}) collective-permute-start(bf16[4,128,128]{2,1,0:T(8,128)(2,1)S(1)} %get-tuple-element.87), channel_id=1, source_target_pairs={{0,4},{2,10},{8,0},{10,18},{16,8},{18,26},{24,16},{26,30},{28,24},... | collective-permute-start | bytes 393224 | tf_op jit(solution)/shard_map/ppermute | solution.py:527
  68.2 0.4 collective-permute-start.30
  68.7 3.0 %collective-permute-done.31 = bf16[4,128,128]{2,1,0:T(8,128)(2,1)S(1)} collective-permute-done((bf16[4,128,128]{2,1,0:T(8,128)(2,1)S(1)}, bf16[4,128,128]{2,1,0:T(8,128)(2,1)S(1)}, u32[]{:S(2)}, u32[]{:S(2)}) %collective-permute-start.31) | collective-permute-done | bytes 131104 | tf_op jit(solution)/shard_map/ppermute | solution.py:527
  71.6 1.5 %collective-permute-done.30 = bf16[4,128,128]{2,1,0:T(8,128)(2,1)S(1)} collective-permute-done((bf16[4,128,128]{2,1,0:T(8,128)(2,1)S(1)}, bf16[4,128,128]{2,1,0:T(8,128)(2,1)S(1)}, u32[]{:S(2)}, u32[]{:S(2)}) %collective-permute-start.30) | collective-permute-done | bytes 131104 | tf_op jit(solution)/shard_map/ppermute | solution.py:525
  73.2 0.8 add_convert_fusion.10
  73.9 0.4 collective-permute-start.32
  74.4 0.6 pad.29.refs_0_
  75.1 1.6 %recv.1.refs_1_ = s32[8,128]{1,0:T(8,128)} custom-call(f32[16,128]{1,0:T(8,128)} %pad.29.refs_0_), custom_call_target="tpu_custom_call" | custom-call | flops 1000000 | bytes 4000000 | tf_op jit(solution)/shard_map/recv/pallas_call | solution.py:427
  76.7 1.3 %slice.228 = s32[1,1]{1,0:T(1,128)} slice(s32[8,128]{1,0:T(8,128)} %recv.1.refs_1_), slice={[0:1], [4:5]} | slice | bytes 8 | tf_op jit(solution)/shard_map/slice | solution.py:591
  77.9 0.7 fusion.28
  79.9 0.0 copy-start.6
  79.9 2.3 %conditional.1 = (bf16[44,128,128]{2,1,0:T(8,128)(2,1)}, bf16[2,128,128]{2,1,0:T(8,128)(2,1)}, bf16[1,128,128]{2,1,0:T(8,128)(2,1)S(1)}, bf16[1,128,128]{2,1,0:T(8,128)(2,1)S(1)}) conditional(s32[]{:T(128)} %bitcast.23, (bf16[32,128,128]{2,1,0:T(8,128)(2,1)}, bf16[44,128,128]{2,1,0:T(8,128)(2,1)}) %tuple.34, (bf16[44,128,128]{2,1,0:T(8,128)(2,1)}, ...), branch_computations={%region_0.2_spmd, %region_1.3_spmd} | conditional | flops 1507328 | bytes 15794568 | solution.py:592
  79.9 1.5 %slice.173 = bf16[2,128,128]{2,1,0:T(8,128)(2,1)} slice(bf16[32,128,128]{2,1,0:T(8,128)(2,1)} %get-tuple-element.32), slice={[0:2], [0:128], [0:128]} | slice | bytes 131072 | tf_op jit(solution)/shard_map/cond/branch_0_fun/slice | solution.py:589
  81.4 0.8 fusion.26
  82.2 1.6 %collective-permute-start.34 = (bf16[4,128,128]{2,1,0:T(8,128)(2,1)S(1)}, bf16[4,128,128]{2,1,0:T(8,128)(2,1)S(1)}, u32[]{:S(2)}, u32[]{:S(2)}) collective-permute-start(bf16[4,128,128]{2,1,0:T(8,128)(2,1)S(1)} %get-tuple-element.89), channel_id=1, source_target_pairs={{0,4},{2,10},{8,0},{10,18},{16,8},{18,26},{24,16},{26,30},{28,24},... | collective-permute-start | bytes 393224 | tf_op jit(solution)/shard_map/ppermute | solution.py:527
  83.8 1.0 add_convert_fusion.9
  84.7 0.5 collective-permute-start.33
  107.7 3.2 %join.1 = (bf16[128,4096]{1,0:T(8,128)(2,1)}, bf16[128,4096]{1,0:T(8,128)(2,1)}) custom-call(s32[32,128]{1,0:T(8,128)S(1)} %copy-done.5, s32[8,128]{1,0:T(8,128)S(1)} %copy-done.6, bf16[20,128,128]{2,1,0:T(8,128)(2,1)S(1)} %get-tuple-element.71.refs_2_, bf16[20,128,128]{2,1,0:T(8,128)(2,1)} %collective-permute-done.25.refs_3_, ...), custom_call_target="tpu_custom_call" | custom-call | flops 1000000 | bytes 6000000 | tf_op jit(solution)/shard_map/join/pallas_call | solution.py:483
  111.0 1.0 add_convert_fusion.8
  112.0 0.6 maximum_bitcast_fusion
  112.7 0.6 maximum_bitcast_fusion.1
  113.3 0.6 maximum_bitcast_fusion.2
  (53 shorter events, 0.3 us)
Async XLA Ops:
  1.6 17.4 %collective-permute-start.9 = (bf16[6,128,128]{2,1,0:T(8,128)(2,1)S(1)}, bf16[6,128,128]{2,1,0:T(8,128)(2,1)S(1)}, u32[]{:S(2)}, u32[]{:S(2)}) collective-permute-start(bf16[6,128,128]{2,1,0:T(8,128)(2,1)S(1)} %pad_maximum_fusion.refs_10_), channel_id=1, source_target_pairs={{0,8},{2,6},{8,16},{10,2},{16,24},{18,10},{24,28},{26,18},{28,20},... | collective-permute-start | bytes 589832 | tf_op jit(solution)/shard_map/ppermute | solution.py:502
  4.6 14.3 %collective-permute-start.10 = (bf16[6,128,128]{2,1,0:T(8,128)(2,1)S(1)}, bf16[6,128,128]{2,1,0:T(8,128)(2,1)S(1)}, u32[]{:S(2)}, u32[]{:S(2)}) collective-permute-start(bf16[6,128,128]{2,1,0:T(8,128)(2,1)S(1)} %pad_maximum_fusion.refs_10_), channel_id=1, source_target_pairs={{0,4},{2,10},{8,0},{10,18},{16,8},{18,26},{24,16},{26,30},{28,24},... | collective-permute-start | bytes 589832 | tf_op jit(solution)/shard_map/ppermute | solution.py:505
  5.4 4.3 %collective-permute-start.11 = (s32[99]{0:T(128)S(1)}, s32[99]{0:T(128)S(1)}, u32[]{:S(2)}, u32[]{:S(2)}) collective-permute-start(s32[99]{0:T(128)S(1)} %pad_add_fusion.1), channel_id=1, source_target_pairs={{0,1},{1,0},{2,3},{3,2},{4,5},{5,4},{6,7},{7,6},{8,9},{9,8},{10,11... | collective-permute-start | bytes 1196 | tf_op jit(solution)/shard_map/ppermute | solution.py:558
  18.9 7.0 %collective-permute-start.12 = (bf16[6,128,128]{2,1,0:T(8,128)(2,1)S(1)}, bf16[6,128,128]{2,1,0:T(8,128)(2,1)S(1)}, u32[]{:S(2)}, u32[]{:S(2)}) collective-permute-start(bf16[6,128,128]{2,1,0:T(8,128)(2,1)S(1)} %collective-permute-done.9.refs_8_), channel_id=1, source_target_pairs={{0,8},{2,6},{8,16},{10,2},{16,24},{18,10},{24,28},{26,18},{28,20},... | collective-permute-start | bytes 589832 | tf_op jit(solution)/shard_map/ppermute | solution.py:502
  20.5 7.2 %collective-permute-start.15 = (bf16[6,128,128]{2,1,0:T(8,128)(2,1)S(1)}, bf16[6,128,128]{2,1,0:T(8,128)(2,1)S(1)}, u32[]{:S(2)}, u32[]{:S(2)}) collective-permute-start(bf16[6,128,128]{2,1,0:T(8,128)(2,1)S(1)} %collective-permute-done.10.refs_9_), channel_id=1, source_target_pairs={{0,4},{2,10},{8,0},{10,18},{16,8},{18,26},{24,16},{26,30},{28,24},... | collective-permute-start | bytes 589832 | tf_op jit(solution)/shard_map/ppermute | solution.py:505
  26.0 6.5 %collective-permute-start.13 = (bf16[6,128,128]{2,1,0:T(8,128)(2,1)S(1)}, bf16[6,128,128]{2,1,0:T(8,128)(2,1)S(1)}, u32[]{:S(2)}, u32[]{:S(2)}) collective-permute-start(bf16[6,128,128]{2,1,0:T(8,128)(2,1)S(1)} %collective-permute-done.12.refs_6_), channel_id=1, source_target_pairs={{0,8},{2,6},{8,16},{10,2},{16,24},{18,10},{24,28},{26,18},{28,20},... | collective-permute-start | bytes 589832 | tf_op jit(solution)/shard_map/ppermute | solution.py:502
  26.5 6.0 %collective-permute-start.24 = (bf16[6,128,128]{2,1,0:T(8,128)(2,1)S(1)}, bf16[6,128,128]{2,1,0:T(8,128)(2,1)S(1)}, u32[]{:S(2)}, u32[]{:S(2)}) collective-permute-start(bf16[6,128,128]{2,1,0:T(8,128)(2,1)S(1)} %pad_maximum_fusion.refs_10_), channel_id=1, source_target_pairs={{0,2},{2,0},{8,10},{10,8},{16,18},{18,16},{24,26},{26,24},{28,30},... | collective-permute-start | bytes 589832 | tf_op jit(solution)/shard_map/ppermute | solution.py:507
  26.5 6.0 %collective-permute-start.22 = (bf16[6,128,128]{2,1,0:T(8,128)(2,1)S(1)}, bf16[6,128,128]{2,1,0:T(8,128)(2,1)S(1)}, u32[]{:S(2)}, u32[]{:S(2)}) collective-permute-start(bf16[6,128,128]{2,1,0:T(8,128)(2,1)S(1)} %collective-permute-done.9.refs_8_), channel_id=1, source_target_pairs={{0,2},{2,0},{8,10},{10,8},{16,18},{18,16},{24,26},{26,24},{28,30},... | collective-permute-start | bytes 589832 | tf_op jit(solution)/shard_map/ppermute | solution.py:507
  27.0 6.0 %collective-permute-start.23 = (bf16[6,128,128]{2,1,0:T(8,128)(2,1)S(1)}, bf16[6,128,128]{2,1,0:T(8,128)(2,1)S(1)}, u32[]{:S(2)}, u32[]{:S(2)}) collective-permute-start(bf16[6,128,128]{2,1,0:T(8,128)(2,1)S(1)} %collective-permute-done.10.refs_9_), channel_id=1, source_target_pairs={{0,2},{2,0},{8,10},{10,8},{16,18},{18,16},{24,26},{26,24},{28,30},... | collective-permute-start | bytes 589832 | tf_op jit(solution)/shard_map/ppermute | solution.py:507
  27.0 0.7 copy-start.2
  27.7 7.0 %collective-permute-start.16 = (bf16[6,128,128]{2,1,0:T(8,128)(2,1)S(1)}, bf16[6,128,128]{2,1,0:T(8,128)(2,1)S(1)}, u32[]{:S(2)}, u32[]{:S(2)}) collective-permute-start(bf16[6,128,128]{2,1,0:T(8,128)(2,1)S(1)} %collective-permute-done.15.refs_7_), channel_id=1, source_target_pairs={{0,4},{2,10},{8,0},{10,18},{16,8},{18,26},{24,16},{26,30},{28,24},... | collective-permute-start | bytes 589832 | tf_op jit(solution)/shard_map/ppermute | solution.py:505
  32.5 5.7 %collective-permute-start.14 = (bf16[6,128,128]{2,1,0:T(8,128)(2,1)S(1)}, bf16[6,128,128]{2,1,0:T(8,128)(2,1)S(1)}, u32[]{:S(2)}, u32[]{:S(2)}) collective-permute-start(bf16[6,128,128]{2,1,0:T(8,128)(2,1)S(1)} %collective-permute-done.13.refs_4_), channel_id=1, source_target_pairs={{0,8},{2,6},{8,16},{10,2},{16,24},{18,10},{24,28},{26,18},{28,20},... | collective-permute-start | bytes 589832 | tf_op jit(solution)/shard_map/ppermute | solution.py:502
  32.5 5.7 %collective-permute-start.20 = (bf16[6,128,128]{2,1,0:T(8,128)(2,1)S(1)}, bf16[6,128,128]{2,1,0:T(8,128)(2,1)S(1)}, u32[]{:S(2)}, u32[]{:S(2)}) collective-permute-start(bf16[6,128,128]{2,1,0:T(8,128)(2,1)S(1)} %collective-permute-done.12.refs_6_), channel_id=1, source_target_pairs={{0,2},{2,0},{8,10},{10,8},{16,18},{18,16},{24,26},{26,24},{28,30},... | collective-permute-start | bytes 589832 | tf_op jit(solution)/shard_map/ppermute | solution.py:507
  32.5 5.7 %collective-permute-start.21 = (bf16[6,128,128]{2,1,0:T(8,128)(2,1)S(1)}, bf16[6,128,128]{2,1,0:T(8,128)(2,1)S(1)}, u32[]{:S(2)}, u32[]{:S(2)}) collective-permute-start(bf16[6,128,128]{2,1,0:T(8,128)(2,1)S(1)} %collective-permute-done.15.refs_7_), channel_id=1, source_target_pairs={{0,2},{2,0},{8,10},{10,8},{16,18},{18,16},{24,26},{26,24},{28,30},... | collective-permute-start | bytes 589832 | tf_op jit(solution)/shard_map/ppermute | solution.py:507
  33.0 5.2 %collective-permute-start.18 = (bf16[6,128,128]{2,1,0:T(8,128)(2,1)S(1)}, bf16[6,128,128]{2,1,0:T(8,128)(2,1)S(1)}, u32[]{:S(2)}, u32[]{:S(2)}) collective-permute-start(bf16[6,128,128]{2,1,0:T(8,128)(2,1)S(1)} %collective-permute-done.13.refs_4_), channel_id=1, source_target_pairs={{0,2},{2,0},{8,10},{10,8},{16,18},{18,16},{24,26},{26,24},{28,30},... | collective-permute-start | bytes 589832 | tf_op jit(solution)/shard_map/ppermute | solution.py:507
  34.7 3.5 %collective-permute-start.19 = (bf16[6,128,128]{2,1,0:T(8,128)(2,1)S(1)}, bf16[6,128,128]{2,1,0:T(8,128)(2,1)S(1)}, u32[]{:S(2)}, u32[]{:S(2)}) collective-permute-start(bf16[6,128,128]{2,1,0:T(8,128)(2,1)S(1)} %collective-permute-done.16.refs_5_), channel_id=1, source_target_pairs={{0,2},{2,0},{8,10},{10,8},{16,18},{18,16},{24,26},{26,24},{28,30},... | collective-permute-start | bytes 589832 | tf_op jit(solution)/shard_map/ppermute | solution.py:507
  38.2 1.4 %collective-permute-start.17 = (bf16[6,128,128]{2,1,0:T(8,128)(2,1)S(1)}, bf16[6,128,128]{2,1,0:T(8,128)(2,1)S(1)}, u32[]{:S(2)}, u32[]{:S(2)}) collective-permute-start(bf16[6,128,128]{2,1,0:T(8,128)(2,1)S(1)} %collective-permute-done.14.refs_3_), channel_id=1, source_target_pairs={{0,2},{2,0},{8,10},{10,8},{16,18},{18,16},{24,26},{26,24},{28,30},... | collective-permute-start | bytes 589832 | tf_op jit(solution)/shard_map/ppermute | solution.py:507
  39.6 1.6 %copy-start = (bf16[128,8192]{1,0:T(8,128)(2,1)S(1)}, bf16[128,8192]{1,0:T(8,128)(2,1)}, u32[]{:S(2)}) copy-start(bf16[128,8192]{1,0:T(8,128)(2,1)} %refs_1_.1) | copy-start | bytes 6291460
  41.2 1.6 %copy-start.1 = (bf16[128,8192]{1,0:T(8,128)(2,1)S(1)}, bf16[128,8192]{1,0:T(8,128)(2,1)}, u32[]{:S(2)}) copy-start(bf16[128,8192]{1,0:T(8,128)(2,1)} %refs_2_.1) | copy-start | bytes 6291460
  42.8 0.9 copy-start.3
  43.7 0.7 copy-start.4
  57.7 2.0 %collective-permute-start.27 = (bf16[16,128,128]{2,1,0:T(8,128)(2,1)S(1)}, bf16[16,128,128]{2,1,0:T(8,128)(2,1)S(1)}, u32[]{:S(2)}, u32[]{:S(2)}) collective-permute-start(bf16[16,128,128]{2,1,0:T(8,128)(2,1)S(1)} %get-tuple-element.83), channel_id=1, source_target_pairs={{0,2},{2,0},{8,10},{10,8},{16,18},{18,16},{24,26},{26,24},{28,30},... | collective-permute-start | bytes 1572872 | tf_op jit(solution)/shard_map/ppermute | solution.py:569
  57.9 10.7 %collective-permute-start.26 = (bf16[16,128,128]{2,1,0:T(8,128)(2,1)S(1)}, bf16[16,128,128]{2,1,0:T(8,128)(2,1)S(1)}, u32[]{:S(2)}, u32[]{:S(2)}) collective-permute-start(bf16[16,128,128]{2,1,0:T(8,128)(2,1)S(1)} %get-tuple-element.82), channel_id=1, source_target_pairs={{0,2},{2,0},{8,10},{10,8},{16,18},{18,16},{24,26},{26,24},{28,30},... | collective-permute-start | bytes 1572872 | tf_op jit(solution)/shard_map/ppermute | solution.py:569
  59.7 14.7 %copy-start.8 = (f32[1,128]{1,0:T(1,128)S(1)}, f32[1,128]{1,0:T(1,128)}, u32[]{:S(2)}) copy-start(f32[1,128]{1,0:T(1,128)} %get-tuple-element.131) | copy-start | bytes 1540
  59.7 14.7 %copy-start.9 = (f32[1,128]{1,0:T(1,128)S(1)}, f32[1,128]{1,0:T(1,128)}, u32[]{:S(2)}) copy-start(f32[1,128]{1,0:T(1,128)} %get-tuple-element.132) | copy-start | bytes 1540
  59.7 14.7 %copy-start.10 = (f32[1,128]{1,0:T(1,128)S(1)}, f32[1,128]{1,0:T(1,128)}, u32[]{:S(2)}) copy-start(f32[1,128]{1,0:T(1,128)} %get-tuple-element.90) | copy-start | bytes 1540
  59.7 14.7 %copy-start.11 = (f32[1,128]{1,0:T(1,128)S(1)}, f32[1,128]{1,0:T(1,128)}, u32[]{:S(2)}) copy-start(f32[1,128]{1,0:T(1,128)} %get-tuple-element.124) | copy-start | bytes 1540
  59.7 14.7 %copy-start.12 = (f32[1,128]{1,0:T(1,128)S(1)}, f32[1,128]{1,0:T(1,128)}, u32[]{:S(2)}) copy-start(f32[1,128]{1,0:T(1,128)} %get-tuple-element.133) | copy-start | bytes 1540
  59.7 18.2 %copy-start.5 = (s32[32,128]{1,0:T(8,128)S(1)}, s32[32,128]{1,0:T(8,128)}, u32[]{:S(2)}) copy-start(s32[32,128]{1,0:T(8,128)} %plan.1.refs_0_) | copy-start | bytes 49156
  59.8 5.7 %collective-permute-start.29 = (bf16[4,128,128]{2,1,0:T(8,128)(2,1)S(1)}, bf16[4,128,128]{2,1,0:T(8,128)(2,1)S(1)}, u32[]{:S(2)}, u32[]{:S(2)}) collective-permute-start(bf16[4,128,128]{2,1,0:T(8,128)(2,1)S(1)} %get-tuple-element.85), channel_id=1, source_target_pairs={{0,4},{2,10},{8,0},{10,18},{16,8},{18,26},{24,16},{26,30},{28,24},... | collective-permute-start | bytes 393224 | tf_op jit(solution)/shard_map/ppermute | solution.py:527
  61.5 5.0 %collective-permute-start.28 = (bf16[4,128,128]{2,1,0:T(8,128)(2,1)S(1)}, bf16[4,128,128]{2,1,0:T(8,128)(2,1)S(1)}, u32[]{:S(2)}, u32[]{:S(2)}) collective-permute-start(bf16[4,128,128]{2,1,0:T(8,128)(2,1)S(1)} %get-tuple-element.84), channel_id=1, source_target_pairs={{0,8},{2,6},{8,16},{10,2},{16,24},{18,10},{24,28},{26,18},{28,20},... | collective-permute-start | bytes 393224 | tf_op jit(solution)/shard_map/ppermute | solution.py:525
  66.6 5.1 %collective-permute-start.31 = (bf16[4,128,128]{2,1,0:T(8,128)(2,1)S(1)}, bf16[4,128,128]{2,1,0:T(8,128)(2,1)S(1)}, u32[]{:S(2)}, u32[]{:S(2)}) collective-permute-start(bf16[4,128,128]{2,1,0:T(8,128)(2,1)S(1)} %get-tuple-element.87), channel_id=1, source_target_pairs={{0,4},{2,10},{8,0},{10,18},{16,8},{18,26},{24,16},{26,30},{28,24},... | collective-permute-start | bytes 393224 | tf_op jit(solution)/shard_map/ppermute | solution.py:527
  68.2 5.0 %collective-permute-start.30 = (bf16[4,128,128]{2,1,0:T(8,128)(2,1)S(1)}, bf16[4,128,128]{2,1,0:T(8,128)(2,1)S(1)}, u32[]{:S(2)}, u32[]{:S(2)}) collective-permute-start(bf16[4,128,128]{2,1,0:T(8,128)(2,1)S(1)} %get-tuple-element.86), channel_id=1, source_target_pairs={{0,8},{2,6},{8,16},{10,2},{16,24},{18,10},{24,28},{26,18},{28,20},... | collective-permute-start | bytes 393224 | tf_op jit(solution)/shard_map/ppermute | solution.py:525
  68.7 39.1 %collective-permute-start.25 = (bf16[20,128,128]{2,1,0:T(8,128)(2,1)}, bf16[20,128,128]{2,1,0:T(8,128)(2,1)}, u32[]{:S(2)}, u32[]{:S(2)}) collective-permute-start(bf16[20,128,128]{2,1,0:T(8,128)(2,1)} %get-tuple-element.72), channel_id=1, source_target_pairs={{0,1},{1,0},{2,3},{3,2},{4,5},{5,4},{6,7},{7,6},{8,9},{9,8},{10,11... | collective-permute-start | bytes 1966088 | tf_op jit(solution)/shard_map/ppermute | solution.py:567
  68.7 4.5 %copy-start.7 = (bf16[16,128,128]{2,1,0:T(8,128)(2,1)}, bf16[16,128,128]{2,1,0:T(8,128)(2,1)S(1)}, u32[]{:S(2)}) copy-start(bf16[16,128,128]{2,1,0:T(8,128)(2,1)S(1)} %collective-permute-done.26) | copy-start | bytes 1572868
  73.9 9.8 %collective-permute-start.32 = (bf16[4,128,128]{2,1,0:T(8,128)(2,1)}, bf16[4,128,128]{2,1,0:T(8,128)(2,1)S(1)}, u32[]{:S(2)}, u32[]{:S(2)}) collective-permute-start(bf16[4,128,128]{2,1,0:T(8,128)(2,1)} %get-tuple-element.88), channel_id=1, source_target_pairs={{0,8},{2,6},{8,16},{10,2},{16,24},{18,10},{24,28},{26,18},{28,20},... | collective-permute-start | bytes 393224 | tf_op jit(solution)/shard_map/ppermute | solution.py:525
  79.9 27.8 %copy-start.6 = (s32[8,128]{1,0:T(8,128)S(1)}, s32[8,128]{1,0:T(8,128)}, u32[]{:S(2)}) copy-start(s32[8,128]{1,0:T(8,128)} %recv.1.refs_1_) | copy-start | bytes 12292
  82.2 28.8 %collective-permute-start.34 = (bf16[4,128,128]{2,1,0:T(8,128)(2,1)S(1)}, bf16[4,128,128]{2,1,0:T(8,128)(2,1)S(1)}, u32[]{:S(2)}, u32[]{:S(2)}) collective-permute-start(bf16[4,128,128]{2,1,0:T(8,128)(2,1)S(1)} %get-tuple-element.89), channel_id=1, source_target_pairs={{0,4},{2,10},{8,0},{10,18},{16,8},{18,26},{24,16},{26,30},{28,24},... | collective-permute-start | bytes 393224 | tf_op jit(solution)/shard_map/ppermute | solution.py:527
  84.7 26.2 %collective-permute-start.33 = (bf16[4,128,128]{2,1,0:T(8,128)(2,1)S(1)}, bf16[4,128,128]{2,1,0:T(8,128)(2,1)S(1)}, u32[]{:S(2)}, u32[]{:S(2)}) collective-permute-start(bf16[4,128,128]{2,1,0:T(8,128)(2,1)S(1)} %add_convert_fusion.9), channel_id=1, source_target_pairs={{0,8},{2,6},{8,16},{10,2},{16,24},{18,10},{24,28},{26,18},{28,20},... | collective-permute-start | bytes 393224 | tf_op jit(solution)/shard_map/ppermute | solution.py:525

commit v2 on v1

--- a/solution.py
+++ b/solution.py
@@ -12,8 +12,7 @@
 GROUP = 4
 FIRST_SEND = 20
 FIRST_GRADS = 4
-COL, ROW, LIVE, OWNER, BASE, SHIFT, LOCAL, MINE, WAT = range(9)
-TABLE_ROWS = 16
+SMALL = 4 * 1024 * 1024
 PLACE, PART, STRIP, CIDX, CWAS, OIDX, OWAS = range(7)
 FIELDS = 7
 COLS_ROW = 3 * FIELDS
@@ -66,56 +65,59 @@
     return ahead, behind, swap
 
 
-def group_table(sz, where, counts, f, rank):
-    S, R, top = sz.slots, sz.ring, sz.top
-    lane = lax.iota(jnp.int32, sz.lanes)
-    kind = (lane >= S).astype(jnp.int32) + (lane >= 2 * S).astype(jnp.int32)
-    n = lane - kind * S
-    pad = sz.lanes - sz.all
-    w = jnp.pad(where, (0, pad))
-    limit = jnp.pad(jnp.repeat(counts, S, total_repeat_length=sz.all), (0, pad))
-    live = (n < limit) & (lane < sz.all)
-    down = kind == 2
-    row = jnp.where(down, w % sz.rb, w // sz.cb)
-    col = jnp.where(down, w // sz.rb, w % sz.cb)
-    owner = n // sz.nb
-
-    def position(chip):
-        return jnp.where(chip % 2 == 0, chip // 2, R - 1 - chip // 2)
-
-    away = position(owner // 2) - position(f // 2)
-    away = jnp.where(owner % 2 == 0, away, -away)
-    rel = (away + R) % R
-    j = jnp.where(rel > top, 2 * (rel - top) - 1, 2 * (top - rel))
-    j = jnp.where(rel == 0, R - 1, j)
-    base = jnp.where(owner % 2 == f % 2, 0, R) + j
-    shift = (row // sz.rbt - rank + sz.n_tensor) % sz.n_tensor
-    local = jnp.where(down, 0, sz.rbt) + row % sz.rbt
-    mine = (lane // sz.nb) * S + f * sz.nb + lane % sz.nb
-    at = kind * sz.nb + n % sz.nb
-    rows = [col, row, live.astype(jnp.int32), owner, base, shift, local, mine, at]
-    table = jnp.stack([r.astype(jnp.float32) for r in rows])
-    return jnp.pad(table, ((0, TABLE_ROWS - len(rows)), (0, 0)))
+def ratio(x, d):
+    return jnp.floor((x + 0.5) * (1.0 / d))
+
+
+def rest_of(x, d):
+    return x - d * ratio(x, d)
+
+
+def ring_position(sz, chip):
+    return jnp.where(rest_of(chip, 2) == 0, ratio(chip, 2), sz.ring - 1 - ratio(chip, 2))
 
 
 class Marks:
-    def __init__(self, sz, table):
+    def __init__(self, sz, own, raw):
         N, L, S = sz.all, sz.lanes, sz.slots
         f32 = jnp.float32
+        self.sz = sz
         self.sub = lax.broadcasted_iota(jnp.int32, (N, L), 0)
         self.lane = lax.broadcasted_iota(jnp.int32, (N, L), 1)
-        same = self.sub == self.lane
-        self.row = lambda i: table[i:i + 1, :]
-        self.col = lambda i: jnp.sum(jnp.where(same, table[i:i + 1, :], 0.0), axis=1, keepdims=True)
-        sub_c = self.sub[:, :1]
-        lane_r = self.lane[:1, :]
+        self.same = self.sub == self.lane
+        sub_c = self.sub[:, :1].astype(f32)
+        lane_r = lax.broadcasted_iota(jnp.int32, (1, L), 1).astype(f32)
+        self.sub_c, self.lane_r = sub_c, lane_r
+        raw_r = raw[...].astype(f32)
+        own_r = own[...].astype(f32)
+
+        def single(row, at):
+            return jnp.sum(jnp.where(lane_r == at, row, 0.0), axis=1, keepdims=True)
+
+        self.f, self.rank = single(own_r, N + 3), single(own_r, N + 4)
 
         def kind(x):
             return (x >= S).astype(f32) + (x >= 2 * S).astype(f32)
 
         self.kind_c, self.kind_r = kind(sub_c), kind(lane_r)
-        live_c, live_r = self.col(LIVE), self.row(LIVE)
-        self.same_col = (self.col(COL) == self.row(COL)).astype(f32)
+        self.n_r = lane_r - S * self.kind_r
+        self.n_c = sub_c - S * self.kind_c
+        limit = jnp.zeros((1, L), f32)
+        for k in range(3):
+            limit = limit + jnp.where(self.kind_r == k, single(raw_r, N + k), 0.0)
+        live_r = jnp.where((lane_r < N) & (self.n_r < limit), 1.0, 0.0)
+        w_c = self.col(raw_r)
+        live_c = self.col(live_r)
+
+        def place(w, k):
+            gate, down = ratio(w, sz.cb), ratio(w, sz.rb)
+            is_down = k == 2
+            return jnp.where(is_down, w - down * sz.rb, gate), jnp.where(is_down, down, w - gate * sz.cb)
+
+        self.row_c, col_c = place(w_c, self.kind_c)
+        self.row_r, col_r = place(raw_r, self.kind_r)
+        self.owner_c, self.owner_r = ratio(self.n_c, sz.nb), ratio(self.n_r, sz.nb)
+        self.same_col = (col_c == col_r).astype(f32)
         act_c, act_r = live_c, live_r
         for k in range(3):
             lanes = self.same_col * (live_r * (self.kind_r == k).astype(f32))
@@ -123,8 +125,8 @@
             subs = self.same_col * (live_c * (self.kind_c == k).astype(f32))
             act_r = act_r * jnp.max(subs, axis=0, keepdims=True)
         self.act_c, self.act_r = act_c, act_r
-        out_c = jnp.where(self.kind_c == 2, 0.0, f32(sz.rb)) + self.col(ROW)
-        out_r = jnp.where(self.kind_r == 2, 0.0, f32(sz.rb)) + self.row(ROW)
+        out_c = jnp.where(self.kind_c == 2, 0.0, f32(sz.rb)) + self.row_c
+        out_r = jnp.where(self.kind_r == 2, 0.0, f32(sz.rb)) + self.row_r
         self.same_out = (out_c == out_r).astype(f32)
         self.before = (self.lane < self.sub).astype(f32)
         self.after = (self.sub < self.lane).astype(f32)
@@ -132,6 +134,26 @@
         self.owas_r = jnp.max(self.same_out * self.after * act_c, axis=0, keepdims=True)
         self.lead_c = act_c * (1.0 - self.owas_c)
         self.lead_r = act_r * (1.0 - self.owas_r)
+        self.owned = (self.owner_c == self.owner_r).astype(f32)
+
+        def shift(row):
+            away = ratio(row, sz.rbt) - self.rank
+            return jnp.where(away < 0, away + sz.n_tensor, away)
+
+        self.shift_c, self.shift_r = shift(self.row_c), shift(self.row_r)
+        self.local_c = jnp.where(self.kind_c == 2, 0.0, f32(sz.rbt)) + rest_of(self.row_c, sz.rbt)
+
+    def col(self, row):
+        return jnp.sum(jnp.where(self.same, row, 0.0), axis=1, keepdims=True)
+
+    def base_c(self):
+        sz = self.sz
+        away = ring_position(sz, ratio(self.owner_c, 2)) - ring_position(sz, ratio(self.f, 2))
+        away = jnp.where(rest_of(self.owner_c, 2) == 0, away, -away)
+        rel = jnp.where(away < 0, away + sz.ring, away)
+        j = jnp.where(rel > sz.top, 2 * (rel - sz.top) - 1, 2 * (sz.top - rel))
+        j = jnp.where(rel == 0, sz.ring - 1.0, j)
+        return j + jnp.where(rest_of(self.owner_c, 2) == rest_of(self.f, 2), 0.0, float(sz.ring))
 
     def ranks(self, chosen_r):
         return jnp.sum(self.before * chosen_r, axis=1, keepdims=True)
@@ -141,8 +163,7 @@
         return jnp.sum(jnp.where(at, chosen_c[lo:hi] * value_c[lo:hi], 0.0), axis=0, keepdims=True)
 
     def most_owned(self):
-        owned = (self.col(OWNER) == self.row(OWNER)).astype(jnp.float32)
-        return jnp.max(jnp.sum(owned * self.act_r, axis=1, keepdims=True), axis=0, keepdims=True)
+        return jnp.max(jnp.sum(self.owned * self.act_r, axis=1, keepdims=True), axis=0, keepdims=True)
 
 
 def total(x):
@@ -157,11 +178,11 @@
     return row
 
 
-def plan_kernel(sz, table_ref, plan):
+def plan_kernel(sz, own, plan):
     S, N = sz.slots, sz.all
-    m = Marks(sz, table_ref)
+    m = Marks(sz, own, own)
     f32 = jnp.float32
-    lane_r = m.lane[:1, :].astype(f32)
+    lane_r, sub_c = m.lane_r, m.sub_c
     same_kind = (m.kind_c == m.kind_r).astype(f32)
     rank_c = jnp.sum(m.before * same_kind * m.act_r, axis=1, keepdims=True)
     cwas_c = jnp.max(m.before * same_kind * m.same_col * m.act_r, axis=1, keepdims=True)
@@ -171,14 +192,13 @@
     gates_r = m.act_r * (m.kind_r == 0).astype(f32)
     cidx_c = jnp.min(jnp.where(m.same_col * gates_r > 0, lanes_f, big), axis=1, keepdims=True)
     oidx_c = jnp.min(jnp.where(m.same_out * m.act_r > 0, lanes_f, big), axis=1, keepdims=True)
-    owned = (m.col(OWNER) == m.row(OWNER)).astype(f32)
-    pos_c = jnp.sum(m.before * owned * m.act_r, axis=1, keepdims=True)
-    base_c = m.col(BASE)
-    place_c = base_c * sz.chunk + m.col(WAT)
+    pos_c = jnp.sum(m.before * m.owned * m.act_r, axis=1, keepdims=True)
+    base_c = m.base_c()
+    place_c = base_c * sz.chunk + m.kind_c * sz.nb + rest_of(m.n_c, sz.nb)
     part_c = jnp.where(
         pos_c < sz.keep, base_c * sz.keep + pos_c, sz.main + base_c * sz.more + pos_c - sz.keep)
     fields = [
-        (place_c, sz.blocks), (part_c, sz.blocks), (m.col(ROW), 0), (cidx_c, S), (cwas_c, 0), (oidx_c, N), (m.owas_c, 0)]
+        (place_c, sz.blocks), (part_c, sz.blocks), (m.row_c, 0), (cidx_c, S), (cwas_c, 0), (oidx_c, N), (m.owas_c, 0)]
     rows = []
     head = []
     for k in range(3):
@@ -188,26 +208,24 @@
         for value, spare in fields:
             row = m.listed(m.act_c, rank_c, value, lo, hi)
             rows.append(jnp.where(lane_r < n_k, row, f32(spare)))
-    sub_c = m.sub[:, :1].astype(f32)
     leader_c = m.act_c * (1.0 - cwas_c) * (m.kind_c == 0).astype(f32)
     leader_r = m.act_r * (1.0 - cwas_r) * (m.kind_r == 0).astype(f32)
     rows.append(m.listed(leader_c, m.ranks(leader_r), sub_c, 0, S))
     head.append((HEAD_COLS, total(leader_c)))
     over = (m.most_owned() > sz.keep).astype(f32)
     lists = []
-    shift_c, shift_r = m.col(SHIFT), m.row(SHIFT)
     for s in range(sz.n_tensor):
-        chosen_c = m.lead_c * (shift_c == s).astype(f32)
-        chosen_r = m.lead_r * (shift_r == s).astype(f32)
+        chosen_c = m.lead_c * (m.shift_c == s).astype(f32)
+        chosen_r = m.lead_r * (m.shift_r == s).astype(f32)
         rank = m.ranks(chosen_r)
         lists.append(m.listed(chosen_c, rank, sub_c))
-        lists.append(m.listed(chosen_c, rank, m.col(LOCAL)))
+        lists.append(m.listed(chosen_c, rank, m.local_c))
         n = total(chosen_c)
         head.append((HEAD_LISTS + s, n))
         over = jnp.maximum(over, (n > sz.first).astype(f32))
     head.append((HEAD_OVER, over))
     rows.append(head_row(sz, head))
-    mine = m.sub.astype(f32) == m.row(MINE)
+    mine = sub_c == ratio(lane_r, sz.nb) * S + m.f * sz.nb + rest_of(lane_r, sz.nb)
     rows.append(jnp.sum(jnp.where(mine, m.act_c * (pos_c + 1.0), 0.0), axis=0, keepdims=True))
     rows += lists
     for i, row in enumerate(rows):
@@ -215,20 +233,19 @@
 
 
 def recv_kernel(sz, *refs):
-    tables, recv = refs[:-1], refs[-1]
+    own, raws, recv = refs[0], refs[1:-1], refs[-1]
     f32 = jnp.float32
     head = []
     over = jnp.zeros((1, 1), f32)
-    for s, table in enumerate(tables, 1):
-        m = Marks(sz, table)
-        shift_c, shift_r = m.col(SHIFT), m.row(SHIFT)
-        chosen_c = m.lead_c * (shift_c == 0).astype(f32)
-        chosen_r = m.lead_r * (shift_r == 0).astype(f32)
-        recv[s:s + 1, :] = m.listed(chosen_c, m.ranks(chosen_r), m.col(LOCAL)).astype(jnp.int32)
+    for s, raw in enumerate(raws, 1):
+        m = Marks(sz, own, raw)
+        chosen_c = m.lead_c * (m.shift_c == 0).astype(f32)
+        chosen_r = m.lead_r * (m.shift_r == 0).astype(f32)
+        recv[s:s + 1, :] = m.listed(chosen_c, m.ranks(chosen_r), m.local_c).astype(jnp.int32)
         head.append((HEAD_LISTS + s, total(chosen_c)))
         over = jnp.maximum(over, (m.most_owned() > sz.keep).astype(f32))
         for d in range(sz.n_tensor):
-            n = total(m.lead_c * (shift_c == d).astype(f32))
+            n = total(m.lead_c * (m.shift_c == d).astype(f32))
             over = jnp.maximum(over, (n > sz.first).astype(f32))
     head.append((HEAD_OVER, over))
     recv[0:1, :] = head_row(sz, head).astype(jnp.int32)
@@ -244,9 +261,9 @@
     chunks = refs[3:3 + n_chunks]
     refs = refs[3 + n_chunks:]
     T = sz.n_tensor
-    same, far, near, extra = refs[:4]
-    firsts, rests = refs[4:4 + T], refs[4 + T:4 + 2 * T]
-    (xs, wbuf, parts, gate_acc, up_acc, hg_acc, hid, gate_d, up_d, out_acc, stage, strip_sems, sems, rest_sems) = refs[4 + 2 * T:]
+    same, far, near, extra, _ = refs[:5]
+    firsts, rests = refs[5:5 + T], refs[5 + T:5 + 2 * T]
+    (xs, wbuf, parts, gate_acc, up_acc, hg_acc, hid, gate_d, up_d, out_acc, stage, strip_sems, sems, rest_sems) = refs[5 + 2 * T:]
 
     def field(k, j, e):
         return plan[k * FIELDS + j, e]
@@ -401,37 +418,51 @@
             lax.fori_loop(jnp.minimum(n, sz.first), n, late, None)
 
 
+def finish_kernel(sz, plan, here, ahead, behind, late, *outs):
+    for k in range(3):
+        for a in range(sz.nb):
+            at = plan[MINE_ROW, k * sz.nb + a]
+            p = jnp.minimum(jnp.maximum(at - 1, 0), sz.keep - 1)
+            value = here[p] + ahead[p].astype(jnp.float32) + behind[p].astype(jnp.float32)
+            if sz.more > 0:
+                q = jnp.minimum(jnp.maximum(at - 1 - sz.keep, 0), sz.more - 1)
+                value = jnp.where(at > sz.keep, late[q].astype(jnp.float32), value)
+            outs[k][0, a] = jnp.where(at > 0, value, 0.0).astype(jnp.bfloat16)
+
+
 def spec(space):
     return pl.BlockSpec(memory_space=space)
 
 
-ANY, VMEM, SMEM = pl.ANY, pltpu.VMEM, pltpu.SMEM
+ANY, HBM, VMEM, SMEM = pl.ANY, pltpu.HBM, pltpu.VMEM, pltpu.SMEM
 
 
 def cost(flops, moved):
     return pl.CostEstimate(flops=flops, bytes_accessed=moved, transcendentals=0)
 
 
-def call_plan(sz, table):
+def call_plan(sz, own):
     return pl.pallas_call(
         functools.partial(plan_kernel, sz),
         out_shape=jax.ShapeDtypeStruct((sz.plan_rows, sz.lanes), jnp.int32),
         in_specs=[spec(VMEM)],
         out_specs=spec(VMEM),
+        compiler_params=pltpu.CompilerParams(vmem_limit_bytes=SMALL),
         cost_estimate=cost(1_000_000, 4_000_000),
         name="plan",
-    )(table)
-
-
-def call_recv(sz, tables):
+    )(own)
+
+
+def call_recv(sz, own, raws):
     return pl.pallas_call(
         functools.partial(recv_kernel, sz),
         out_shape=jax.ShapeDtypeStruct((sz.recv_rows, sz.lanes), jnp.int32),
-        in_specs=[spec(VMEM)] * len(tables),
+        in_specs=[spec(VMEM)] * (1 + len(raws)),
         out_specs=spec(VMEM),
+        compiler_params=pltpu.CompilerParams(vmem_limit_bytes=SMALL),
         cost_estimate=cost(1_000_000, 4_000_000),
         name="recv",
-    )(*tables)
+    )(own, *raws)
 
 
 def call_compute(sz, plan, tokens, cot, chunks):
@@ -446,6 +477,7 @@
         blocks(sz.far * sz.keep),
         blocks((sz.ring - sz.far) * sz.keep),
         blocks(sz.blocks - sz.main),
+        blocks(sz.more),
     ]
     out_shape += [blocks(sz.first)] * T + [blocks(sz.rest)] * T
     scratch = [
@@ -465,7 +497,7 @@
     return pl.pallas_call(
         functools.partial(compute_kernel, sz),
         out_shape=out_shape,
-        in_specs=[spec(SMEM)] + [spec(ANY)] * (2 + len(chunks)),
+        in_specs=[spec(SMEM)] + [spec(HBM)] * 2 + [spec(ANY)] * len(chunks),
         out_specs=[spec(ANY)] * len(out_shape),
         scratch_shapes=[pltpu.VMEM(s, t) for s, t in scratch] + [
             pltpu.SemaphoreType.DMA((3 * sz.room,)),
@@ -475,7 +507,7 @@
         compiler_params=pltpu.CompilerParams(vmem_limit_bytes=held + 2 * 1024 * 1024),
         cost_estimate=cost(1_000_000_000, 20_000_000),
         name="compute",
-    )(plan, tokens, cot, *chunks)
+    )(plan, pltpu.with_memory_space_constraint(tokens, HBM), pltpu.with_memory_space_constraint(cot, HBM), *chunks)
 
 
 def call_join(sz, plan, recv, firsts, rests):
@@ -486,49 +518,69 @@
         in_specs=[spec(SMEM)] * 2 + [spec(VMEM)] * len(firsts) + [spec(ANY)] * len(rests),
         out_specs=[spec(VMEM), spec(VMEM)],
         scratch_shapes=[pltpu.VMEM((sz.tok, BLK), jnp.bfloat16), pltpu.SemaphoreType.DMA],
-        compiler_params=pltpu.CompilerParams(vmem_limit_bytes=16 * 1024 * 1024),
+        compiler_params=pltpu.CompilerParams(vmem_limit_bytes=10 * 1024 * 1024),
         cost_estimate=cost(1_000_000, 6_000_000),
         name="join",
     )(plan, recv, *firsts, *rests)
 
 
-def gather_chunks(sz, chunk, plan_of):
+def call_finish(sz, plan, here, ahead, behind, late):
+    out = jax.ShapeDtypeStruct((1, sz.nb, BLK, BLK), jnp.bfloat16)
+    return pl.pallas_call(
+        functools.partial(finish_kernel, sz),
+        out_shape=[out] * 3,
+        in_specs=[spec(SMEM)] + [spec(VMEM)] * 4,
+        out_specs=[spec(VMEM)] * 3,
+        compiler_params=pltpu.CompilerParams(vmem_limit_bytes=SMALL),
+        cost_estimate=cost(1_000_000, 1_000_000),
+        name="finish",
+    )(plan, here, ahead, behind, late)
+
+
+def gather_chunks(sz, chunk, plan_of, recv_of):
     ahead, behind, swap = permutations(sz)
     same = {0: chunk}
     a = b = chunk
     for s in range(1, sz.top + 1):
         if s == 2:
             (a, b), plan = lax.optimization_barrier(((a, b), plan_of()))
+        if s == 3 or s == sz.top < 3:
+            (a, b), recv = lax.optimization_barrier(((a, b), recv_of()))
         a = lax.ppermute(a, "fsdp", ahead)
         same[sz.ring - s] = a
         if s < sz.top:
             b = lax.ppermute(b, "fsdp", behind)
             same[s] = b
     other = {d: lax.ppermute(same[d], "fsdp", swap) for d in same}
-    return [side[d] for side in (same, other) for d in sz.order], plan
-
-
-def reduce_parts(sz, per, same, pair):
+    return [side[d] for side in (same, other) for d in sz.order], plan, recv
+
+
+def reduce_parts(sz, per, same, pair, beside=lambda a: a):
     ahead, behind, _ = permutations(sz)
 
-    def term(d, *more):
+    def wide(d, *more):
         j = sz.order.index(d)
         out = same[j * per:(j + 1) * per].astype(jnp.float32) + pair(j).astype(jnp.float32)
         for m in more:
             out = out + m.astype(jnp.float32)
-        return out.astype(jnp.bfloat16)
-
-    a, b = term(sz.top), term(sz.top + 1) if sz.top > 1 else None
+        return out
+
+    def term(d, *more):
+        return wide(d, *more).astype(jnp.bfloat16)
+
+    a, b = term(sz.top), term(sz.top + 1)
     for s in range(1, sz.top + 1):
-        if b is not None and s < sz.top:
+        if s < sz.top:
             a, b = lax.optimization_barrier((a, b))
+        else:
+            a = beside(a)
         a = lax.ppermute(a, "fsdp", ahead)
         if s < sz.top:
             b = lax.ppermute(b, "fsdp", behind)
             a = term(sz.top - s, a)
             if s + 1 < sz.top:
                 b = term(sz.top + 1 + s, b)
-    return term(0, a, b) if b is not None else term(0, a)
+    return wide(0), a, b
 
 
 def shards(
@@ -548,19 +600,21 @@
     _, _, swap = permutations(sz)
 
     chunk = jnp.concatenate([gate_blocks[0], up_blocks[0], down_blocks[0]])
-    where = jnp.concatenate([gate_where[0], up_where[0], down_where[0], block_counts[:, 0]])
-
-    def table_of(raw):
-        return group_table(sz, raw[:sz.all], raw[sz.all:], f, rank)
-
-    chunks, plan = gather_chunks(sz, chunk, lambda: call_plan(sz, table_of(where)))
-    theirs = [
-        lax.ppermute(where, "tensor", [(i, (i + s) % T) for i in range(T)]) for s in range(1, T)]
-    recv = call_recv(sz, [table_of(raw) for raw in theirs])
+    own = jnp.concatenate([
+        gate_where[0], up_where[0], down_where[0], block_counts[:, 0],
+        f.astype(jnp.int32)[None], rank.astype(jnp.int32)[None]])
+    own = jnp.pad(own, (0, sz.lanes - own.shape[0]))[None]
+
+    def recv_of():
+        raws = [
+            lax.ppermute(own, "tensor", [(i, (i + s) % T) for i in range(T)]) for s in range(1, T)]
+        return call_recv(sz, own, raws)
+
+    chunks, plan, recv = gather_chunks(sz, chunk, lambda: call_plan(sz, own), recv_of)
 
     outs = call_compute(sz, plan, tokens, cotangent, chunks)
-    same, far, near, extra = outs[:4]
-    firsts, rests = outs[4:4 + T], outs[4 + T:]
+    same, far, near, extra, idle = outs[:5]
+    firsts, rests = outs[5:5 + T], list(outs[5 + T:])
 
     def exchange(arrays):
         return [arrays[0]] + [
@@ -573,37 +627,31 @@
         at = j * sz.keep
         return far[at:at + sz.keep] if j < sz.far else near[at - sz.far * sz.keep:][:sz.keep]
 
-    grads = reduce_parts(sz, sz.keep, same, pair)
-
-    if sz.rest + sz.more > 0:
-        def spill(rests, extra):
+    late = idle
+
+    def beside(a):
+        nonlocal rests, late
+        if sz.rest + sz.more == 0:
+            return a
+
+        def spill(rests, extra, idle):
             moved = exchange(rests)
             if sz.more == 0:
-                return moved, extra
+                return moved, idle
             n = sz.ring * sz.more
             other = lax.ppermute(extra[n:], "fsdp", swap)
-            late = reduce_parts(sz, sz.more, extra[:n], lambda j: other[j * sz.more:(j + 1) * sz.more])
-            return moved, late
-
-        def none(rests, extra):
-            return list(rests), extra[:max(sz.more, 1)]
+            terms = reduce_parts(sz, sz.more, extra[:n], lambda j: other[j * sz.more:(j + 1) * sz.more])
+            return moved, sum(t.astype(jnp.float32) for t in terms).astype(jnp.bfloat16)
 
         over = plan[HEAD_ROW, HEAD_OVER] + recv[0, HEAD_OVER]
-        rests, late = lax.cond(over > 0, spill, none, list(rests), extra)
-        if sz.more > 0:
-            grads = jnp.concatenate([grads, late])
+        a, over, rests, more = lax.optimization_barrier((a, over, rests, extra))
+        rests, late = lax.cond(over > 0, spill, lambda r, e, i: (r, i), rests, more, idle)
+        return a
+
+    here, ahead, behind = reduce_parts(sz, sz.keep, same, pair, beside)
     outputs, input_grads = call_join(sz, plan, recv, firsts, rests)
-
-    def owned(i):
-        at = plan[MINE_ROW, i]
-        out = jnp.zeros((BLK, BLK), jnp.bfloat16)
-        for p in range(sz.chunk):
-            out = jnp.where(at == p + 1, grads[p], out)
-        return out
-
-    mine = [
-        jnp.stack([owned(k * sz.nb + a) for a in range(sz.nb)])[None] for k in range(3)]
-    return outputs, input_grads, *mine
+    grads = call_finish(sz, plan, here, ahead, behind, late)
+    return (outputs, input_grads, *grads)
 
 
 def solution(mesh):

time: 114 us -> 74.1 us (0.65)
  between operations: 24.7 us -> 2.07 us
  other arithmetic: 13.7 us -> 1.3 us
  local copies, waits for them, and re-layouts: 13 us -> 1.95 us
  waiting for transfers between devices: 25.3 us -> 30.9 us
  starting transfers between devices: 17.4 us -> 21.7 us
  Pallas kernels: 19.8 us -> 16.6 us
    unnamed x26 -> x0, local copies, waits for them, and re-layouts: 5.54 us -> none
    ppermute x1, waiting for transfers between devices: 0.01 us -> 5.21 us  [exchange(): lax.ppermute(arrays[s], 'tensor', [(i, (i + s) % T) for i in range(T)])]
    gather x1 -> x0, other arithmetic: 4.51 us -> none  [group_table(): limit = jnp.pad(jnp.repeat(counts, S, total_repeat_length=sz.all), (0, pad))]
    ppermute x4, starting transfers between devices: 5.16 us -> 8.61 us  [gather_chunks(): a = lax.ppermute(a, 'fsdp', ahead)]
    slice x4 -> x2, local copies, waits for them, and re-layouts: 4.2 us -> 1.16 us  [beside(): over = plan[HEAD_ROW, HEAD_OVER] + recv[0, HEAD_OVER]]
    convert_element_type x7 -> x3, other arithmetic: 2.95 us -> 0.24 us  [term(): return wide(d, *more).astype(jnp.bfloat16)]
    gather x2 -> x0, local copies, waits for them, and re-layouts: 2 us -> none  [group_table(): limit = jnp.pad(jnp.repeat(counts, S, total_repeat_length=sz.all), (0, pad))]
    broadcast_in_dim x3 -> x0, other arithmetic: 1.91 us -> none  [shards(): jnp.stack([owned(k * sz.nb + a) for a in range(sz.nb)])[None]]
  transfers between devices with their start and end apart: 26 -> 26, of which waited for: 10 -> 15; matrix products, arithmetic and copies ran while one was open for 15% -> 3% of each run, Pallas kernels for 4% -> 4%
where the time goes in v2:
time: 74.1 us; the launch traced here: 74.6 us
  waiting for transfers between devices  30.9 us (42%)
  starting transfers between devices  21.7 us (29%)
  Pallas kernels  16.6 us (22%)
  between operations  2.07 us (3%)
  local copies, waits for them, and re-layouts  1.95 us (3%)
  other arithmetic  1.3 us (2%)
    pallas_call x1, Pallas kernels, call_compute(): pl.pallas_call(functools.partial(compute_kernel, sz), out_shape=out_shape...  11.6 us
    ppermute x4, waiting for transfers between devices, gather_chunks(): a = lax.ppermute(a, 'fsdp', ahead)  10.1 us
    ppermute x4, starting transfers between devices, gather_chunks(): a = lax.ppermute(a, 'fsdp', ahead)  8.61 us
    ppermute x3, waiting for transfers between devices, reduce_parts(): b = lax.ppermute(b, 'fsdp', behind)  7.23 us
    ppermute x3, starting transfers between devices, reduce_parts(): b = lax.ppermute(b, 'fsdp', behind)  6.35 us
    ppermute x1, waiting for transfers between devices, exchange(): lax.ppermute(arrays[s], 'tensor', [(i, (i + s) % T) for i in range(T)])  5.21 us
    ppermute x4, waiting for transfers between devices, reduce_parts(): a = lax.ppermute(a, 'fsdp', ahead)  3.25 us
    pallas_call x1, Pallas kernels, call_join(): pl.pallas_call(functools.partial(join_kernel, sz), out_shape=[half, half]...  2.74 us
  transfers between devices with their start and end apart: 26, of which 15 were waited for; matrix products, arithmetic and copies ran while one was open for 3% of the time, Pallas kernels for 4%

profile of v2, /device:TPU:0, one launch (start us, length us, event | category | flops | bytes accessed | tf_op | source)
XLA Modules:
  0.0 74.6 jit_solution(16991432668114300126)
XLA Ops:
  0.6 0.9 %pad_maximum_fusion.refs_10_ = bf16[6,128,128]{2,1,0:T(8,128)(2,1)S(1)} fusion(bf16[2,128,128]{2,1,0:T(8,128)(2,1)} %bitcast.12, bf16[2,128,128]{2,1,0:T(8,128)(2,1)} %bitcast.13, bf16[2,128,128]{2,1,0:T(8,128)(2,1)} %bitcast.14), kind=kLoop, calls=%fused_computation.16 | loop fusion | flops 196608 | bytes 393216 | tf_op jit(solution)/shard_map/concatenate | solution.py:602
  1.6 3.1 %collective-permute-start.9 = (bf16[6,128,128]{2,1,0:T(8,128)(2,1)S(1)}, bf16[6,128,128]{2,1,0:T(8,128)(2,1)S(1)}, u32[]{:S(2)}, u32[]{:S(2)}) collective-permute-start(bf16[6,128,128]{2,1,0:T(8,128)(2,1)S(1)} %pad_maximum_fusion.refs_10_), channel_id=1, source_target_pairs={{0,8},{2,6},{8,16},{10,2},{16,24},{18,10},{24,28},{26,18},{28,20},... | collective-permute-start | bytes 589832 | tf_op jit(solution)/shard_map/ppermute | solution.py:549
  4.6 0.0 collective-permute-start.10
  4.6 0.8 %concatenate.7 = s32[101]{0:T(128)S(1)} concatenate(s32[32]{0:T(128)} %bitcast.15, s32[32]{0:T(128)} %bitcast.16, s32[32]{0:T(128)} %bitcast.17, s32[3]{0:T(128)} %bitcast.18, s32[1]{0:T(128)} %bitcast.7, s32[1]{0:T(128)} %bitcast.8), dimensions={0} | concatenate | bytes 808 | tf_op jit(solution)/shard_map/concatenate | solution.py:603
  5.4 0.5 plan.1.refs_0_
  5.9 3.9 %collective-permute-done.9.refs_8_ = bf16[6,128,128]{2,1,0:T(8,128)(2,1)S(1)} collective-permute-done((bf16[6,128,128]{2,1,0:T(8,128)(2,1)S(1)}, bf16[6,128,128]{2,1,0:T(8,128)(2,1)S(1)}, u32[]{:S(2)}, u32[]{:S(2)}) %collective-permute-start.9) | collective-permute-done | bytes 196640 | tf_op jit(solution)/shard_map/ppermute | solution.py:549
  9.8 0.5 collective-permute-done.10.refs_9_
  10.3 1.6 %collective-permute-start.11 = (bf16[6,128,128]{2,1,0:T(8,128)(2,1)S(1)}, bf16[6,128,128]{2,1,0:T(8,128)(2,1)S(1)}, u32[]{:S(2)}, u32[]{:S(2)}) collective-permute-start(bf16[6,128,128]{2,1,0:T(8,128)(2,1)S(1)} %collective-permute-done.9.refs_8_), channel_id=1, source_target_pairs={{0,8},{2,6},{8,16},{10,2},{16,24},{18,10},{24,28},{26,18},{28,20},... | collective-permute-start | bytes 589832 | tf_op jit(solution)/shard_map/ppermute | solution.py:549
  11.9 0.4 collective-permute-start.12
  12.3 1.9 %collective-permute-start.13 = (s32[1,128]{1,0:T(1,128)S(1)}, s32[1,128]{1,0:T(1,128)S(1)}, u32[]{:S(2)}, u32[]{:S(2)}) collective-permute-start(s32[1,128]{1,0:T(1,128)S(1)} %pad_bitcast_fusion.own.refs_0_), channel_id=1, source_target_pairs={{0,1},{1,0},{2,3},{3,2},{4,5},{5,4},{6,7},{7,6},{8,9},{9,8},{10,11... | collective-permute-start | bytes 1544 | tf_op jit(solution)/shard_map/ppermute | solution.py:610
  14.3 1.6 %collective-permute-done.13.refs_1_ = s32[1,128]{1,0:T(1,128)S(1)} collective-permute-done((s32[1,128]{1,0:T(1,128)S(1)}, s32[1,128]{1,0:T(1,128)S(1)}, u32[]{:S(2)}, u32[]{:S(2)}) %collective-permute-start.13) | collective-permute-done | bytes 544 | tf_op jit(solution)/shard_map/ppermute | solution.py:610
  15.9 0.3 recv.1.refs_1_
  16.2 1.2 %collective-permute-done.11.refs_6_ = bf16[6,128,128]{2,1,0:T(8,128)(2,1)S(1)} collective-permute-done((bf16[6,128,128]{2,1,0:T(8,128)(2,1)S(1)}, bf16[6,128,128]{2,1,0:T(8,128)(2,1)S(1)}, u32[]{:S(2)}, u32[]{:S(2)}) %collective-permute-start.11) | collective-permute-done | bytes 196640 | tf_op jit(solution)/shard_map/ppermute | solution.py:549
  17.4 0.2 collective-permute-done.12.refs_7_
  17.6 1.6 %collective-permute-start.14 = (bf16[6,128,128]{2,1,0:T(8,128)(2,1)S(1)}, bf16[6,128,128]{2,1,0:T(8,128)(2,1)S(1)}, u32[]{:S(2)}, u32[]{:S(2)}) collective-permute-start(bf16[6,128,128]{2,1,0:T(8,128)(2,1)S(1)} %collective-permute-done.11.refs_6_), channel_id=1, source_target_pairs={{0,8},{2,6},{8,16},{10,2},{16,24},{18,10},{24,28},{26,18},{28,20},... | collective-permute-start | bytes 589832 | tf_op jit(solution)/shard_map/ppermute | solution.py:549
  19.1 0.4 collective-permute-start.24
  19.5 0.1 collective-permute-start.22
  19.6 0.4 collective-permute-start.23
  20.0 1.6 %collective-permute-start.16 = (bf16[6,128,128]{2,1,0:T(8,128)(2,1)S(1)}, bf16[6,128,128]{2,1,0:T(8,128)(2,1)S(1)}, u32[]{:S(2)}, u32[]{:S(2)}) collective-permute-start(bf16[6,128,128]{2,1,0:T(8,128)(2,1)S(1)} %collective-permute-done.12.refs_7_), channel_id=1, source_target_pairs={{0,4},{2,10},{8,0},{10,18},{16,8},{18,26},{24,16},{26,30},{28,24},... | collective-permute-start | bytes 589832 | tf_op jit(solution)/shard_map/ppermute | solution.py:552
  21.6 2.1 %collective-permute-done.14.refs_4_ = bf16[6,128,128]{2,1,0:T(8,128)(2,1)S(1)} collective-permute-done((bf16[6,128,128]{2,1,0:T(8,128)(2,1)S(1)}, bf16[6,128,128]{2,1,0:T(8,128)(2,1)S(1)}, u32[]{:S(2)}, u32[]{:S(2)}) %collective-permute-start.14) | collective-permute-done | bytes 196640 | tf_op jit(solution)/shard_map/ppermute | solution.py:549
  23.7 2.4 %collective-permute-start.15 = (bf16[6,128,128]{2,1,0:T(8,128)(2,1)S(1)}, bf16[6,128,128]{2,1,0:T(8,128)(2,1)S(1)}, u32[]{:S(2)}, u32[]{:S(2)}) collective-permute-start(bf16[6,128,128]{2,1,0:T(8,128)(2,1)S(1)} %collective-permute-done.14.refs_4_), channel_id=1, source_target_pairs={{0,8},{2,6},{8,16},{10,2},{16,24},{18,10},{24,28},{26,18},{28,20},... | collective-permute-start | bytes 589832 | tf_op jit(solution)/shard_map/ppermute | solution.py:549
  26.1 0.0 collective-permute-done.24.refs_18_
  26.1 0.0 collective-permute-start.20
  26.1 0.0 collective-permute-done.22.refs_16_
  26.1 0.5 collective-permute-start.21
  26.6 0.0 collective-permute-done.23.refs_17_
  26.6 0.1 collective-permute-start.18
  26.7 0.0 collective-permute-done.16.refs_5_
  26.7 0.4 collective-permute-start.19
  27.1 2.9 %collective-permute-done.15.refs_3_ = bf16[6,128,128]{2,1,0:T(8,128)(2,1)S(1)} collective-permute-done((bf16[6,128,128]{2,1,0:T(8,128)(2,1)S(1)}, bf16[6,128,128]{2,1,0:T(8,128)(2,1)S(1)}, u32[]{:S(2)}, u32[]{:S(2)}) %collective-permute-start.15) | collective-permute-done | bytes 196640 | tf_op jit(solution)/shard_map/ppermute | solution.py:549
  30.0 0.0 collective-permute-start.17
  30.0 0.0 collective-permute-done.20.refs_14_
  30.0 0.0 collective-permute-done.21.refs_15_
  30.0 0.0 collective-permute-done.18.refs_12_
  30.1 0.0 collective-permute-done.19.refs_13_
  30.1 1.4 %collective-permute-done.17.refs_11_ = bf16[6,128,128]{2,1,0:T(8,128)(2,1)S(1)} collective-permute-done((bf16[6,128,128]{2,1,0:T(8,128)(2,1)S(1)}, bf16[6,128,128]{2,1,0:T(8,128)(2,1)S(1)}, u32[]{:S(2)}, u32[]{:S(2)}) %collective-permute-start.17) | collective-permute-done | bytes 196640 | tf_op jit(solution)/shard_map/ppermute | solution.py:554
  31.5 11.6 %compute.1 = (bf16[32,128,128]{2,1,0:T(8,128)(2,1)S(1)}, bf16[16,128,128]{2,1,0:T(8,128)(2,1)S(1)}, bf16[16,128,128]{2,1,0:T(8,128)(2,1)S(1)}, bf16[32,128,128]{...) custom-call(s32[32,128]{1,0:T(8,128)S(1)} %plan.1.refs_0_, ...), custom_call_target="tpu_custom_call" | custom-call | flops 1000000000 | bytes 20000000 | tf_op jit(solution)/shard_map/compute/pallas_call | solution.py:497
  43.1 0.2 collective-permute-start.27
  43.3 0.4 collective-permute-start.26
  43.6 1.4 %collective-permute-done.27 = bf16[16,128,128]{2,1,0:T(8,128)(2,1)S(1)} collective-permute-done((bf16[16,128,128]{2,1,0:T(8,128)(2,1)S(1)}, bf16[16,128,128]{2,1,0:T(8,128)(2,1)S(1)}, u32[]{:S(2)}, u32[]{:S(2)}) %collective-permute-start.27) | collective-permute-done | bytes 524320 | tf_op jit(solution)/shard_map/ppermute | solution.py:623
  45.0 0.1 add_convert_fusion.13
  45.1 2.2 %collective-permute-start.29 = (bf16[4,128,128]{2,1,0:T(8,128)(2,1)S(1)}, bf16[4,128,128]{2,1,0:T(8,128)(2,1)S(1)}, u32[]{:S(2)}, u32[]{:S(2)}) collective-permute-start(bf16[4,128,128]{2,1,0:T(8,128)(2,1)S(1)} %get-tuple-element.66), channel_id=1, source_target_pairs={{0,4},{2,10},{8,0},{10,18},{16,8},{18,26},{24,16},{26,30},{28,24},... | collective-permute-start | bytes 393224 | tf_op jit(solution)/shard_map/ppermute | solution.py:579
  47.3 0.0 collective-permute-start.28
  47.3 3.1 %collective-permute-done.29 = bf16[4,128,128]{2,1,0:T(8,128)(2,1)S(1)} collective-permute-done((bf16[4,128,128]{2,1,0:T(8,128)(2,1)S(1)}, bf16[4,128,128]{2,1,0:T(8,128)(2,1)S(1)}, u32[]{:S(2)}, u32[]{:S(2)}) %collective-permute-start.29) | collective-permute-done | bytes 131104 | tf_op jit(solution)/shard_map/ppermute | solution.py:579
  50.4 1.8 %collective-permute-done.28 = bf16[4,128,128]{2,1,0:T(8,128)(2,1)S(1)} collective-permute-done((bf16[4,128,128]{2,1,0:T(8,128)(2,1)S(1)}, bf16[4,128,128]{2,1,0:T(8,128)(2,1)S(1)}, u32[]{:S(2)}, u32[]{:S(2)}) %collective-permute-start.28) | collective-permute-done | bytes 131104 | tf_op jit(solution)/shard_map/ppermute | solution.py:577
  52.3 0.1 add_convert_fusion.11
  52.4 2.1 %collective-permute-start.31 = (bf16[4,128,128]{2,1,0:T(8,128)(2,1)S(1)}, bf16[4,128,128]{2,1,0:T(8,128)(2,1)S(1)}, u32[]{:S(2)}, u32[]{:S(2)}) collective-permute-start(bf16[4,128,128]{2,1,0:T(8,128)(2,1)S(1)} %get-tuple-element.68), channel_id=1, source_target_pairs={{0,4},{2,10},{8,0},{10,18},{16,8},{18,26},{24,16},{26,30},{28,24},... | collective-permute-start | bytes 393224 | tf_op jit(solution)/shard_map/ppermute | solution.py:579
  54.5 0.0 collective-permute-start.30
  54.5 0.2 collective-permute-start.25
  54.7 0.0 collective-permute-done.26
  54.7 4.1 %collective-permute-done.31 = bf16[4,128,128]{2,1,0:T(8,128)(2,1)S(1)} collective-permute-done((bf16[4,128,128]{2,1,0:T(8,128)(2,1)S(1)}, bf16[4,128,128]{2,1,0:T(8,128)(2,1)S(1)}, u32[]{:S(2)}, u32[]{:S(2)}) %collective-permute-start.31) | collective-permute-done | bytes 131104 | tf_op jit(solution)/shard_map/ppermute | solution.py:579
  58.8 0.6 collective-permute-done.30
  59.4 0.1 convert_add_fusion
  59.6 0.1 collective-permute-start.32
  59.6 0.6 slice.132
  60.2 0.6 slice.133
  62.1 2.1 %collective-permute-start.34 = (bf16[4,128,128]{2,1,0:T(8,128)(2,1)S(1)}, bf16[4,128,128]{2,1,0:T(8,128)(2,1)S(1)}, u32[]{:S(2)}, u32[]{:S(2)}) collective-permute-start(bf16[4,128,128]{2,1,0:T(8,128)(2,1)S(1)} %get-tuple-element.82), channel_id=1, source_target_pairs={{0,4},{2,10},{8,0},{10,18},{16,8},{18,26},{24,16},{26,30},{28,24},... | collective-permute-start | bytes 393224 | tf_op jit(solution)/shard_map/ppermute | solution.py:579
  64.2 0.8 %collective-permute-done.32 = bf16[4,128,128]{2,1,0:T(8,128)(2,1)S(1)} collective-permute-done((bf16[4,128,128]{2,1,0:T(8,128)(2,1)S(1)}, bf16[4,128,128]{2,1,0:T(8,128)(2,1)S(1)}, u32[]{:S(2)}, u32[]{:S(2)}) %collective-permute-start.32) | collective-permute-done | bytes 131104 | tf_op jit(solution)/shard_map/ppermute | solution.py:577
  64.9 0.1 add_convert_fusion.8
  65.0 0.1 collective-permute-start.33
  65.1 5.2 %collective-permute-done.25.refs_3_ = bf16[20,128,128]{2,1,0:T(8,128)(2,1)S(1)} collective-permute-done((bf16[20,128,128]{2,1,0:T(8,128)(2,1)}, bf16[20,128,128]{2,1,0:T(8,128)(2,1)S(1)}, u32[]{:S(2)}, u32[]{:S(2)}) %collective-permute-start.25) | collective-permute-done | bytes 655392 | tf_op jit(solution)/shard_map/ppermute | solution.py:621
  70.3 2.7 %join.1 = (bf16[128,4096]{1,0:T(8,128)(2,1)}, bf16[128,4096]{1,0:T(8,128)(2,1)}) custom-call(s32[32,128]{1,0:T(8,128)S(1)} %plan.1.refs_0_, s32[8,128]{1,0:T(8,128)S(1)} %recv.1.refs_1_, bf16[20,128,128]{2,1,0:T(8,128)(2,1)S(1)} %get-tuple-element.60.refs_2_, bf16[20,128,128]{2,1,0:T(8,128)(2,1)S(1)} %collective-permute-done.25.refs_3_, ...), custom_call_target="tpu_custom_call" | custom-call | flops 1000000 | bytes 6000000 | tf_op jit(solution)/shard_map/join/pallas_call | solution.py:515
  73.0 0.0 collective-permute-done.34.behind
  73.1 1.5 %finish.1 = (bf16[1,2,128,128]{3,2,1,0:T(8,128)(2,1)}, bf16[1,2,128,128]{3,2,1,0:T(8,128)(2,1)}, bf16[1,2,128,128]{3,2,1,0:T(8,128)(2,1)}) custom-call(s32[32,128]{1,0:T(8,128)S(1)} %plan.1.refs_0_, f32[4,128,128]{2,1,0:T(8,128)S(1)} %get-tuple-element.93.here, bf16[4,128,128]{2,1,0:T(8,128)(2,1)S(1)} %collective-permute-done.33.ahead, ...), custom_call_target="tpu_custom_call" | custom-call | flops 1000000 | bytes 1000000 | tf_op jit(solution)/shard_map/finish/pallas_call | solution.py:529
  (3 shorter events, 0.0 us)
Async XLA Ops:
  1.6 8.2 %collective-permute-start.9 = (bf16[6,128,128]{2,1,0:T(8,128)(2,1)S(1)}, bf16[6,128,128]{2,1,0:T(8,128)(2,1)S(1)}, u32[]{:S(2)}, u32[]{:S(2)}) collective-permute-start(bf16[6,128,128]{2,1,0:T(8,128)(2,1)S(1)} %pad_maximum_fusion.refs_10_), channel_id=1, source_target_pairs={{0,8},{2,6},{8,16},{10,2},{16,24},{18,10},{24,28},{26,18},{28,20},... | collective-permute-start | bytes 589832 | tf_op jit(solution)/shard_map/ppermute | solution.py:549
  4.6 5.7 %collective-permute-start.10 = (bf16[6,128,128]{2,1,0:T(8,128)(2,1)S(1)}, bf16[6,128,128]{2,1,0:T(8,128)(2,1)S(1)}, u32[]{:S(2)}, u32[]{:S(2)}) collective-permute-start(bf16[6,128,128]{2,1,0:T(8,128)(2,1)S(1)} %pad_maximum_fusion.refs_10_), channel_id=1, source_target_pairs={{0,4},{2,10},{8,0},{10,18},{16,8},{18,26},{24,16},{26,30},{28,24},... | collective-permute-start | bytes 589832 | tf_op jit(solution)/shard_map/ppermute | solution.py:552
  10.3 7.1 %collective-permute-start.11 = (bf16[6,128,128]{2,1,0:T(8,128)(2,1)S(1)}, bf16[6,128,128]{2,1,0:T(8,128)(2,1)S(1)}, u32[]{:S(2)}, u32[]{:S(2)}) collective-permute-start(bf16[6,128,128]{2,1,0:T(8,128)(2,1)S(1)} %collective-permute-done.9.refs_8_), channel_id=1, source_target_pairs={{0,8},{2,6},{8,16},{10,2},{16,24},{18,10},{24,28},{26,18},{28,20},... | collective-permute-start | bytes 589832 | tf_op jit(solution)/shard_map/ppermute | solution.py:549
  11.9 5.7 %collective-permute-start.12 = (bf16[6,128,128]{2,1,0:T(8,128)(2,1)S(1)}, bf16[6,128,128]{2,1,0:T(8,128)(2,1)S(1)}, u32[]{:S(2)}, u32[]{:S(2)}) collective-permute-start(bf16[6,128,128]{2,1,0:T(8,128)(2,1)S(1)} %collective-permute-done.10.refs_9_), channel_id=1, source_target_pairs={{0,4},{2,10},{8,0},{10,18},{16,8},{18,26},{24,16},{26,30},{28,24},... | collective-permute-start | bytes 589832 | tf_op jit(solution)/shard_map/ppermute | solution.py:552
  12.3 3.5 %collective-permute-start.13 = (s32[1,128]{1,0:T(1,128)S(1)}, s32[1,128]{1,0:T(1,128)S(1)}, u32[]{:S(2)}, u32[]{:S(2)}) collective-permute-start(s32[1,128]{1,0:T(1,128)S(1)} %pad_bitcast_fusion.own.refs_0_), channel_id=1, source_target_pairs={{0,1},{1,0},{2,3},{3,2},{4,5},{5,4},{6,7},{7,6},{8,9},{9,8},{10,11... | collective-permute-start | bytes 1544 | tf_op jit(solution)/shard_map/ppermute | solution.py:610
  17.6 6.2 %collective-permute-start.14 = (bf16[6,128,128]{2,1,0:T(8,128)(2,1)S(1)}, bf16[6,128,128]{2,1,0:T(8,128)(2,1)S(1)}, u32[]{:S(2)}, u32[]{:S(2)}) collective-permute-start(bf16[6,128,128]{2,1,0:T(8,128)(2,1)S(1)} %collective-permute-done.11.refs_6_), channel_id=1, source_target_pairs={{0,8},{2,6},{8,16},{10,2},{16,24},{18,10},{24,28},{26,18},{28,20},... | collective-permute-start | bytes 589832 | tf_op jit(solution)/shard_map/ppermute | solution.py:549
  19.1 7.0 %collective-permute-start.24 = (bf16[6,128,128]{2,1,0:T(8,128)(2,1)S(1)}, bf16[6,128,128]{2,1,0:T(8,128)(2,1)S(1)}, u32[]{:S(2)}, u32[]{:S(2)}) collective-permute-start(bf16[6,128,128]{2,1,0:T(8,128)(2,1)S(1)} %pad_maximum_fusion.refs_10_), channel_id=1, source_target_pairs={{0,2},{2,0},{8,10},{10,8},{16,18},{18,16},{24,26},{26,24},{28,30},... | collective-permute-start | bytes 589832 | tf_op jit(solution)/shard_map/ppermute | solution.py:554
  19.5 6.6 %collective-permute-start.22 = (bf16[6,128,128]{2,1,0:T(8,128)(2,1)S(1)}, bf16[6,128,128]{2,1,0:T(8,128)(2,1)S(1)}, u32[]{:S(2)}, u32[]{:S(2)}) collective-permute-start(bf16[6,128,128]{2,1,0:T(8,128)(2,1)S(1)} %collective-permute-done.9.refs_8_), channel_id=1, source_target_pairs={{0,2},{2,0},{8,10},{10,8},{16,18},{18,16},{24,26},{26,24},{28,30},... | collective-permute-start | bytes 589832 | tf_op jit(solution)/shard_map/ppermute | solution.py:554
  19.6 7.0 %collective-permute-start.23 = (bf16[6,128,128]{2,1,0:T(8,128)(2,1)S(1)}, bf16[6,128,128]{2,1,0:T(8,128)(2,1)S(1)}, u32[]{:S(2)}, u32[]{:S(2)}) collective-permute-start(bf16[6,128,128]{2,1,0:T(8,128)(2,1)S(1)} %collective-permute-done.10.refs_9_), channel_id=1, source_target_pairs={{0,2},{2,0},{8,10},{10,8},{16,18},{18,16},{24,26},{26,24},{28,30},... | collective-permute-start | bytes 589832 | tf_op jit(solution)/shard_map/ppermute | solution.py:554
  20.0 6.7 %collective-permute-start.16 = (bf16[6,128,128]{2,1,0:T(8,128)(2,1)S(1)}, bf16[6,128,128]{2,1,0:T(8,128)(2,1)S(1)}, u32[]{:S(2)}, u32[]{:S(2)}) collective-permute-start(bf16[6,128,128]{2,1,0:T(8,128)(2,1)S(1)} %collective-permute-done.12.refs_7_), channel_id=1, source_target_pairs={{0,4},{2,10},{8,0},{10,18},{16,8},{18,26},{24,16},{26,30},{28,24},... | collective-permute-start | bytes 589832 | tf_op jit(solution)/shard_map/ppermute | solution.py:552
  23.7 6.3 %collective-permute-start.15 = (bf16[6,128,128]{2,1,0:T(8,128)(2,1)S(1)}, bf16[6,128,128]{2,1,0:T(8,128)(2,1)S(1)}, u32[]{:S(2)}, u32[]{:S(2)}) collective-permute-start(bf16[6,128,128]{2,1,0:T(8,128)(2,1)S(1)} %collective-permute-done.14.refs_4_), channel_id=1, source_target_pairs={{0,8},{2,6},{8,16},{10,2},{16,24},{18,10},{24,28},{26,18},{28,20},... | collective-permute-start | bytes 589832 | tf_op jit(solution)/shard_map/ppermute | solution.py:549
  26.1 3.9 %collective-permute-start.20 = (bf16[6,128,128]{2,1,0:T(8,128)(2,1)S(1)}, bf16[6,128,128]{2,1,0:T(8,128)(2,1)S(1)}, u32[]{:S(2)}, u32[]{:S(2)}) collective-permute-start(bf16[6,128,128]{2,1,0:T(8,128)(2,1)S(1)} %collective-permute-done.11.refs_6_), channel_id=1, source_target_pairs={{0,2},{2,0},{8,10},{10,8},{16,18},{18,16},{24,26},{26,24},{28,30},... | collective-permute-start | bytes 589832 | tf_op jit(solution)/shard_map/ppermute | solution.py:554
  26.1 3.9 %collective-permute-start.21 = (bf16[6,128,128]{2,1,0:T(8,128)(2,1)S(1)}, bf16[6,128,128]{2,1,0:T(8,128)(2,1)S(1)}, u32[]{:S(2)}, u32[]{:S(2)}) collective-permute-start(bf16[6,128,128]{2,1,0:T(8,128)(2,1)S(1)} %collective-permute-done.12.refs_7_), channel_id=1, source_target_pairs={{0,2},{2,0},{8,10},{10,8},{16,18},{18,16},{24,26},{26,24},{28,30},... | collective-permute-start | bytes 589832 | tf_op jit(solution)/shard_map/ppermute | solution.py:554
  26.6 3.4 %collective-permute-start.18 = (bf16[6,128,128]{2,1,0:T(8,128)(2,1)S(1)}, bf16[6,128,128]{2,1,0:T(8,128)(2,1)S(1)}, u32[]{:S(2)}, u32[]{:S(2)}) collective-permute-start(bf16[6,128,128]{2,1,0:T(8,128)(2,1)S(1)} %collective-permute-done.14.refs_4_), channel_id=1, source_target_pairs={{0,2},{2,0},{8,10},{10,8},{16,18},{18,16},{24,26},{26,24},{28,30},... | collective-permute-start | bytes 589832 | tf_op jit(solution)/shard_map/ppermute | solution.py:554
  26.7 3.4 %collective-permute-start.19 = (bf16[6,128,128]{2,1,0:T(8,128)(2,1)S(1)}, bf16[6,128,128]{2,1,0:T(8,128)(2,1)S(1)}, u32[]{:S(2)}, u32[]{:S(2)}) collective-permute-start(bf16[6,128,128]{2,1,0:T(8,128)(2,1)S(1)} %collective-permute-done.16.refs_5_), channel_id=1, source_target_pairs={{0,2},{2,0},{8,10},{10,8},{16,18},{18,16},{24,26},{26,24},{28,30},... | collective-permute-start | bytes 589832 | tf_op jit(solution)/shard_map/ppermute | solution.py:554
  30.0 1.4 %collective-permute-start.17 = (bf16[6,128,128]{2,1,0:T(8,128)(2,1)S(1)}, bf16[6,128,128]{2,1,0:T(8,128)(2,1)S(1)}, u32[]{:S(2)}, u32[]{:S(2)}) collective-permute-start(bf16[6,128,128]{2,1,0:T(8,128)(2,1)S(1)} %collective-permute-done.15.refs_3_), channel_id=1, source_target_pairs={{0,2},{2,0},{8,10},{10,8},{16,18},{18,16},{24,26},{26,24},{28,30},... | collective-permute-start | bytes 589832 | tf_op jit(solution)/shard_map/ppermute | solution.py:554
  43.1 2.0 %collective-permute-start.27 = (bf16[16,128,128]{2,1,0:T(8,128)(2,1)S(1)}, bf16[16,128,128]{2,1,0:T(8,128)(2,1)S(1)}, u32[]{:S(2)}, u32[]{:S(2)}) collective-permute-start(bf16[16,128,128]{2,1,0:T(8,128)(2,1)S(1)} %get-tuple-element.64), channel_id=1, source_target_pairs={{0,2},{2,0},{8,10},{10,8},{16,18},{18,16},{24,26},{26,24},{28,30},... | collective-permute-start | bytes 1572872 | tf_op jit(solution)/shard_map/ppermute | solution.py:623
  43.3 11.4 %collective-permute-start.26 = (bf16[16,128,128]{2,1,0:T(8,128)(2,1)S(1)}, bf16[16,128,128]{2,1,0:T(8,128)(2,1)S(1)}, u32[]{:S(2)}, u32[]{:S(2)}) collective-permute-start(bf16[16,128,128]{2,1,0:T(8,128)(2,1)S(1)} %get-tuple-element.63), channel_id=1, source_target_pairs={{0,2},{2,0},{8,10},{10,8},{16,18},{18,16},{24,26},{26,24},{28,30},... | collective-permute-start | bytes 1572872 | tf_op jit(solution)/shard_map/ppermute | solution.py:623
  45.1 5.3 %collective-permute-start.29 = (bf16[4,128,128]{2,1,0:T(8,128)(2,1)S(1)}, bf16[4,128,128]{2,1,0:T(8,128)(2,1)S(1)}, u32[]{:S(2)}, u32[]{:S(2)}) collective-permute-start(bf16[4,128,128]{2,1,0:T(8,128)(2,1)S(1)} %get-tuple-element.66), channel_id=1, source_target_pairs={{0,4},{2,10},{8,0},{10,18},{16,8},{18,26},{24,16},{26,30},{28,24},... | collective-permute-start | bytes 393224 | tf_op jit(solution)/shard_map/ppermute | solution.py:579
  47.3 5.0 %collective-permute-start.28 = (bf16[4,128,128]{2,1,0:T(8,128)(2,1)S(1)}, bf16[4,128,128]{2,1,0:T(8,128)(2,1)S(1)}, u32[]{:S(2)}, u32[]{:S(2)}) collective-permute-start(bf16[4,128,128]{2,1,0:T(8,128)(2,1)S(1)} %get-tuple-element.65), channel_id=1, source_target_pairs={{0,8},{2,6},{8,16},{10,2},{16,24},{18,10},{24,28},{26,18},{28,20},... | collective-permute-start | bytes 393224 | tf_op jit(solution)/shard_map/ppermute | solution.py:577
  52.4 6.4 %collective-permute-start.31 = (bf16[4,128,128]{2,1,0:T(8,128)(2,1)S(1)}, bf16[4,128,128]{2,1,0:T(8,128)(2,1)S(1)}, u32[]{:S(2)}, u32[]{:S(2)}) collective-permute-start(bf16[4,128,128]{2,1,0:T(8,128)(2,1)S(1)} %get-tuple-element.68), channel_id=1, source_target_pairs={{0,4},{2,10},{8,0},{10,18},{16,8},{18,26},{24,16},{26,30},{28,24},... | collective-permute-start | bytes 393224 | tf_op jit(solution)/shard_map/ppermute | solution.py:579
  54.5 5.0 %collective-permute-start.30 = (bf16[4,128,128]{2,1,0:T(8,128)(2,1)S(1)}, bf16[4,128,128]{2,1,0:T(8,128)(2,1)S(1)}, u32[]{:S(2)}, u32[]{:S(2)}) collective-permute-start(bf16[4,128,128]{2,1,0:T(8,128)(2,1)S(1)} %get-tuple-element.67), channel_id=1, source_target_pairs={{0,8},{2,6},{8,16},{10,2},{16,24},{18,10},{24,28},{26,18},{28,20},... | collective-permute-start | bytes 393224 | tf_op jit(solution)/shard_map/ppermute | solution.py:577
  54.5 15.8 %collective-permute-start.25 = (bf16[20,128,128]{2,1,0:T(8,128)(2,1)}, bf16[20,128,128]{2,1,0:T(8,128)(2,1)S(1)}, u32[]{:S(2)}, u32[]{:S(2)}) collective-permute-start(bf16[20,128,128]{2,1,0:T(8,128)(2,1)} %get-tuple-element.61), channel_id=1, source_target_pairs={{0,1},{1,0},{2,3},{3,2},{4,5},{5,4},{6,7},{7,6},{8,9},{9,8},{10,11... | collective-permute-start | bytes 1966088 | tf_op jit(solution)/shard_map/ppermute | solution.py:621
  59.6 5.4 %collective-permute-start.32 = (bf16[4,128,128]{2,1,0:T(8,128)(2,1)S(1)}, bf16[4,128,128]{2,1,0:T(8,128)(2,1)S(1)}, u32[]{:S(2)}, u32[]{:S(2)}) collective-permute-start(bf16[4,128,128]{2,1,0:T(8,128)(2,1)S(1)} %get-tuple-element.69), channel_id=1, source_target_pairs={{0,8},{2,6},{8,16},{10,2},{16,24},{18,10},{24,28},{26,18},{28,20},... | collective-permute-start | bytes 393224 | tf_op jit(solution)/shard_map/ppermute | solution.py:577
  62.1 10.9 %collective-permute-start.34 = (bf16[4,128,128]{2,1,0:T(8,128)(2,1)S(1)}, bf16[4,128,128]{2,1,0:T(8,128)(2,1)S(1)}, u32[]{:S(2)}, u32[]{:S(2)}) collective-permute-start(bf16[4,128,128]{2,1,0:T(8,128)(2,1)S(1)} %get-tuple-element.82), channel_id=1, source_target_pairs={{0,4},{2,10},{8,0},{10,18},{16,8},{18,26},{24,16},{26,30},{28,24},... | collective-permute-start | bytes 393224 | tf_op jit(solution)/shard_map/ppermute | solution.py:579
  65.0 8.0 %collective-permute-start.33 = (bf16[4,128,128]{2,1,0:T(8,128)(2,1)S(1)}, bf16[4,128,128]{2,1,0:T(8,128)(2,1)S(1)}, u32[]{:S(2)}, u32[]{:S(2)}) collective-permute-start(bf16[4,128,128]{2,1,0:T(8,128)(2,1)S(1)} %add_convert_fusion.8), channel_id=1, source_target_pairs={{0,8},{2,6},{8,16},{10,2},{16,24},{18,10},{24,28},{26,18},{28,20},... | collective-permute-start | bytes 393224 | tf_op jit(solution)/shard_map/ppermute | solution.py:577

commit v3 on v2

--- a/solution.py
+++ b/solution.py
@@ -10,7 +10,7 @@
 FF = 14336
 BLK = 128
 GROUP = 4
-FIRST_SEND = 20
+FIRST_SEND = 16
 FIRST_GRADS = 4
 SMALL = 4 * 1024 * 1024
 PLACE, PART, STRIP, CIDX, CWAS, OIDX, OWAS = range(7)
@@ -56,13 +56,14 @@
 
 def permutations(sz):
     seq = list(range(0, sz.ring, 2)) + list(range(sz.ring - 1, 0, -2))
-    ahead, behind, swap = [], [], []
+    ahead, behind, far, swap = [], [], [], []
     for i, q in enumerate(seq):
         up, down = seq[(i + 1) % sz.ring], seq[i - 1]
+        far += [(q * 2, seq[(i + 2) % sz.ring] * 2), (q * 2 + 1, seq[i - 2] * 2 + 1)]
         ahead += [(q * 2, up * 2), (q * 2 + 1, down * 2 + 1)]
         behind += [(q * 2, down * 2), (q * 2 + 1, up * 2 + 1)]
         swap += [(q * 2, q * 2 + 1), (q * 2 + 1, q * 2)]
-    return ahead, behind, swap
+    return ahead, behind, far, swap
 
 
 def ratio(x, d):
@@ -233,7 +234,7 @@
 
 
 def recv_kernel(sz, *refs):
-    own, raws, recv = refs[0], refs[1:-1], refs[-1]
+    own, plan, raws, recv, flag = refs[0], refs[1], refs[2:-2], refs[-2], refs[-1]
     f32 = jnp.float32
     head = []
     over = jnp.zeros((1, 1), f32)
@@ -247,7 +248,8 @@
         for d in range(sz.n_tensor):
             n = total(m.lead_c * (m.shift_c == d).astype(f32))
             over = jnp.maximum(over, (n > sz.first).astype(f32))
-    head.append((HEAD_OVER, over))
+    known = plan[HEAD_ROW:HEAD_ROW + 1, HEAD_OVER:HEAD_OVER + 1]
+    flag[...] = jnp.maximum(known, over.astype(jnp.int32))
     recv[0:1, :] = head_row(sz, head).astype(jnp.int32)
 
 
@@ -453,16 +455,32 @@
     )(own)
 
 
-def call_recv(sz, own, raws):
+def call_recv(sz, own, plan, raws):
     return pl.pallas_call(
         functools.partial(recv_kernel, sz),
-        out_shape=jax.ShapeDtypeStruct((sz.recv_rows, sz.lanes), jnp.int32),
-        in_specs=[spec(VMEM)] * (1 + len(raws)),
-        out_specs=spec(VMEM),
+        out_shape=[
+            jax.ShapeDtypeStruct((sz.recv_rows, sz.lanes), jnp.int32),
+            jax.ShapeDtypeStruct((1, 1), jnp.int32),
+        ],
+        in_specs=[spec(VMEM)] * (2 + len(raws)),
+        out_specs=[spec(VMEM)] * 2,
         compiler_params=pltpu.CompilerParams(vmem_limit_bytes=SMALL),
         cost_estimate=cost(1_000_000, 4_000_000),
         name="recv",
-    )(own, *raws)
+    )(own, plan, *raws)
+
+
+def call_turn(handed, arrived):
+    return pl.pallas_call(
+        lambda *_: None,
+        out_shape=[jax.ShapeDtypeStruct(x.shape, x.dtype) for x in handed],
+        in_specs=[spec(ANY)] * (len(handed) + len(arrived)),
+        out_specs=[spec(ANY)] * len(handed),
+        input_output_aliases={i: i for i in range(len(handed))},
+        compiler_params=pltpu.CompilerParams(vmem_limit_bytes=SMALL),
+        cost_estimate=cost(1000, 1000),
+        name="turn",
+    )(*handed, *arrived)
 
 
 def call_compute(sz, plan, tokens, cot, chunks):
@@ -537,26 +555,24 @@
     )(plan, here, ahead, behind, late)
 
 
-def gather_chunks(sz, chunk, plan_of, recv_of):
-    ahead, behind, swap = permutations(sz)
-    same = {0: chunk}
+def gather_chunks(sz, chunk):
+    ahead, behind, far, swap = permutations(sz)
+    same, other = {0: chunk}, {}
     a = b = chunk
-    for s in range(1, sz.top + 1):
-        if s == 2:
-            (a, b), plan = lax.optimization_barrier(((a, b), plan_of()))
-        if s == 3 or s == sz.top < 3:
-            (a, b), recv = lax.optimization_barrier(((a, b), recv_of()))
-        a = lax.ppermute(a, "fsdp", ahead)
-        same[sz.ring - s] = a
-        if s < sz.top:
-            b = lax.ppermute(b, "fsdp", behind)
-            same[s] = b
-    other = {d: lax.ppermute(same[d], "fsdp", swap) for d in same}
-    return [side[d] for side in (same, other) for d in sz.order], plan, recv
-
-
-def reduce_parts(sz, per, same, pair, beside=lambda a: a):
-    ahead, behind, _ = permutations(sz)
+    for s in range(1, sz.top):
+        if s == sz.top - 1:
+            same[sz.top] = lax.ppermute(a, "fsdp", far)
+            other[sz.top] = lax.ppermute(a, "fsdp", [(i, j ^ 1) for i, j in far])
+        a, b = lax.ppermute(a, "fsdp", ahead), lax.ppermute(b, "fsdp", behind)
+        same[sz.ring - s], same[s] = a, b
+    for d in same:
+        if d != sz.top:
+            other[d] = lax.ppermute(same[d], "fsdp", swap)
+    return [side[d] for side in (same, other) for d in sz.order]
+
+
+def reduce_parts(sz, per, same, pair, beside=lambda s, a, b: (a, b)):
+    ahead, behind, far, _ = permutations(sz)
 
     def wide(d, *more):
         j = sz.order.index(d)
@@ -568,18 +584,14 @@
     def term(d, *more):
         return wide(d, *more).astype(jnp.bfloat16)
 
-    a, b = term(sz.top), term(sz.top + 1)
-    for s in range(1, sz.top + 1):
-        if s < sz.top:
-            a, b = lax.optimization_barrier((a, b))
-        else:
-            a = beside(a)
-        a = lax.ppermute(a, "fsdp", ahead)
-        if s < sz.top:
-            b = lax.ppermute(b, "fsdp", behind)
-            a = term(sz.top - s, a)
-            if s + 1 < sz.top:
-                b = term(sz.top + 1 + s, b)
+    c, a, b = lax.optimization_barrier((term(sz.top), term(sz.top - 1), term(sz.top + 1)))
+    c = lax.ppermute(c, "fsdp", far)
+    for s in range(1, sz.top):
+        if s > 1:
+            a = term(sz.top - s, a, c) if s == 2 else term(sz.top - s, a)
+            b = term(sz.top + s, b)
+            a, b = beside(s, *lax.optimization_barrier((a, b)))
+        a, b = lax.ppermute(a, "fsdp", ahead), lax.ppermute(b, "fsdp", behind)
     return wide(0), a, b
 
 
@@ -597,7 +609,7 @@
     n_fsdp, T = lax.axis_size("fsdp"), lax.axis_size("tensor")
     sz = Sizes(tokens, gate_blocks, gate_where.shape[1], n_fsdp, T)
     f, rank = lax.axis_index("fsdp"), lax.axis_index("tensor")
-    _, _, swap = permutations(sz)
+    swap = permutations(sz)[-1]
 
     chunk = jnp.concatenate([gate_blocks[0], up_blocks[0], down_blocks[0]])
     own = jnp.concatenate([
@@ -605,12 +617,10 @@
         f.astype(jnp.int32)[None], rank.astype(jnp.int32)[None]])
     own = jnp.pad(own, (0, sz.lanes - own.shape[0]))[None]
 
-    def recv_of():
-        raws = [
-            lax.ppermute(own, "tensor", [(i, (i + s) % T) for i in range(T)]) for s in range(1, T)]
-        return call_recv(sz, own, raws)
-
-    chunks, plan, recv = gather_chunks(sz, chunk, lambda: call_plan(sz, own), recv_of)
+    plan = call_plan(sz, own)
+    raws = [lax.ppermute(own, "tensor", [(i, (i + s) % T) for i in range(T)]) for s in range(1, T)]
+    recv, flag = call_recv(sz, own, plan, raws)
+    chunks = gather_chunks(sz, chunk)
 
     outs = call_compute(sz, plan, tokens, cotangent, chunks)
     same, far, near, extra, idle = outs[:5]
@@ -629,10 +639,13 @@
 
     late = idle
 
-    def beside(a):
+    def beside(s, a, b):
         nonlocal rests, late
+        if s != sz.top - 1:
+            return a, b
+        a, more = call_turn([a, extra], firsts[1:])
         if sz.rest + sz.more == 0:
-            return a
+            return a, b
 
         def spill(rests, extra, idle):
             moved = exchange(rests)
@@ -643,10 +656,8 @@
             terms = reduce_parts(sz, sz.more, extra[:n], lambda j: other[j * sz.more:(j + 1) * sz.more])
             return moved, sum(t.astype(jnp.float32) for t in terms).astype(jnp.bfloat16)
 
-        over = plan[HEAD_ROW, HEAD_OVER] + recv[0, HEAD_OVER]
-        a, over, rests, more = lax.optimization_barrier((a, over, rests, extra))
-        rests, late = lax.cond(over > 0, spill, lambda r, e, i: (r, i), rests, more, idle)
-        return a
+        rests, late = lax.cond(flag[0, 0] > 0, spill, lambda r, e, i: (r, i), rests, more, idle)
+        return a, b
 
     here, ahead, behind = reduce_parts(sz, sz.keep, same, pair, beside)
     outputs, input_grads = call_join(sz, plan, recv, firsts, rests)

time: 74.1 us -> 87.8 us (1.18); the launches traced: 74.6 us -> 87.4 us
  local copies, waits for them, and re-layouts: 1.95 us -> 18.4 us
  waiting for transfers between devices: 30.9 us -> 28.3 us
    unnamed x0 -> x44, local copies, waits for them, and re-layouts: none -> 17.6 us
    ppermute x1, waiting for transfers between devices: 5.21 us -> 0.01 us  [exchange(): lax.ppermute(arrays[s], 'tensor', [(i, (i + s) % T) for i in range(T)])]
    ppermute x23, waiting for transfers between devices: 24.3 us -> 26.9 us  [the longest x6 9.39 us: gather_chunks(): a, b = (lax.ppermute(a, 'fsdp', ahead), lax.ppermute(b, 'fsdp', behind))]
    slice x2 -> x0, local copies, waits for them, and re-layouts: 1.16 us -> none  [beside(): over = plan[HEAD_ROW, HEAD_OVER] + recv[0, HEAD_OVER]]
    pallas_call x1, Pallas kernels: 11.6 us -> 10.6 us  [call_compute(): pl.pallas_call(functools.partial(compute_kernel, sz), out_shape=out_shape...]
  transfers between devices with their start and end apart: 26 -> 26, of which waited for: 15 -> 11; matrix products, arithmetic and copies ran while one was open for 3% -> 1% of each run, Pallas kernels for 4% -> 4%
where the time goes in v3:
time: 87.8 us; the launch traced here: 87.4 us
  waiting for transfers between devices  28.3 us (32%)
  starting transfers between devices  21.5 us (24%)
  local copies, waits for them, and re-layouts  18.4 us (21%)
  Pallas kernels  16.4 us (19%)
  between operations  1.42 us (2%)
  other arithmetic  1.3 us (1%)
    unnamed x44, local copies, waits for them, and re-layouts  17.6 us
    pallas_call x1, Pallas kernels, call_compute(): pl.pallas_call(functools.partial(compute_kernel, sz), out_shape=out_shape...  10.6 us
    ppermute x6, waiting for transfers between devices, gather_chunks(): a, b = (lax.ppermute(a, 'fsdp', ahead), lax.ppermute(b, 'fsdp', behind))  9.39 us
    ppermute x6, starting transfers between devices, gather_chunks(): a, b = (lax.ppermute(a, 'fsdp', ahead), lax.ppermute(b, 'fsdp', behind))  6.6 us
    ppermute x1, waiting for transfers between devices, shards(): lax.ppermute(own, 'tensor', [(i, (i + s) % T) for i in range(T)])  5.42 us
    ppermute x6, starting transfers between devices, reduce_parts(): a, b = (lax.ppermute(a, 'fsdp', ahead), lax.ppermute(b, 'fsdp', behind))  5.41 us
    ppermute x1, waiting for transfers between devices, gather_chunks(): same[sz.top] = lax.ppermute(a, 'fsdp', far)  4.72 us
    ppermute x1, waiting for transfers between devices, reduce_parts(): c = lax.ppermute(c, 'fsdp', far)  4.04 us
  transfers between devices with their start and end apart: 26, of which 11 were waited for; matrix products, arithmetic and copies ran while one was open for 1% of the time, Pallas kernels for 4%

profile of v3, /device:TPU:0, one launch (start us, length us, event | category | flops | bytes accessed | tf_op | source)
XLA Modules:
  0.0 87.4 jit_solution(8052405016336855643)
XLA Ops:
  0.6 0.9 %pad_maximum_fusion.refs_10_ = bf16[6,128,128]{2,1,0:T(8,128)(2,1)S(1)} fusion(bf16[2,128,128]{2,1,0:T(8,128)(2,1)} %bitcast.12, bf16[2,128,128]{2,1,0:T(8,128)(2,1)} %bitcast.13, bf16[2,128,128]{2,1,0:T(8,128)(2,1)} %bitcast.14), kind=kLoop, calls=%fused_computation.16 | loop fusion | flops 196608 | bytes 393216 | tf_op jit(solution)/shard_map/concatenate | solution.py:614
  1.6 3.1 %collective-permute-start.10 = (bf16[6,128,128]{2,1,0:T(8,128)(2,1)S(1)}, bf16[6,128,128]{2,1,0:T(8,128)(2,1)S(1)}, u32[]{:S(2)}, u32[]{:S(2)}) collective-permute-start(bf16[6,128,128]{2,1,0:T(8,128)(2,1)S(1)} %pad_maximum_fusion.refs_10_), channel_id=1, source_target_pairs={{0,8},{2,6},{8,16},{10,2},{16,24},{18,10},{24,28},{26,18},{28,20},... | collective-permute-start | bytes 589832 | tf_op jit(solution)/shard_map/ppermute | solution.py:566
  4.6 0.0 collective-permute-start.14
  4.6 5.1 %collective-permute-done.10.refs_8_ = bf16[6,128,128]{2,1,0:T(8,128)(2,1)S(1)} collective-permute-done((bf16[6,128,128]{2,1,0:T(8,128)(2,1)S(1)}, bf16[6,128,128]{2,1,0:T(8,128)(2,1)S(1)}, u32[]{:S(2)}, u32[]{:S(2)}) %collective-permute-start.10) | collective-permute-done | bytes 196640 | tf_op jit(solution)/shard_map/ppermute | solution.py:566
  9.8 1.6 %collective-permute-start.11 = (bf16[6,128,128]{2,1,0:T(8,128)(2,1)S(1)}, bf16[6,128,128]{2,1,0:T(8,128)(2,1)S(1)}, u32[]{:S(2)}, u32[]{:S(2)}) collective-permute-start(bf16[6,128,128]{2,1,0:T(8,128)(2,1)S(1)} %collective-permute-done.10.refs_8_), channel_id=1, source_target_pairs={{0,8},{2,6},{8,16},{10,2},{16,24},{18,10},{24,28},{26,18},{28,20},... | collective-permute-start | bytes 589832 | tf_op jit(solution)/shard_map/ppermute | solution.py:566
  11.4 0.9 %collective-permute-start.15 = (bf16[6,128,128]{2,1,0:T(8,128)(2,1)S(1)}, bf16[6,128,128]{2,1,0:T(8,128)(2,1)S(1)}, u32[]{:S(2)}, u32[]{:S(2)}) collective-permute-start(bf16[6,128,128]{2,1,0:T(8,128)(2,1)S(1)} %collective-permute-done.14.refs_9_), channel_id=1, source_target_pairs={{0,4},{2,10},{8,0},{10,18},{16,8},{18,26},{24,16},{26,30},{28,24},... | collective-permute-start | bytes 589832 | tf_op jit(solution)/shard_map/ppermute | solution.py:566
  12.3 1.0 %collective-permute-start.22 = (bf16[6,128,128]{2,1,0:T(8,128)(2,1)S(1)}, bf16[6,128,128]{2,1,0:T(8,128)(2,1)S(1)}, u32[]{:S(2)}, u32[]{:S(2)}) collective-permute-start(bf16[6,128,128]{2,1,0:T(8,128)(2,1)S(1)} %collective-permute-done.10.refs_8_), channel_id=1, source_target_pairs={{0,2},{2,0},{8,10},{10,8},{16,18},{18,16},{24,26},{26,24},{28,30},... | collective-permute-start | bytes 589832 | tf_op jit(solution)/shard_map/ppermute | solution.py:570
  13.3 0.0 collective-permute-start.23
  13.3 4.0 %collective-permute-done.11.refs_6_ = bf16[6,128,128]{2,1,0:T(8,128)(2,1)S(1)} collective-permute-done((bf16[6,128,128]{2,1,0:T(8,128)(2,1)S(1)}, bf16[6,128,128]{2,1,0:T(8,128)(2,1)S(1)}, u32[]{:S(2)}, u32[]{:S(2)}) %collective-permute-start.11) | collective-permute-done | bytes 196640 | tf_op jit(solution)/shard_map/ppermute | solution.py:566
  17.3 0.6 collective-permute-start.13
  17.9 0.0 collective-permute-done.24.refs_18_
  17.9 2.8 %collective-permute-start.12 = (bf16[6,128,128]{2,1,0:T(8,128)(2,1)S(1)}, bf16[6,128,128]{2,1,0:T(8,128)(2,1)S(1)}, u32[]{:S(2)}, u32[]{:S(2)}) collective-permute-start(bf16[6,128,128]{2,1,0:T(8,128)(2,1)S(1)} %collective-permute-done.11.refs_6_), channel_id=1, source_target_pairs={{0,16},{2,14},{8,24},{10,6},{16,28},{18,2},{24,20},{26,10},{28,12}... | collective-permute-start | bytes 589832 | tf_op jit(solution)/shard_map/ppermute | solution.py:564
  20.7 0.5 collective-permute-start.16
  21.1 0.7 copy-done.2
  21.8 0.1 collective-permute-start.17
  21.9 0.7 copy-done.4
  22.6 1.9 %collective-permute-start.20 = (bf16[6,128,128]{2,1,0:T(8,128)(2,1)S(1)}, bf16[6,128,128]{2,1,0:T(8,128)(2,1)S(1)}, u32[]{:S(2)}, u32[]{:S(2)}) collective-permute-start(bf16[6,128,128]{2,1,0:T(8,128)(2,1)S(1)} %collective-permute-done.11.refs_6_), channel_id=1, source_target_pairs={{0,2},{2,0},{8,10},{10,8},{16,18},{18,16},{24,26},{26,24},{28,30},... | collective-permute-start | bytes 589832 | tf_op jit(solution)/shard_map/ppermute | solution.py:570
  24.6 0.2 collective-permute-done.13.refs_4_
  24.8 0.7 copy-done
  25.5 4.7 %collective-permute-done.12.refs_3_ = bf16[6,128,128]{2,1,0:T(8,128)(2,1)S(1)} collective-permute-done((bf16[6,128,128]{2,1,0:T(8,128)(2,1)S(1)}, bf16[6,128,128]{2,1,0:T(8,128)(2,1)S(1)}, u32[]{:S(2)}, u32[]{:S(2)}) %collective-permute-start.12) | collective-permute-done | bytes 196640 | tf_op jit(solution)/shard_map/ppermute | solution.py:564
  30.2 0.7 copy-done.8
  30.9 0.7 copy-done.6
  31.6 0.5 collective-permute-start.19
  32.1 0.7 copy-done.10
  32.8 0.8 concatenate.6
  33.5 0.5 plan.1.refs_1_.refs_0_
  34.0 0.7 copy-done.12
  34.7 0.7 copy-done.14
  35.4 0.7 copy-done.16
  36.1 0.7 copy-done.18
  36.7 0.7 copy-done.20
  37.4 0.9 %copy-done.1 = bf16[6,128,128]{2,1,0:T(8,128)(2,1)S(1)} copy-done((bf16[6,128,128]{2,1,0:T(8,128)(2,1)S(1)}, bf16[6,128,128]{2,1,0:T(8,128)(2,1)}, u32[]{:S(2)}) %copy-start.1) | copy-done | bytes 196632
  38.3 0.9 %copy-done.3 = bf16[6,128,128]{2,1,0:T(8,128)(2,1)S(1)} copy-done((bf16[6,128,128]{2,1,0:T(8,128)(2,1)S(1)}, bf16[6,128,128]{2,1,0:T(8,128)(2,1)}, u32[]{:S(2)}) %copy-start.3) | copy-done | bytes 196632
  39.3 0.9 %copy-done.5 = bf16[6,128,128]{2,1,0:T(8,128)(2,1)S(1)} copy-done((bf16[6,128,128]{2,1,0:T(8,128)(2,1)S(1)}, bf16[6,128,128]{2,1,0:T(8,128)(2,1)}, u32[]{:S(2)}) %copy-start.5) | copy-done | bytes 196632
  40.2 0.9 %copy-done.7 = bf16[6,128,128]{2,1,0:T(8,128)(2,1)S(1)} copy-done((bf16[6,128,128]{2,1,0:T(8,128)(2,1)S(1)}, bf16[6,128,128]{2,1,0:T(8,128)(2,1)}, u32[]{:S(2)}) %copy-start.7) | copy-done | bytes 196632
  41.1 0.9 %copy-done.9 = bf16[6,128,128]{2,1,0:T(8,128)(2,1)S(1)} copy-done((bf16[6,128,128]{2,1,0:T(8,128)(2,1)S(1)}, bf16[6,128,128]{2,1,0:T(8,128)(2,1)}, u32[]{:S(2)}) %copy-start.9) | copy-done | bytes 196632
  42.0 0.9 %copy-done.11 = bf16[6,128,128]{2,1,0:T(8,128)(2,1)S(1)} copy-done((bf16[6,128,128]{2,1,0:T(8,128)(2,1)S(1)}, bf16[6,128,128]{2,1,0:T(8,128)(2,1)}, u32[]{:S(2)}) %copy-start.11) | copy-done | bytes 196632
  43.0 0.9 %copy-done.13 = bf16[6,128,128]{2,1,0:T(8,128)(2,1)S(1)} copy-done((bf16[6,128,128]{2,1,0:T(8,128)(2,1)S(1)}, bf16[6,128,128]{2,1,0:T(8,128)(2,1)}, u32[]{:S(2)}) %copy-start.13) | copy-done | bytes 196632
  43.9 0.9 %copy-done.15 = bf16[6,128,128]{2,1,0:T(8,128)(2,1)S(1)} copy-done((bf16[6,128,128]{2,1,0:T(8,128)(2,1)S(1)}, bf16[6,128,128]{2,1,0:T(8,128)(2,1)}, u32[]{:S(2)}) %copy-start.15) | copy-done | bytes 196632
  44.8 0.9 %copy-done.17 = bf16[6,128,128]{2,1,0:T(8,128)(2,1)S(1)} copy-done((bf16[6,128,128]{2,1,0:T(8,128)(2,1)S(1)}, bf16[6,128,128]{2,1,0:T(8,128)(2,1)}, u32[]{:S(2)}) %copy-start.17) | copy-done | bytes 196632
  45.8 0.9 %copy-done.19 = bf16[6,128,128]{2,1,0:T(8,128)(2,1)S(1)} copy-done((bf16[6,128,128]{2,1,0:T(8,128)(2,1)S(1)}, bf16[6,128,128]{2,1,0:T(8,128)(2,1)}, u32[]{:S(2)}) %copy-start.19) | copy-done | bytes 196632
  46.7 0.9 %copy-done.21 = bf16[6,128,128]{2,1,0:T(8,128)(2,1)S(1)} copy-done((bf16[6,128,128]{2,1,0:T(8,128)(2,1)S(1)}, bf16[6,128,128]{2,1,0:T(8,128)(2,1)}, u32[]{:S(2)}) %copy-start.21) | copy-done | bytes 196632
  47.6 10.6 %compute.1 = (bf16[32,128,128]{2,1,0:T(8,128)(2,1)S(1)}, bf16[16,128,128]{2,1,0:T(8,128)(2,1)S(1)}, bf16[16,128,128]{2,1,0:T(8,128)(2,1)S(1)}, bf16[32,128,128]{...) custom-call(s32[32,128]{1,0:T(8,128)S(1)} %plan.1.refs_1_.refs_0_, ...), custom_call_target="tpu_custom_call" | custom-call | flops 1000000000 | bytes 20000000 | tf_op jit(solution)/shard_map/compute/pallas_call | solution.py:515
  58.2 0.1 collective-permute-start.27
  58.3 0.5 collective-permute-start.26
  58.8 1.4 %collective-permute-done.27 = bf16[16,128,128]{2,1,0:T(8,128)(2,1)S(1)} collective-permute-done((bf16[16,128,128]{2,1,0:T(8,128)(2,1)S(1)}, bf16[16,128,128]{2,1,0:T(8,128)(2,1)S(1)}, u32[]{:S(2)}, u32[]{:S(2)}) %collective-permute-start.27) | collective-permute-done | bytes 524320 | tf_op jit(solution)/shard_map/ppermute | solution.py:633
  60.2 0.1 add_convert_fusion.12
  60.3 0.7 collective-permute-start.28
  61.0 2.5 %collective-permute-start.29 = (bf16[4,128,128]{2,1,0:T(8,128)(2,1)S(1)}, bf16[4,128,128]{2,1,0:T(8,128)(2,1)S(1)}, u32[]{:S(2)}, u32[]{:S(2)}) collective-permute-start(bf16[4,128,128]{2,1,0:T(8,128)(2,1)S(1)} %get-tuple-element.60), channel_id=1, source_target_pairs={{0,16},{2,14},{8,24},{10,6},{16,28},{18,2},{24,20},{26,10},{28,12}... | collective-permute-start | bytes 393224 | tf_op jit(solution)/shard_map/ppermute | solution.py:588
  63.5 1.8 %collective-permute-done.28 = bf16[4,128,128]{2,1,0:T(8,128)(2,1)S(1)} collective-permute-done((bf16[4,128,128]{2,1,0:T(8,128)(2,1)S(1)}, bf16[4,128,128]{2,1,0:T(8,128)(2,1)S(1)}, u32[]{:S(2)}, u32[]{:S(2)}) %collective-permute-start.28) | collective-permute-done | bytes 131104 | tf_op jit(solution)/shard_map/ppermute | solution.py:594
  65.3 4.0 %collective-permute-done.29 = bf16[4,128,128]{2,1,0:T(8,128)(2,1)S(1)} collective-permute-done((bf16[4,128,128]{2,1,0:T(8,128)(2,1)S(1)}, bf16[4,128,128]{2,1,0:T(8,128)(2,1)S(1)}, u32[]{:S(2)}, u32[]{:S(2)}) %collective-permute-start.29) | collective-permute-done | bytes 131104 | tf_op jit(solution)/shard_map/ppermute | solution.py:588
  69.4 0.7 collective-permute-done.30
  70.0 0.1 add_convert_fusion.10
  70.1 0.2 collective-permute-start.31
  70.3 2.5 %collective-permute-start.32 = (bf16[4,128,128]{2,1,0:T(8,128)(2,1)S(1)}, bf16[4,128,128]{2,1,0:T(8,128)(2,1)S(1)}, u32[]{:S(2)}, u32[]{:S(2)}) collective-permute-start(bf16[4,128,128]{2,1,0:T(8,128)(2,1)S(1)} %get-tuple-element.63), channel_id=1, source_target_pairs={{0,4},{2,10},{8,0},{10,18},{16,8},{18,26},{24,16},{26,30},{28,24},... | collective-permute-start | bytes 393224 | tf_op jit(solution)/shard_map/ppermute | solution.py:594
  72.8 5.4 %collective-permute-done.9.refs_2_ = s32[1,128]{1,0:T(1,128)S(1)} collective-permute-done((s32[1,128]{1,0:T(1,128)S(1)}, s32[1,128]{1,0:T(1,128)S(1)}, u32[]{:S(2)}, u32[]{:S(2)}) %collective-permute-start.9) | collective-permute-done | bytes 544 | tf_op jit(solution)/shard_map/ppermute | solution.py:621
  78.2 0.9 %recv.1 = (s32[8,128]{1,0:T(8,128)S(1)}, s32[1,1]{1,0:T(1,128)}) custom-call(s32[1,128]{1,0:T(1,128)S(1)} %pad_bitcast_fusion.own.refs_0_, s32[32,128]{1,0:T(8,128)S(1)} %plan.1.refs_1_.refs_0_, s32[1,128]{1,0:T(1,128)S(1)} %collective-permute-done.9.refs_2_), custom_call_target="tpu_custom_call" | custom-call | flops 1000000 | bytes 4000000 | tf_op jit(solution)/shard_map/recv/pallas_call | solution.py:459
  79.8 0.1 convert_add_fusion
  80.0 0.9 %collective-permute-start.33 = (bf16[4,128,128]{2,1,0:T(8,128)(2,1)S(1)}, bf16[4,128,128]{2,1,0:T(8,128)(2,1)S(1)}, u32[]{:S(2)}, u32[]{:S(2)}) collective-permute-start(bf16[4,128,128]{2,1,0:T(8,128)(2,1)S(1)} %get-tuple-element.70), channel_id=1, source_target_pairs={{0,8},{2,6},{8,16},{10,2},{16,24},{18,10},{24,28},{26,18},{28,20},... | collective-permute-start | bytes 393224 | tf_op jit(solution)/shard_map/ppermute | solution.py:594
  80.9 1.2 %collective-permute-start.34 = (bf16[4,128,128]{2,1,0:T(8,128)(2,1)S(1)}, bf16[4,128,128]{2,1,0:T(8,128)(2,1)S(1)}, u32[]{:S(2)}, u32[]{:S(2)}) collective-permute-start(bf16[4,128,128]{2,1,0:T(8,128)(2,1)S(1)} %get-tuple-element.71), channel_id=1, source_target_pairs={{0,4},{2,10},{8,0},{10,18},{16,8},{18,26},{24,16},{26,30},{28,24},... | collective-permute-start | bytes 393224 | tf_op jit(solution)/shard_map/ppermute | solution.py:594
  82.0 2.9 %join.1 = (bf16[128,4096]{1,0:T(8,128)(2,1)}, bf16[128,4096]{1,0:T(8,128)(2,1)}) custom-call(s32[32,128]{1,0:T(8,128)S(1)} %plan.1.refs_1_.refs_0_, s32[8,128]{1,0:T(8,128)S(1)} %get-tuple-element.49.refs_1_, bf16[16,128,128]{2,1,0:T(8,128)(2,1)S(1)} %get-tuple-element.50.refs_2_, bf16[16,128,128]{2,1,0:T(8,128)(2,1)S(1)} %collective-permute-done.25.__2_.refs_3_, ...), custom_call_target="tpu_custom_call" | custom-call | flops 1000000 | bytes 6000000 | tf_op jit(solution)/shard_map/join/pallas_call | solution.py:533
  85.0 0.6 collective-permute-done.33.ahead
  85.5 0.3 collective-permute-done.34.behind
  85.8 1.5 %finish.1 = (bf16[1,2,128,128]{3,2,1,0:T(8,128)(2,1)}, bf16[1,2,128,128]{3,2,1,0:T(8,128)(2,1)}, bf16[1,2,128,128]{3,2,1,0:T(8,128)(2,1)}) custom-call(s32[32,128]{1,0:T(8,128)S(1)} %plan.1.refs_1_.refs_0_, f32[4,128,128]{2,1,0:T(8,128)S(1)} %get-tuple-element.83.here, bf16[4,128,128]{2,1,0:T(8,128)(2,1)S(1)} %collective-permute-done.33.ahead, ...), custom_call_target="tpu_custom_call" | custom-call | flops 1000000 | bytes 1000000 | tf_op jit(solution)/shard_map/finish/pallas_call | solution.py:547
  (45 shorter events, 0.1 us)
Async XLA Ops:
  1.6 8.2 %collective-permute-start.10 = (bf16[6,128,128]{2,1,0:T(8,128)(2,1)S(1)}, bf16[6,128,128]{2,1,0:T(8,128)(2,1)S(1)}, u32[]{:S(2)}, u32[]{:S(2)}) collective-permute-start(bf16[6,128,128]{2,1,0:T(8,128)(2,1)S(1)} %pad_maximum_fusion.refs_10_), channel_id=1, source_target_pairs={{0,8},{2,6},{8,16},{10,2},{16,24},{18,10},{24,28},{26,18},{28,20},... | collective-permute-start | bytes 589832 | tf_op jit(solution)/shard_map/ppermute | solution.py:566
  4.6 6.7 %collective-permute-start.14 = (bf16[6,128,128]{2,1,0:T(8,128)(2,1)S(1)}, bf16[6,128,128]{2,1,0:T(8,128)(2,1)S(1)}, u32[]{:S(2)}, u32[]{:S(2)}) collective-permute-start(bf16[6,128,128]{2,1,0:T(8,128)(2,1)S(1)} %pad_maximum_fusion.refs_10_), channel_id=1, source_target_pairs={{0,4},{2,10},{8,0},{10,18},{16,8},{18,26},{24,16},{26,30},{28,24},... | collective-permute-start | bytes 589832 | tf_op jit(solution)/shard_map/ppermute | solution.py:566
  9.8 7.5 %collective-permute-start.11 = (bf16[6,128,128]{2,1,0:T(8,128)(2,1)S(1)}, bf16[6,128,128]{2,1,0:T(8,128)(2,1)S(1)}, u32[]{:S(2)}, u32[]{:S(2)}) collective-permute-start(bf16[6,128,128]{2,1,0:T(8,128)(2,1)S(1)} %collective-permute-done.10.refs_8_), channel_id=1, source_target_pairs={{0,8},{2,6},{8,16},{10,2},{16,24},{18,10},{24,28},{26,18},{28,20},... | collective-permute-start | bytes 589832 | tf_op jit(solution)/shard_map/ppermute | solution.py:566
  11.3 6.5 %collective-permute-start.24 = (bf16[6,128,128]{2,1,0:T(8,128)(2,1)S(1)}, bf16[6,128,128]{2,1,0:T(8,128)(2,1)S(1)}, u32[]{:S(2)}, u32[]{:S(2)}) collective-permute-start(bf16[6,128,128]{2,1,0:T(8,128)(2,1)S(1)} %pad_maximum_fusion.refs_10_), channel_id=1, source_target_pairs={{0,2},{2,0},{8,10},{10,8},{16,18},{18,16},{24,26},{26,24},{28,30},... | collective-permute-start | bytes 589832 | tf_op jit(solution)/shard_map/ppermute | solution.py:570
  11.4 9.3 %collective-permute-start.15 = (bf16[6,128,128]{2,1,0:T(8,128)(2,1)S(1)}, bf16[6,128,128]{2,1,0:T(8,128)(2,1)S(1)}, u32[]{:S(2)}, u32[]{:S(2)}) collective-permute-start(bf16[6,128,128]{2,1,0:T(8,128)(2,1)S(1)} %collective-permute-done.14.refs_9_), channel_id=1, source_target_pairs={{0,4},{2,10},{8,0},{10,18},{16,8},{18,26},{24,16},{26,30},{28,24},... | collective-permute-start | bytes 589832 | tf_op jit(solution)/shard_map/ppermute | solution.py:566
  12.3 8.9 %collective-permute-start.22 = (bf16[6,128,128]{2,1,0:T(8,128)(2,1)S(1)}, bf16[6,128,128]{2,1,0:T(8,128)(2,1)S(1)}, u32[]{:S(2)}, u32[]{:S(2)}) collective-permute-start(bf16[6,128,128]{2,1,0:T(8,128)(2,1)S(1)} %collective-permute-done.10.refs_8_), channel_id=1, source_target_pairs={{0,2},{2,0},{8,10},{10,8},{16,18},{18,16},{24,26},{26,24},{28,30},... | collective-permute-start | bytes 589832 | tf_op jit(solution)/shard_map/ppermute | solution.py:570
  13.3 8.7 %collective-permute-start.23 = (bf16[6,128,128]{2,1,0:T(8,128)(2,1)S(1)}, bf16[6,128,128]{2,1,0:T(8,128)(2,1)S(1)}, u32[]{:S(2)}, u32[]{:S(2)}) collective-permute-start(bf16[6,128,128]{2,1,0:T(8,128)(2,1)S(1)} %collective-permute-done.14.refs_9_), channel_id=1, source_target_pairs={{0,2},{2,0},{8,10},{10,8},{16,18},{18,16},{24,26},{26,24},{28,30},... | collective-permute-start | bytes 589832 | tf_op jit(solution)/shard_map/ppermute | solution.py:570
  17.3 7.5 %collective-permute-start.13 = (bf16[6,128,128]{2,1,0:T(8,128)(2,1)S(1)}, bf16[6,128,128]{2,1,0:T(8,128)(2,1)S(1)}, u32[]{:S(2)}, u32[]{:S(2)}) collective-permute-start(bf16[6,128,128]{2,1,0:T(8,128)(2,1)S(1)} %collective-permute-done.11.refs_6_), channel_id=1, source_target_pairs={{0,8},{2,6},{8,16},{10,2},{16,24},{18,10},{24,28},{26,18},{28,20},... | collective-permute-start | bytes 589832 | tf_op jit(solution)/shard_map/ppermute | solution.py:566
  17.9 12.3 %collective-permute-start.12 = (bf16[6,128,128]{2,1,0:T(8,128)(2,1)S(1)}, bf16[6,128,128]{2,1,0:T(8,128)(2,1)S(1)}, u32[]{:S(2)}, u32[]{:S(2)}) collective-permute-start(bf16[6,128,128]{2,1,0:T(8,128)(2,1)S(1)} %collective-permute-done.11.refs_6_), channel_id=1, source_target_pairs={{0,16},{2,14},{8,24},{10,6},{16,28},{18,2},{24,20},{26,10},{28,12}... | collective-permute-start | bytes 589832 | tf_op jit(solution)/shard_map/ppermute | solution.py:564
  20.7 10.9 %collective-permute-start.16 = (bf16[6,128,128]{2,1,0:T(8,128)(2,1)S(1)}, bf16[6,128,128]{2,1,0:T(8,128)(2,1)S(1)}, u32[]{:S(2)}, u32[]{:S(2)}) collective-permute-start(bf16[6,128,128]{2,1,0:T(8,128)(2,1)S(1)} %collective-permute-done.15.refs_7_), channel_id=1, source_target_pairs={{0,4},{2,10},{8,0},{10,18},{16,8},{18,26},{24,16},{26,30},{28,24},... | collective-permute-start | bytes 589832 | tf_op jit(solution)/shard_map/ppermute | solution.py:566
  21.1 0.7 copy-start.2
  21.8 12.2 %collective-permute-start.17 = (bf16[6,128,128]{2,1,0:T(8,128)(2,1)S(1)}, bf16[6,128,128]{2,1,0:T(8,128)(2,1)S(1)}, u32[]{:S(2)}, u32[]{:S(2)}) collective-permute-start(bf16[6,128,128]{2,1,0:T(8,128)(2,1)S(1)} %collective-permute-done.11.refs_6_), channel_id=1, source_target_pairs={{0,18},{2,12},{8,26},{10,4},{16,30},{18,0},{24,22},{26,8},{28,14},... | collective-permute-start | bytes 589832 | tf_op jit(solution)/shard_map/ppermute | solution.py:565
  21.9 0.7 copy-start.4
  22.6 12.0 %collective-permute-start.20 = (bf16[6,128,128]{2,1,0:T(8,128)(2,1)S(1)}, bf16[6,128,128]{2,1,0:T(8,128)(2,1)S(1)}, u32[]{:S(2)}, u32[]{:S(2)}) collective-permute-start(bf16[6,128,128]{2,1,0:T(8,128)(2,1)S(1)} %collective-permute-done.11.refs_6_), channel_id=1, source_target_pairs={{0,2},{2,0},{8,10},{10,8},{16,18},{18,16},{24,26},{26,24},{28,30},... | collective-permute-start | bytes 589832 | tf_op jit(solution)/shard_map/ppermute | solution.py:570
  24.8 10.6 %collective-permute-start.21 = (bf16[6,128,128]{2,1,0:T(8,128)(2,1)S(1)}, bf16[6,128,128]{2,1,0:T(8,128)(2,1)S(1)}, u32[]{:S(2)}, u32[]{:S(2)}) collective-permute-start(bf16[6,128,128]{2,1,0:T(8,128)(2,1)S(1)} %collective-permute-done.15.refs_7_), channel_id=1, source_target_pairs={{0,2},{2,0},{8,10},{10,8},{16,18},{18,16},{24,26},{26,24},{28,30},... | collective-permute-start | bytes 589832 | tf_op jit(solution)/shard_map/ppermute | solution.py:570
  24.8 0.7 copy-start
  30.2 0.7 copy-start.8
  30.9 5.2 %collective-permute-start.18 = (bf16[6,128,128]{2,1,0:T(8,128)(2,1)S(1)}, bf16[6,128,128]{2,1,0:T(8,128)(2,1)S(1)}, u32[]{:S(2)}, u32[]{:S(2)}) collective-permute-start(bf16[6,128,128]{2,1,0:T(8,128)(2,1)S(1)} %collective-permute-done.13.refs_4_), channel_id=1, source_target_pairs={{0,2},{2,0},{8,10},{10,8},{16,18},{18,16},{24,26},{26,24},{28,30},... | collective-permute-start | bytes 589832 | tf_op jit(solution)/shard_map/ppermute | solution.py:570
  30.9 0.7 copy-start.6
  31.6 5.1 %collective-permute-start.19 = (bf16[6,128,128]{2,1,0:T(8,128)(2,1)S(1)}, bf16[6,128,128]{2,1,0:T(8,128)(2,1)S(1)}, u32[]{:S(2)}, u32[]{:S(2)}) collective-permute-start(bf16[6,128,128]{2,1,0:T(8,128)(2,1)S(1)} %collective-permute-done.16.refs_5_), channel_id=1, source_target_pairs={{0,2},{2,0},{8,10},{10,8},{16,18},{18,16},{24,26},{26,24},{28,30},... | collective-permute-start | bytes 589832 | tf_op jit(solution)/shard_map/ppermute | solution.py:570
  32.1 0.7 copy-start.10
  34.0 0.7 copy-start.12
  34.7 0.7 copy-start.14
  35.4 0.7 copy-start.16
  36.0 0.7 copy-start.18
  36.7 0.7 copy-start.20
  37.4 0.9 %copy-start.1 = (bf16[6,128,128]{2,1,0:T(8,128)(2,1)S(1)}, bf16[6,128,128]{2,1,0:T(8,128)(2,1)}, u32[]{:S(2)}) copy-start(bf16[6,128,128]{2,1,0:T(8,128)(2,1)} %copy-done) | copy-start | bytes 589828
  38.3 0.9 %copy-start.3 = (bf16[6,128,128]{2,1,0:T(8,128)(2,1)S(1)}, bf16[6,128,128]{2,1,0:T(8,128)(2,1)}, u32[]{:S(2)}) copy-start(bf16[6,128,128]{2,1,0:T(8,128)(2,1)} %copy-done.2) | copy-start | bytes 589828
  39.3 0.9 %copy-start.5 = (bf16[6,128,128]{2,1,0:T(8,128)(2,1)S(1)}, bf16[6,128,128]{2,1,0:T(8,128)(2,1)}, u32[]{:S(2)}) copy-start(bf16[6,128,128]{2,1,0:T(8,128)(2,1)} %copy-done.4) | copy-start | bytes 589828
  40.2 0.9 %copy-start.7 = (bf16[6,128,128]{2,1,0:T(8,128)(2,1)S(1)}, bf16[6,128,128]{2,1,0:T(8,128)(2,1)}, u32[]{:S(2)}) copy-start(bf16[6,128,128]{2,1,0:T(8,128)(2,1)} %copy-done.6) | copy-start | bytes 589828
  41.1 0.9 %copy-start.9 = (bf16[6,128,128]{2,1,0:T(8,128)(2,1)S(1)}, bf16[6,128,128]{2,1,0:T(8,128)(2,1)}, u32[]{:S(2)}) copy-start(bf16[6,128,128]{2,1,0:T(8,128)(2,1)} %copy-done.8) | copy-start | bytes 589828
  42.0 0.9 %copy-start.11 = (bf16[6,128,128]{2,1,0:T(8,128)(2,1)S(1)}, bf16[6,128,128]{2,1,0:T(8,128)(2,1)}, u32[]{:S(2)}) copy-start(bf16[6,128,128]{2,1,0:T(8,128)(2,1)} %copy-done.10) | copy-start | bytes 589828
  43.0 0.9 %copy-start.13 = (bf16[6,128,128]{2,1,0:T(8,128)(2,1)S(1)}, bf16[6,128,128]{2,1,0:T(8,128)(2,1)}, u32[]{:S(2)}) copy-start(bf16[6,128,128]{2,1,0:T(8,128)(2,1)} %copy-done.12) | copy-start | bytes 589828
  43.9 0.9 %copy-start.15 = (bf16[6,128,128]{2,1,0:T(8,128)(2,1)S(1)}, bf16[6,128,128]{2,1,0:T(8,128)(2,1)}, u32[]{:S(2)}) copy-start(bf16[6,128,128]{2,1,0:T(8,128)(2,1)} %copy-done.14) | copy-start | bytes 589828
  44.8 0.9 %copy-start.17 = (bf16[6,128,128]{2,1,0:T(8,128)(2,1)S(1)}, bf16[6,128,128]{2,1,0:T(8,128)(2,1)}, u32[]{:S(2)}) copy-start(bf16[6,128,128]{2,1,0:T(8,128)(2,1)} %copy-done.16) | copy-start | bytes 589828
  45.8 0.9 %copy-start.19 = (bf16[6,128,128]{2,1,0:T(8,128)(2,1)S(1)}, bf16[6,128,128]{2,1,0:T(8,128)(2,1)}, u32[]{:S(2)}) copy-start(bf16[6,128,128]{2,1,0:T(8,128)(2,1)} %copy-done.18) | copy-start | bytes 589828
  46.7 0.9 %copy-start.21 = (bf16[6,128,128]{2,1,0:T(8,128)(2,1)S(1)}, bf16[6,128,128]{2,1,0:T(8,128)(2,1)}, u32[]{:S(2)}) copy-start(bf16[6,128,128]{2,1,0:T(8,128)(2,1)} %copy-done.20) | copy-start | bytes 589828
  58.2 2.0 %collective-permute-start.27 = (bf16[16,128,128]{2,1,0:T(8,128)(2,1)S(1)}, bf16[16,128,128]{2,1,0:T(8,128)(2,1)S(1)}, u32[]{:S(2)}, u32[]{:S(2)}) collective-permute-start(bf16[16,128,128]{2,1,0:T(8,128)(2,1)S(1)} %get-tuple-element.58), channel_id=1, source_target_pairs={{0,2},{2,0},{8,10},{10,8},{16,18},{18,16},{24,26},{26,24},{28,30},... | collective-permute-start | bytes 1572872 | tf_op jit(solution)/shard_map/ppermute | solution.py:633
  58.3 5.2 %collective-permute-start.26 = (bf16[16,128,128]{2,1,0:T(8,128)(2,1)S(1)}, bf16[16,128,128]{2,1,0:T(8,128)(2,1)S(1)}, u32[]{:S(2)}, u32[]{:S(2)}) collective-permute-start(bf16[16,128,128]{2,1,0:T(8,128)(2,1)S(1)} %get-tuple-element.57), channel_id=1, source_target_pairs={{0,2},{2,0},{8,10},{10,8},{16,18},{18,16},{24,26},{26,24},{28,30},... | collective-permute-start | bytes 1572872 | tf_op jit(solution)/shard_map/ppermute | solution.py:633
  60.3 5.0 %collective-permute-start.28 = (bf16[4,128,128]{2,1,0:T(8,128)(2,1)S(1)}, bf16[4,128,128]{2,1,0:T(8,128)(2,1)S(1)}, u32[]{:S(2)}, u32[]{:S(2)}) collective-permute-start(bf16[4,128,128]{2,1,0:T(8,128)(2,1)S(1)} %get-tuple-element.59), channel_id=1, source_target_pairs={{0,8},{2,6},{8,16},{10,2},{16,24},{18,10},{24,28},{26,18},{28,20},... | collective-permute-start | bytes 393224 | tf_op jit(solution)/shard_map/ppermute | solution.py:594
  61.0 8.4 %collective-permute-start.29 = (bf16[4,128,128]{2,1,0:T(8,128)(2,1)S(1)}, bf16[4,128,128]{2,1,0:T(8,128)(2,1)S(1)}, u32[]{:S(2)}, u32[]{:S(2)}) collective-permute-start(bf16[4,128,128]{2,1,0:T(8,128)(2,1)S(1)} %get-tuple-element.60), channel_id=1, source_target_pairs={{0,16},{2,14},{8,24},{10,6},{16,28},{18,2},{24,20},{26,10},{28,12}... | collective-permute-start | bytes 393224 | tf_op jit(solution)/shard_map/ppermute | solution.py:588
  63.5 6.5 %collective-permute-start.30 = (bf16[4,128,128]{2,1,0:T(8,128)(2,1)S(1)}, bf16[4,128,128]{2,1,0:T(8,128)(2,1)S(1)}, u32[]{:S(2)}, u32[]{:S(2)}) collective-permute-start(bf16[4,128,128]{2,1,0:T(8,128)(2,1)S(1)} %get-tuple-element.61), channel_id=1, source_target_pairs={{0,4},{2,10},{8,0},{10,18},{16,8},{18,26},{24,16},{26,30},{28,24},... | collective-permute-start | bytes 393224 | tf_op jit(solution)/shard_map/ppermute | solution.py:594
  63.5 16.4 %collective-permute-start.25 = (bf16[16,128,128]{2,1,0:T(8,128)(2,1)S(1)}, bf16[16,128,128]{2,1,0:T(8,128)(2,1)S(1)}, u32[]{:S(2)}, u32[]{:S(2)}) collective-permute-start(bf16[16,128,128]{2,1,0:T(8,128)(2,1)S(1)} %get-tuple-element.51), channel_id=1, source_target_pairs={{0,1},{1,0},{2,3},{3,2},{4,5},{5,4},{6,7},{7,6},{8,9},{9,8},{10,11... | collective-permute-start | bytes 1572872 | tf_op jit(solution)/shard_map/ppermute | solution.py:631
  70.1 9.6 %collective-permute-start.31 = (bf16[4,128,128]{2,1,0:T(8,128)(2,1)S(1)}, bf16[4,128,128]{2,1,0:T(8,128)(2,1)S(1)}, u32[]{:S(2)}, u32[]{:S(2)}) collective-permute-start(bf16[4,128,128]{2,1,0:T(8,128)(2,1)S(1)} %get-tuple-element.62), channel_id=1, source_target_pairs={{0,8},{2,6},{8,16},{10,2},{16,24},{18,10},{24,28},{26,18},{28,20},... | collective-permute-start | bytes 393224 | tf_op jit(solution)/shard_map/ppermute | solution.py:594
  70.3 9.5 %collective-permute-start.32 = (bf16[4,128,128]{2,1,0:T(8,128)(2,1)S(1)}, bf16[4,128,128]{2,1,0:T(8,128)(2,1)S(1)}, u32[]{:S(2)}, u32[]{:S(2)}) collective-permute-start(bf16[4,128,128]{2,1,0:T(8,128)(2,1)S(1)} %get-tuple-element.63), channel_id=1, source_target_pairs={{0,4},{2,10},{8,0},{10,18},{16,8},{18,26},{24,16},{26,30},{28,24},... | collective-permute-start | bytes 393224 | tf_op jit(solution)/shard_map/ppermute | solution.py:594
  72.8 5.4 %collective-permute-start.9 = (s32[1,128]{1,0:T(1,128)S(1)}, s32[1,128]{1,0:T(1,128)S(1)}, u32[]{:S(2)}, u32[]{:S(2)}) collective-permute-start(s32[1,128]{1,0:T(1,128)S(1)} %pad_bitcast_fusion.own.refs_0_), channel_id=1, source_target_pairs={{0,1},{1,0},{2,3},{3,2},{4,5},{5,4},{6,7},{7,6},{8,9},{9,8},{10,11... | collective-permute-start | bytes 1544 | tf_op jit(solution)/shard_map/ppermute | solution.py:621
  80.0 5.6 %collective-permute-start.33 = (bf16[4,128,128]{2,1,0:T(8,128)(2,1)S(1)}, bf16[4,128,128]{2,1,0:T(8,128)(2,1)S(1)}, u32[]{:S(2)}, u32[]{:S(2)}) collective-permute-start(bf16[4,128,128]{2,1,0:T(8,128)(2,1)S(1)} %get-tuple-element.70), channel_id=1, source_target_pairs={{0,8},{2,6},{8,16},{10,2},{16,24},{18,10},{24,28},{26,18},{28,20},... | collective-permute-start | bytes 393224 | tf_op jit(solution)/shard_map/ppermute | solution.py:594
  80.9 5.0 %collective-permute-start.34 = (bf16[4,128,128]{2,1,0:T(8,128)(2,1)S(1)}, bf16[4,128,128]{2,1,0:T(8,128)(2,1)S(1)}, u32[]{:S(2)}, u32[]{:S(2)}) collective-permute-start(bf16[4,128,128]{2,1,0:T(8,128)(2,1)S(1)} %get-tuple-element.71), channel_id=1, source_target_pairs={{0,4},{2,10},{8,0},{10,18},{16,8},{18,26},{24,16},{26,30},{28,24},... | collective-permute-start | bytes 393224 | tf_op jit(solution)/shard_map/ppermute | solution.py:594

commit v4 on v3

--- a/solution.py
+++ b/solution.py
@@ -555,7 +555,7 @@
     )(plan, here, ahead, behind, late)
 
 
-def gather_chunks(sz, chunk):
+def gather_chunks(sz, chunk, beside=()):
     ahead, behind, far, swap = permutations(sz)
     same, other = {0: chunk}, {}
     a = b = chunk
@@ -564,6 +564,8 @@
             same[sz.top] = lax.ppermute(a, "fsdp", far)
             other[sz.top] = lax.ppermute(a, "fsdp", [(i, j ^ 1) for i, j in far])
         a, b = lax.ppermute(a, "fsdp", ahead), lax.ppermute(b, "fsdp", behind)
+        if s <= len(beside):
+            a, b = call_turn([a, b], [beside[s - 1]])
         same[sz.ring - s], same[s] = a, b
     for d in same:
         if d != sz.top:
@@ -620,7 +622,7 @@
     plan = call_plan(sz, own)
     raws = [lax.ppermute(own, "tensor", [(i, (i + s) % T) for i in range(T)]) for s in range(1, T)]
     recv, flag = call_recv(sz, own, plan, raws)
-    chunks = gather_chunks(sz, chunk)
+    chunks = gather_chunks(sz, chunk, (plan, recv))
 
     outs = call_compute(sz, plan, tokens, cotangent, chunks)
     same, far, near, extra, idle = outs[:5]

time: 87.8 us -> 72 us (0.82)
  local copies, waits for them, and re-layouts: 18.4 us -> 0.79 us
  starting transfers between devices: 21.5 us -> 25.3 us
  waiting for transfers between devices: 28.3 us -> 26.6 us
    unnamed x44 -> x0, local copies, waits for them, and re-layouts: 17.6 us -> none
    ppermute x6, waiting for transfers between devices: 9.39 us -> 5.41 us  [gather_chunks(): a, b = (lax.ppermute(a, 'fsdp', ahead), lax.ppermute(b, 'fsdp', behind))]
    ppermute x1, waiting for transfers between devices: 0.01 us -> 3.92 us  [gather_chunks(): other[sz.top] = lax.ppermute(a, 'fsdp', [(i, j ^ 1) for i, j in far])]
    ppermute x1, waiting for transfers between devices: 5.42 us -> 1.62 us  [shards(): lax.ppermute(own, 'tensor', [(i, (i + s) % T) for i in range(T)])]
    ppermute x7, starting transfers between devices: 3.45 us -> 0.8 us  [gather_chunks(): other[d] = lax.ppermute(same[d], 'fsdp', swap)]
    ppermute x1, starting transfers between devices: 0.12 us -> 2.75 us  [gather_chunks(): other[sz.top] = lax.ppermute(a, 'fsdp', [(i, j ^ 1) for i, j in far])]
    ppermute x1, starting transfers between devices: 0.01 us -> 1.92 us  [shards(): lax.ppermute(own, 'tensor', [(i, (i + s) % T) for i in range(T)])]
    ppermute x1, starting transfers between devices: 0.01 us -> 1.5 us  [exchange(): lax.ppermute(arrays[s], 'tensor', [(i, (i + s) % T) for i in range(T)])]
  transfers between devices with their start and end apart: 26 -> 26, of which waited for: 11 -> 13; matrix products, arithmetic and copies ran while one was open for 1% -> 2% of each run, Pallas kernels for 4% -> 5%
where the time goes in v4:
time: 72 us; the launch traced here: 71.9 us
  waiting for transfers between devices  26.6 us (37%)
  starting transfers between devices  25.3 us (35%)
  Pallas kernels  16.6 us (23%)
  between operations  1.36 us (2%)
  other arithmetic  1.3 us (2%)
  local copies, waits for them, and re-layouts  0.79 us (1%)
    pallas_call x1, Pallas kernels, call_compute(): pl.pallas_call(functools.partial(compute_kernel, sz), out_shape=out_shape...  10.7 us
    ppermute x6, starting transfers between devices, gather_chunks(): a, b = (lax.ppermute(a, 'fsdp', ahead), lax.ppermute(b, 'fsdp', behind))  7.19 us
    ppermute x6, starting transfers between devices, reduce_parts(): a, b = (lax.ppermute(a, 'fsdp', ahead), lax.ppermute(b, 'fsdp', behind))  6.48 us
    ppermute x6, waiting for transfers between devices, gather_chunks(): a, b = (lax.ppermute(a, 'fsdp', ahead), lax.ppermute(b, 'fsdp', behind))  5.41 us
    ppermute x1, waiting for transfers between devices, reduce_parts(): c = lax.ppermute(c, 'fsdp', far)  4.82 us
    ppermute x1, waiting for transfers between devices, gather_chunks(): same[sz.top] = lax.ppermute(a, 'fsdp', far)  4.56 us
    ppermute x1, waiting for transfers between devices, gather_chunks(): other[sz.top] = lax.ppermute(a, 'fsdp', [(i, j ^ 1) for i, j in far])  3.92 us
    ppermute x6, waiting for transfers between devices, reduce_parts(): a, b = (lax.ppermute(a, 'fsdp', ahead), lax.ppermute(b, 'fsdp', behind))  3.4 us
  transfers between devices with their start and end apart: 26, of which 13 were waited for; matrix products, arithmetic and copies ran while one was open for 2% of the time, Pallas kernels for 5%

profile of v4, /device:TPU:0, one launch (start us, length us, event | category | flops | bytes accessed | tf_op | source)
XLA Modules:
  0.0 71.9 jit_solution(761897018772286042)
XLA Ops:
  0.6 0.9 %pad_maximum_fusion.refs_10_ = bf16[6,128,128]{2,1,0:T(8,128)(2,1)S(1)} fusion(bf16[2,128,128]{2,1,0:T(8,128)(2,1)} %bitcast.12, bf16[2,128,128]{2,1,0:T(8,128)(2,1)} %bitcast.13, bf16[2,128,128]{2,1,0:T(8,128)(2,1)} %bitcast.14), kind=kLoop, calls=%fused_computation.16 | loop fusion | flops 196608 | bytes 393216 | tf_op jit(solution)/shard_map/concatenate | solution.py:616
  1.6 3.0 %collective-permute-start.11 = (bf16[6,128,128]{2,1,0:T(8,128)(2,1)S(1)}, bf16[6,128,128]{2,1,0:T(8,128)(2,1)S(1)}, u32[]{:S(2)}, u32[]{:S(2)}) collective-permute-start(bf16[6,128,128]{2,1,0:T(8,128)(2,1)S(1)} %pad_maximum_fusion.refs_10_), channel_id=1, source_target_pairs={{0,4},{2,10},{8,0},{10,18},{16,8},{18,26},{24,16},{26,30},{28,24},... | collective-permute-start | bytes 589832 | tf_op jit(solution)/shard_map/ppermute | solution.py:566
  4.6 0.1 collective-permute-start.10
  4.7 0.8 %concatenate.6 = s32[101]{0:T(128)S(1)} concatenate(s32[32]{0:T(128)} %bitcast.15, s32[32]{0:T(128)} %bitcast.16, s32[32]{0:T(128)} %bitcast.17, s32[3]{0:T(128)} %bitcast.18, s32[1]{0:T(128)} %bitcast.4, s32[1]{0:T(128)} %bitcast.5), dimensions={0} | concatenate | bytes 808 | tf_op jit(solution)/shard_map/concatenate | solution.py:617
  5.5 0.5 plan.1.refs_1_.__2_.refs_0_
  5.9 3.9 %collective-permute-done.11.__1_ = bf16[6,128,128]{2,1,0:T(8,128)(2,1)S(1)} collective-permute-done((bf16[6,128,128]{2,1,0:T(8,128)(2,1)S(1)}, bf16[6,128,128]{2,1,0:T(8,128)(2,1)S(1)}, u32[]{:S(2)}, u32[]{:S(2)}) %collective-permute-start.11) | collective-permute-done | bytes 196640 | tf_op jit(solution)/shard_map/ppermute | solution.py:566
  9.8 0.4 collective-permute-done.10.__0_
  10.3 2.0 %collective-permute-start.12 = (bf16[6,128,128]{2,1,0:T(8,128)(2,1)S(1)}, bf16[6,128,128]{2,1,0:T(8,128)(2,1)S(1)}, u32[]{:S(2)}, u32[]{:S(2)}) collective-permute-start(bf16[6,128,128]{2,1,0:T(8,128)(2,1)S(1)} %get-tuple-element.54.refs_8_), channel_id=1, source_target_pairs={{0,8},{2,6},{8,16},{10,2},{16,24},{18,10},{24,28},{26,18},{28,20},... | collective-permute-start | bytes 589832 | tf_op jit(solution)/shard_map/ppermute | solution.py:566
  12.3 0.0 collective-permute-start.13
  12.3 0.0 collective-permute-start.24
  12.3 1.9 %collective-permute-start.9 = (s32[1,128]{1,0:T(1,128)S(1)}, s32[1,128]{1,0:T(1,128)S(1)}, u32[]{:S(2)}, u32[]{:S(2)}) collective-permute-start(s32[1,128]{1,0:T(1,128)S(1)} %pad_bitcast_fusion.own.refs_0_), channel_id=1, source_target_pairs={{0,1},{1,0},{2,3},{3,2},{4,5},{5,4},{6,7},{7,6},{8,9},{9,8},{10,11... | collective-permute-start | bytes 1544 | tf_op jit(solution)/shard_map/ppermute | solution.py:623
  14.2 1.6 %collective-permute-done.9.refs_2_ = s32[1,128]{1,0:T(1,128)S(1)} collective-permute-done((s32[1,128]{1,0:T(1,128)S(1)}, s32[1,128]{1,0:T(1,128)S(1)}, u32[]{:S(2)}, u32[]{:S(2)}) %collective-permute-start.9) | collective-permute-done | bytes 544 | tf_op jit(solution)/shard_map/ppermute | solution.py:623
  15.8 0.9 %recv.1 = (s32[8,128]{1,0:T(8,128)S(1)}, s32[1,1]{1,0:T(1,128)}) custom-call(s32[1,128]{1,0:T(1,128)S(1)} %pad_bitcast_fusion.own.refs_0_, s32[32,128]{1,0:T(8,128)S(1)} %plan.1.refs_1_.__2_.refs_0_, s32[1,128]{1,0:T(1,128)S(1)} %collective-permute-done.9.refs_2_), custom_call_target="tpu_custom_call" | custom-call | flops 1000000 | bytes 4000000 | tf_op jit(solution)/shard_map/recv/pallas_call | solution.py:459
  16.7 0.0 collective-permute-start.22
  16.7 0.5 collective-permute-start.23
  17.2 0.0 collective-permute-done.12.__0_
  17.2 0.7 collective-permute-done.13.__1_
  17.9 0.0 collective-permute-start.21
  17.9 1.0 %collective-permute-start.16 = (bf16[6,128,128]{2,1,0:T(8,128)(2,1)S(1)}, bf16[6,128,128]{2,1,0:T(8,128)(2,1)S(1)}, u32[]{:S(2)}, u32[]{:S(2)}) collective-permute-start(bf16[6,128,128]{2,1,0:T(8,128)(2,1)S(1)} %get-tuple-element.57.refs_7_), channel_id=1, source_target_pairs={{0,4},{2,10},{8,0},{10,18},{16,8},{18,26},{24,16},{26,30},{28,24},... | collective-permute-start | bytes 589832 | tf_op jit(solution)/shard_map/ppermute | solution.py:566
  18.9 0.0 collective-permute-done.24.refs_18_
  18.9 1.1 %collective-permute-start.15 = (bf16[6,128,128]{2,1,0:T(8,128)(2,1)S(1)}, bf16[6,128,128]{2,1,0:T(8,128)(2,1)S(1)}, u32[]{:S(2)}, u32[]{:S(2)}) collective-permute-start(bf16[6,128,128]{2,1,0:T(8,128)(2,1)S(1)} %get-tuple-element.56.refs_6_), channel_id=1, source_target_pairs={{0,8},{2,6},{8,16},{10,2},{16,24},{18,10},{24,28},{26,18},{28,20},... | collective-permute-start | bytes 589832 | tf_op jit(solution)/shard_map/ppermute | solution.py:566
  20.0 0.0 collective-permute-done.22.refs_16_
  20.0 0.0 collective-permute-start.20
  20.0 0.0 collective-permute-done.23.refs_17_
  20.0 2.8 %collective-permute-start.17 = (bf16[6,128,128]{2,1,0:T(8,128)(2,1)S(1)}, bf16[6,128,128]{2,1,0:T(8,128)(2,1)S(1)}, u32[]{:S(2)}, u32[]{:S(2)}) collective-permute-start(bf16[6,128,128]{2,1,0:T(8,128)(2,1)S(1)} %get-tuple-element.56.refs_6_), channel_id=1, source_target_pairs={{0,18},{2,12},{8,26},{10,4},{16,30},{18,0},{24,22},{26,8},{28,14},... | collective-permute-start | bytes 589832 | tf_op jit(solution)/shard_map/ppermute | solution.py:565
  22.7 0.0 collective-permute-done.21.refs_15_
  22.7 2.1 %collective-permute-start.14 = (bf16[6,128,128]{2,1,0:T(8,128)(2,1)S(1)}, bf16[6,128,128]{2,1,0:T(8,128)(2,1)S(1)}, u32[]{:S(2)}, u32[]{:S(2)}) collective-permute-start(bf16[6,128,128]{2,1,0:T(8,128)(2,1)S(1)} %get-tuple-element.56.refs_6_), channel_id=1, source_target_pairs={{0,16},{2,14},{8,24},{10,6},{16,28},{18,2},{24,20},{26,10},{28,12}... | collective-permute-start | bytes 589832 | tf_op jit(solution)/shard_map/ppermute | solution.py:564
  24.8 0.1 collective-permute-done.16.refs_5_
  24.9 0.0 collective-permute-start.19
  24.9 0.3 collective-permute-done.15.refs_4_
  25.2 0.3 collective-permute-start.18
  25.5 0.0 collective-permute-done.20.refs_14_
  25.5 3.9 %collective-permute-done.17.refs_11_ = bf16[6,128,128]{2,1,0:T(8,128)(2,1)S(1)} collective-permute-done((bf16[6,128,128]{2,1,0:T(8,128)(2,1)S(1)}, bf16[6,128,128]{2,1,0:T(8,128)(2,1)S(1)}, u32[]{:S(2)}, u32[]{:S(2)}) %collective-permute-start.17) | collective-permute-done | bytes 196640 | tf_op jit(solution)/shard_map/ppermute | solution.py:565
  29.5 4.6 %collective-permute-done.14.refs_3_ = bf16[6,128,128]{2,1,0:T(8,128)(2,1)S(1)} collective-permute-done((bf16[6,128,128]{2,1,0:T(8,128)(2,1)S(1)}, bf16[6,128,128]{2,1,0:T(8,128)(2,1)S(1)}, u32[]{:S(2)}, u32[]{:S(2)}) %collective-permute-start.14) | collective-permute-done | bytes 196640 | tf_op jit(solution)/shard_map/ppermute | solution.py:564
  34.0 0.0 collective-permute-done.19.refs_13_
  34.0 0.0 collective-permute-done.18.refs_12_
  34.0 10.7 %compute.1 = (bf16[32,128,128]{2,1,0:T(8,128)(2,1)S(1)}, bf16[16,128,128]{2,1,0:T(8,128)(2,1)S(1)}, bf16[16,128,128]{2,1,0:T(8,128)(2,1)S(1)}, bf16[32,128,128]{...) custom-call(s32[32,128]{1,0:T(8,128)S(1)} %plan.1.refs_1_.__2_.refs_, ...), custom_call_target="tpu_custom_call" | custom-call | flops 1000000000 | bytes 20000000 | tf_op jit(solution)/shard_map/compute/pallas_call | solution.py:515
  44.8 0.1 collective-permute-start.27
  44.8 0.5 collective-permute-start.26
  45.3 1.4 %collective-permute-done.27 = bf16[16,128,128]{2,1,0:T(8,128)(2,1)S(1)} collective-permute-done((bf16[16,128,128]{2,1,0:T(8,128)(2,1)S(1)}, bf16[16,128,128]{2,1,0:T(8,128)(2,1)S(1)}, u32[]{:S(2)}, u32[]{:S(2)}) %collective-permute-start.27) | collective-permute-done | bytes 524320 | tf_op jit(solution)/shard_map/ppermute | solution.py:635
  46.7 0.1 add_convert_fusion.12
  46.9 2.3 %collective-permute-start.28 = (bf16[4,128,128]{2,1,0:T(8,128)(2,1)S(1)}, bf16[4,128,128]{2,1,0:T(8,128)(2,1)S(1)}, u32[]{:S(2)}, u32[]{:S(2)}) collective-permute-start(bf16[4,128,128]{2,1,0:T(8,128)(2,1)S(1)} %get-tuple-element.67), channel_id=1, source_target_pairs={{0,8},{2,6},{8,16},{10,2},{16,24},{18,10},{24,28},{26,18},{28,20},... | collective-permute-start | bytes 393224 | tf_op jit(solution)/shard_map/ppermute | solution.py:596
  49.1 2.0 %collective-permute-start.29 = (bf16[4,128,128]{2,1,0:T(8,128)(2,1)S(1)}, bf16[4,128,128]{2,1,0:T(8,128)(2,1)S(1)}, u32[]{:S(2)}, u32[]{:S(2)}) collective-permute-start(bf16[4,128,128]{2,1,0:T(8,128)(2,1)S(1)} %get-tuple-element.68), channel_id=1, source_target_pairs={{0,16},{2,14},{8,24},{10,6},{16,28},{18,2},{24,20},{26,10},{28,12}... | collective-permute-start | bytes 393224 | tf_op jit(solution)/shard_map/ppermute | solution.py:590
  51.1 0.1 collective-permute-start.30
  51.2 1.5 %collective-permute-start.25 = (bf16[16,128,128]{2,1,0:T(8,128)(2,1)S(1)}, bf16[16,128,128]{2,1,0:T(8,128)(2,1)S(1)}, u32[]{:S(2)}, u32[]{:S(2)}) collective-permute-start(bf16[16,128,128]{2,1,0:T(8,128)(2,1)S(1)} %get-tuple-element.59), channel_id=1, source_target_pairs={{0,1},{1,0},{2,3},{3,2},{4,5},{5,4},{6,7},{7,6},{8,9},{9,8},{10,11... | collective-permute-start | bytes 1572872 | tf_op jit(solution)/shard_map/ppermute | solution.py:633
  52.7 0.0 collective-permute-done.26
  52.7 0.0 collective-permute-done.28
  52.7 4.8 %collective-permute-done.29 = bf16[4,128,128]{2,1,0:T(8,128)(2,1)S(1)} collective-permute-done((bf16[4,128,128]{2,1,0:T(8,128)(2,1)S(1)}, bf16[4,128,128]{2,1,0:T(8,128)(2,1)S(1)}, u32[]{:S(2)}, u32[]{:S(2)}) %collective-permute-start.29) | collective-permute-done | bytes 131104 | tf_op jit(solution)/shard_map/ppermute | solution.py:590
  57.5 0.0 collective-permute-done.30
  57.5 0.1 add_convert_fusion.10
  57.6 0.2 collective-permute-start.31
  57.9 1.9 %collective-permute-start.32 = (bf16[4,128,128]{2,1,0:T(8,128)(2,1)S(1)}, bf16[4,128,128]{2,1,0:T(8,128)(2,1)S(1)}, u32[]{:S(2)}, u32[]{:S(2)}) collective-permute-start(bf16[4,128,128]{2,1,0:T(8,128)(2,1)S(1)} %get-tuple-element.71), channel_id=1, source_target_pairs={{0,4},{2,10},{8,0},{10,18},{16,8},{18,26},{24,16},{26,30},{28,24},... | collective-permute-start | bytes 393224 | tf_op jit(solution)/shard_map/ppermute | solution.py:596
  60.4 3.1 %collective-permute-done.31 = bf16[4,128,128]{2,1,0:T(8,128)(2,1)S(1)} collective-permute-done((bf16[4,128,128]{2,1,0:T(8,128)(2,1)S(1)}, bf16[4,128,128]{2,1,0:T(8,128)(2,1)S(1)}, u32[]{:S(2)}, u32[]{:S(2)}) %collective-permute-start.31) | collective-permute-done | bytes 131104 | tf_op jit(solution)/shard_map/ppermute | solution.py:596
  63.5 0.0 collective-permute-done.32
  63.5 0.1 convert_add_fusion
  63.6 1.4 %collective-permute-done.25.__2_.refs_3_ = bf16[16,128,128]{2,1,0:T(8,128)(2,1)S(1)} collective-permute-done((bf16[16,128,128]{2,1,0:T(8,128)(2,1)S(1)}, bf16[16,128,128]{2,1,0:T(8,128)(2,1)S(1)}, u32[]{:S(2)}, u32[]{:S(2)}) %collective-permute-start.25) | collective-permute-done | bytes 524320 | tf_op jit(solution)/shard_map/ppermute | solution.py:633
  65.1 0.3 collective-permute-start.33
  65.3 1.7 %collective-permute-start.34 = (bf16[4,128,128]{2,1,0:T(8,128)(2,1)S(1)}, bf16[4,128,128]{2,1,0:T(8,128)(2,1)S(1)}, u32[]{:S(2)}, u32[]{:S(2)}) collective-permute-start(bf16[4,128,128]{2,1,0:T(8,128)(2,1)S(1)} %get-tuple-element.79), channel_id=1, source_target_pairs={{0,4},{2,10},{8,0},{10,18},{16,8},{18,26},{24,16},{26,30},{28,24},... | collective-permute-start | bytes 393224 | tf_op jit(solution)/shard_map/ppermute | solution.py:596
  67.1 3.0 %join.1 = (bf16[128,4096]{1,0:T(8,128)(2,1)}, bf16[128,4096]{1,0:T(8,128)(2,1)}) custom-call(s32[32,128]{1,0:T(8,128)S(1)} %plan.1.refs_1_.__2_.refs_0_, s32[8,128]{1,0:T(8,128)S(1)} %get-tuple-element.53.__2_.refs_1_, bf16[16,128,128]{2,1,0:T(8,128)(2,1)S(1)} %get-tuple-element.58.refs_2_, bf16[16,128,128]{2,1,0:T(8,128)(2,1)S(1)} %collective-permute-done.25.__2_.refs_3_, ...), custom_call_target="tpu_custom_call" | custom-call | flops 1000000 | bytes 6000000 | tf_op jit(solution)/shard_map/join/pallas_call | solution.py:533
  70.0 0.3 collective-permute-done.33.ahead
  70.3 0.0 collective-permute-done.34.behind
  70.3 1.5 %finish.1 = (bf16[1,2,128,128]{3,2,1,0:T(8,128)(2,1)}, bf16[1,2,128,128]{3,2,1,0:T(8,128)(2,1)}, bf16[1,2,128,128]{3,2,1,0:T(8,128)(2,1)}) custom-call(s32[32,128]{1,0:T(8,128)S(1)} %plan.1.refs_1_.__2_.refs_0_, f32[4,128,128]{2,1,0:T(8,128)S(1)} %get-tuple-element.91.here, bf16[4,128,128]{2,1,0:T(8,128)(2,1)S(1)} %collective-permute-done.33.ahead, ...), custom_call_target="tpu_custom_call" | custom-call | flops 1000000 | bytes 1000000 | tf_op jit(solution)/shard_map/finish/pallas_call | solution.py:547
  (5 shorter events, 0.0 us)
Async XLA Ops:
  1.6 8.3 %collective-permute-start.11 = (bf16[6,128,128]{2,1,0:T(8,128)(2,1)S(1)}, bf16[6,128,128]{2,1,0:T(8,128)(2,1)S(1)}, u32[]{:S(2)}, u32[]{:S(2)}) collective-permute-start(bf16[6,128,128]{2,1,0:T(8,128)(2,1)S(1)} %pad_maximum_fusion.refs_10_), channel_id=1, source_target_pairs={{0,4},{2,10},{8,0},{10,18},{16,8},{18,26},{24,16},{26,30},{28,24},... | collective-permute-start | bytes 589832 | tf_op jit(solution)/shard_map/ppermute | solution.py:566
  4.6 5.7 %collective-permute-start.10 = (bf16[6,128,128]{2,1,0:T(8,128)(2,1)S(1)}, bf16[6,128,128]{2,1,0:T(8,128)(2,1)S(1)}, u32[]{:S(2)}, u32[]{:S(2)}) collective-permute-start(bf16[6,128,128]{2,1,0:T(8,128)(2,1)S(1)} %pad_maximum_fusion.refs_10_), channel_id=1, source_target_pairs={{0,8},{2,6},{8,16},{10,2},{16,24},{18,10},{24,28},{26,18},{28,20},... | collective-permute-start | bytes 589832 | tf_op jit(solution)/shard_map/ppermute | solution.py:566
  10.3 7.0 %collective-permute-start.12 = (bf16[6,128,128]{2,1,0:T(8,128)(2,1)S(1)}, bf16[6,128,128]{2,1,0:T(8,128)(2,1)S(1)}, u32[]{:S(2)}, u32[]{:S(2)}) collective-permute-start(bf16[6,128,128]{2,1,0:T(8,128)(2,1)S(1)} %get-tuple-element.54.refs_8_), channel_id=1, source_target_pairs={{0,8},{2,6},{8,16},{10,2},{16,24},{18,10},{24,28},{26,18},{28,20},... | collective-permute-start | bytes 589832 | tf_op jit(solution)/shard_map/ppermute | solution.py:566
  12.3 5.7 %collective-permute-start.13 = (bf16[6,128,128]{2,1,0:T(8,128)(2,1)S(1)}, bf16[6,128,128]{2,1,0:T(8,128)(2,1)S(1)}, u32[]{:S(2)}, u32[]{:S(2)}) collective-permute-start(bf16[6,128,128]{2,1,0:T(8,128)(2,1)S(1)} %get-tuple-element.55.refs_9_), channel_id=1, source_target_pairs={{0,4},{2,10},{8,0},{10,18},{16,8},{18,26},{24,16},{26,30},{28,24},... | collective-permute-start | bytes 589832 | tf_op jit(solution)/shard_map/ppermute | solution.py:566
  12.3 6.6 %collective-permute-start.24 = (bf16[6,128,128]{2,1,0:T(8,128)(2,1)S(1)}, bf16[6,128,128]{2,1,0:T(8,128)(2,1)S(1)}, u32[]{:S(2)}, u32[]{:S(2)}) collective-permute-start(bf16[6,128,128]{2,1,0:T(8,128)(2,1)S(1)} %pad_maximum_fusion.refs_10_), channel_id=1, source_target_pairs={{0,2},{2,0},{8,10},{10,8},{16,18},{18,16},{24,26},{26,24},{28,30},... | collective-permute-start | bytes 589832 | tf_op jit(solution)/shard_map/ppermute | solution.py:572
  12.3 3.5 %collective-permute-start.9 = (s32[1,128]{1,0:T(1,128)S(1)}, s32[1,128]{1,0:T(1,128)S(1)}, u32[]{:S(2)}, u32[]{:S(2)}) collective-permute-start(s32[1,128]{1,0:T(1,128)S(1)} %pad_bitcast_fusion.own.refs_0_), channel_id=1, source_target_pairs={{0,1},{1,0},{2,3},{3,2},{4,5},{5,4},{6,7},{7,6},{8,9},{9,8},{10,11... | collective-permute-start | bytes 1544 | tf_op jit(solution)/shard_map/ppermute | solution.py:623
  16.7 3.2 %collective-permute-start.22 = (bf16[6,128,128]{2,1,0:T(8,128)(2,1)S(1)}, bf16[6,128,128]{2,1,0:T(8,128)(2,1)S(1)}, u32[]{:S(2)}, u32[]{:S(2)}) collective-permute-start(bf16[6,128,128]{2,1,0:T(8,128)(2,1)S(1)} %get-tuple-element.54.refs_8_), channel_id=1, source_target_pairs={{0,2},{2,0},{8,10},{10,8},{16,18},{18,16},{24,26},{26,24},{28,30},... | collective-permute-start | bytes 589832 | tf_op jit(solution)/shard_map/ppermute | solution.py:572
  16.7 3.2 %collective-permute-start.23 = (bf16[6,128,128]{2,1,0:T(8,128)(2,1)S(1)}, bf16[6,128,128]{2,1,0:T(8,128)(2,1)S(1)}, u32[]{:S(2)}, u32[]{:S(2)}) collective-permute-start(bf16[6,128,128]{2,1,0:T(8,128)(2,1)S(1)} %get-tuple-element.55.refs_9_), channel_id=1, source_target_pairs={{0,2},{2,0},{8,10},{10,8},{16,18},{18,16},{24,26},{26,24},{28,30},... | collective-permute-start | bytes 589832 | tf_op jit(solution)/shard_map/ppermute | solution.py:572
  17.9 4.8 %collective-permute-start.21 = (bf16[6,128,128]{2,1,0:T(8,128)(2,1)S(1)}, bf16[6,128,128]{2,1,0:T(8,128)(2,1)S(1)}, u32[]{:S(2)}, u32[]{:S(2)}) collective-permute-start(bf16[6,128,128]{2,1,0:T(8,128)(2,1)S(1)} %get-tuple-element.57.refs_7_), channel_id=1, source_target_pairs={{0,2},{2,0},{8,10},{10,8},{16,18},{18,16},{24,26},{26,24},{28,30},... | collective-permute-start | bytes 589832 | tf_op jit(solution)/shard_map/ppermute | solution.py:572
  17.9 7.0 %collective-permute-start.16 = (bf16[6,128,128]{2,1,0:T(8,128)(2,1)S(1)}, bf16[6,128,128]{2,1,0:T(8,128)(2,1)S(1)}, u32[]{:S(2)}, u32[]{:S(2)}) collective-permute-start(bf16[6,128,128]{2,1,0:T(8,128)(2,1)S(1)} %get-tuple-element.57.refs_7_), channel_id=1, source_target_pairs={{0,4},{2,10},{8,0},{10,18},{16,8},{18,26},{24,16},{26,30},{28,24},... | collective-permute-start | bytes 589832 | tf_op jit(solution)/shard_map/ppermute | solution.py:566
  18.9 6.3 %collective-permute-start.15 = (bf16[6,128,128]{2,1,0:T(8,128)(2,1)S(1)}, bf16[6,128,128]{2,1,0:T(8,128)(2,1)S(1)}, u32[]{:S(2)}, u32[]{:S(2)}) collective-permute-start(bf16[6,128,128]{2,1,0:T(8,128)(2,1)S(1)} %get-tuple-element.56.refs_6_), channel_id=1, source_target_pairs={{0,8},{2,6},{8,16},{10,2},{16,24},{18,10},{24,28},{26,18},{28,20},... | collective-permute-start | bytes 589832 | tf_op jit(solution)/shard_map/ppermute | solution.py:566
  20.0 5.6 %collective-permute-start.20 = (bf16[6,128,128]{2,1,0:T(8,128)(2,1)S(1)}, bf16[6,128,128]{2,1,0:T(8,128)(2,1)S(1)}, u32[]{:S(2)}, u32[]{:S(2)}) collective-permute-start(bf16[6,128,128]{2,1,0:T(8,128)(2,1)S(1)} %get-tuple-element.56.refs_6_), channel_id=1, source_target_pairs={{0,2},{2,0},{8,10},{10,8},{16,18},{18,16},{24,26},{26,24},{28,30},... | collective-permute-start | bytes 589832 | tf_op jit(solution)/shard_map/ppermute | solution.py:572
  20.0 9.5 %collective-permute-start.17 = (bf16[6,128,128]{2,1,0:T(8,128)(2,1)S(1)}, bf16[6,128,128]{2,1,0:T(8,128)(2,1)S(1)}, u32[]{:S(2)}, u32[]{:S(2)}) collective-permute-start(bf16[6,128,128]{2,1,0:T(8,128)(2,1)S(1)} %get-tuple-element.56.refs_6_), channel_id=1, source_target_pairs={{0,18},{2,12},{8,26},{10,4},{16,30},{18,0},{24,22},{26,8},{28,14},... | collective-permute-start | bytes 589832 | tf_op jit(solution)/shard_map/ppermute | solution.py:565
  22.7 11.3 %collective-permute-start.14 = (bf16[6,128,128]{2,1,0:T(8,128)(2,1)S(1)}, bf16[6,128,128]{2,1,0:T(8,128)(2,1)S(1)}, u32[]{:S(2)}, u32[]{:S(2)}) collective-permute-start(bf16[6,128,128]{2,1,0:T(8,128)(2,1)S(1)} %get-tuple-element.56.refs_6_), channel_id=1, source_target_pairs={{0,16},{2,14},{8,24},{10,6},{16,28},{18,2},{24,20},{26,10},{28,12}... | collective-permute-start | bytes 589832 | tf_op jit(solution)/shard_map/ppermute | solution.py:564
  24.9 9.1 %collective-permute-start.19 = (bf16[6,128,128]{2,1,0:T(8,128)(2,1)S(1)}, bf16[6,128,128]{2,1,0:T(8,128)(2,1)S(1)}, u32[]{:S(2)}, u32[]{:S(2)}) collective-permute-start(bf16[6,128,128]{2,1,0:T(8,128)(2,1)S(1)} %collective-permute-done.16.refs_5_), channel_id=1, source_target_pairs={{0,2},{2,0},{8,10},{10,8},{16,18},{18,16},{24,26},{26,24},{28,30},... | collective-permute-start | bytes 589832 | tf_op jit(solution)/shard_map/ppermute | solution.py:572
  25.2 8.8 %collective-permute-start.18 = (bf16[6,128,128]{2,1,0:T(8,128)(2,1)S(1)}, bf16[6,128,128]{2,1,0:T(8,128)(2,1)S(1)}, u32[]{:S(2)}, u32[]{:S(2)}) collective-permute-start(bf16[6,128,128]{2,1,0:T(8,128)(2,1)S(1)} %collective-permute-done.15.refs_4_), channel_id=1, source_target_pairs={{0,2},{2,0},{8,10},{10,8},{16,18},{18,16},{24,26},{26,24},{28,30},... | collective-permute-start | bytes 589832 | tf_op jit(solution)/shard_map/ppermute | solution.py:572
  44.8 2.0 %collective-permute-start.27 = (bf16[16,128,128]{2,1,0:T(8,128)(2,1)S(1)}, bf16[16,128,128]{2,1,0:T(8,128)(2,1)S(1)}, u32[]{:S(2)}, u32[]{:S(2)}) collective-permute-start(bf16[16,128,128]{2,1,0:T(8,128)(2,1)S(1)} %get-tuple-element.66), channel_id=1, source_target_pairs={{0,2},{2,0},{8,10},{10,8},{16,18},{18,16},{24,26},{26,24},{28,30},... | collective-permute-start | bytes 1572872 | tf_op jit(solution)/shard_map/ppermute | solution.py:635
  44.8 7.8 %collective-permute-start.26 = (bf16[16,128,128]{2,1,0:T(8,128)(2,1)S(1)}, bf16[16,128,128]{2,1,0:T(8,128)(2,1)S(1)}, u32[]{:S(2)}, u32[]{:S(2)}) collective-permute-start(bf16[16,128,128]{2,1,0:T(8,128)(2,1)S(1)} %get-tuple-element.65), channel_id=1, source_target_pairs={{0,2},{2,0},{8,10},{10,8},{16,18},{18,16},{24,26},{26,24},{28,30},... | collective-permute-start | bytes 1572872 | tf_op jit(solution)/shard_map/ppermute | solution.py:635
  46.9 5.8 %collective-permute-start.28 = (bf16[4,128,128]{2,1,0:T(8,128)(2,1)S(1)}, bf16[4,128,128]{2,1,0:T(8,128)(2,1)S(1)}, u32[]{:S(2)}, u32[]{:S(2)}) collective-permute-start(bf16[4,128,128]{2,1,0:T(8,128)(2,1)S(1)} %get-tuple-element.67), channel_id=1, source_target_pairs={{0,8},{2,6},{8,16},{10,2},{16,24},{18,10},{24,28},{26,18},{28,20},... | collective-permute-start | bytes 393224 | tf_op jit(solution)/shard_map/ppermute | solution.py:596
  49.1 8.4 %collective-permute-start.29 = (bf16[4,128,128]{2,1,0:T(8,128)(2,1)S(1)}, bf16[4,128,128]{2,1,0:T(8,128)(2,1)S(1)}, u32[]{:S(2)}, u32[]{:S(2)}) collective-permute-start(bf16[4,128,128]{2,1,0:T(8,128)(2,1)S(1)} %get-tuple-element.68), channel_id=1, source_target_pairs={{0,16},{2,14},{8,24},{10,6},{16,28},{18,2},{24,20},{26,10},{28,12}... | collective-permute-start | bytes 393224 | tf_op jit(solution)/shard_map/ppermute | solution.py:590
  51.1 6.4 %collective-permute-start.30 = (bf16[4,128,128]{2,1,0:T(8,128)(2,1)S(1)}, bf16[4,128,128]{2,1,0:T(8,128)(2,1)S(1)}, u32[]{:S(2)}, u32[]{:S(2)}) collective-permute-start(bf16[4,128,128]{2,1,0:T(8,128)(2,1)S(1)} %get-tuple-element.69), channel_id=1, source_target_pairs={{0,4},{2,10},{8,0},{10,18},{16,8},{18,26},{24,16},{26,30},{28,24},... | collective-permute-start | bytes 393224 | tf_op jit(solution)/shard_map/ppermute | solution.py:596
  51.2 13.9 %collective-permute-start.25 = (bf16[16,128,128]{2,1,0:T(8,128)(2,1)S(1)}, bf16[16,128,128]{2,1,0:T(8,128)(2,1)S(1)}, u32[]{:S(2)}, u32[]{:S(2)}) collective-permute-start(bf16[16,128,128]{2,1,0:T(8,128)(2,1)S(1)} %get-tuple-element.59), channel_id=1, source_target_pairs={{0,1},{1,0},{2,3},{3,2},{4,5},{5,4},{6,7},{7,6},{8,9},{9,8},{10,11... | collective-permute-start | bytes 1572872 | tf_op jit(solution)/shard_map/ppermute | solution.py:633
  57.6 5.8 %collective-permute-start.31 = (bf16[4,128,128]{2,1,0:T(8,128)(2,1)S(1)}, bf16[4,128,128]{2,1,0:T(8,128)(2,1)S(1)}, u32[]{:S(2)}, u32[]{:S(2)}) collective-permute-start(bf16[4,128,128]{2,1,0:T(8,128)(2,1)S(1)} %get-tuple-element.70), channel_id=1, source_target_pairs={{0,8},{2,6},{8,16},{10,2},{16,24},{18,10},{24,28},{26,18},{28,20},... | collective-permute-start | bytes 393224 | tf_op jit(solution)/shard_map/ppermute | solution.py:596
  57.9 5.6 %collective-permute-start.32 = (bf16[4,128,128]{2,1,0:T(8,128)(2,1)S(1)}, bf16[4,128,128]{2,1,0:T(8,128)(2,1)S(1)}, u32[]{:S(2)}, u32[]{:S(2)}) collective-permute-start(bf16[4,128,128]{2,1,0:T(8,128)(2,1)S(1)} %get-tuple-element.71), channel_id=1, source_target_pairs={{0,4},{2,10},{8,0},{10,18},{16,8},{18,26},{24,16},{26,30},{28,24},... | collective-permute-start | bytes 393224 | tf_op jit(solution)/shard_map/ppermute | solution.py:596
  65.1 5.3 %collective-permute-start.33 = (bf16[4,128,128]{2,1,0:T(8,128)(2,1)S(1)}, bf16[4,128,128]{2,1,0:T(8,128)(2,1)S(1)}, u32[]{:S(2)}, u32[]{:S(2)}) collective-permute-start(bf16[4,128,128]{2,1,0:T(8,128)(2,1)S(1)} %get-tuple-element.78), channel_id=1, source_target_pairs={{0,8},{2,6},{8,16},{10,2},{16,24},{18,10},{24,28},{26,18},{28,20},... | collective-permute-start | bytes 393224 | tf_op jit(solution)/shard_map/ppermute | solution.py:596
  65.3 5.0 %collective-permute-start.34 = (bf16[4,128,128]{2,1,0:T(8,128)(2,1)S(1)}, bf16[4,128,128]{2,1,0:T(8,128)(2,1)S(1)}, u32[]{:S(2)}, u32[]{:S(2)}) collective-permute-start(bf16[4,128,128]{2,1,0:T(8,128)(2,1)S(1)} %get-tuple-element.79), channel_id=1, source_target_pairs={{0,4},{2,10},{8,0},{10,18},{16,8},{18,26},{24,16},{26,30},{28,24},... | collective-permute-start | bytes 393224 | tf_op jit(solution)/shard_map/ppermute | solution.py:596

commit v5 on v4

--- a/solution.py
+++ b/solution.py
@@ -56,14 +56,13 @@
 
 def permutations(sz):
     seq = list(range(0, sz.ring, 2)) + list(range(sz.ring - 1, 0, -2))
-    ahead, behind, far, swap = [], [], [], []
+    ahead, behind, swap = [], [], []
     for i, q in enumerate(seq):
         up, down = seq[(i + 1) % sz.ring], seq[i - 1]
-        far += [(q * 2, seq[(i + 2) % sz.ring] * 2), (q * 2 + 1, seq[i - 2] * 2 + 1)]
         ahead += [(q * 2, up * 2), (q * 2 + 1, down * 2 + 1)]
         behind += [(q * 2, down * 2), (q * 2 + 1, up * 2 + 1)]
         swap += [(q * 2, q * 2 + 1), (q * 2 + 1, q * 2)]
-    return ahead, behind, far, swap
+    return ahead, behind, swap
 
 
 def ratio(x, d):
@@ -556,25 +555,22 @@
 
 
 def gather_chunks(sz, chunk, beside=()):
-    ahead, behind, far, swap = permutations(sz)
-    same, other = {0: chunk}, {}
+    ahead, behind, swap = permutations(sz)
+    same = {0: chunk}
     a = b = chunk
     for s in range(1, sz.top):
-        if s == sz.top - 1:
-            same[sz.top] = lax.ppermute(a, "fsdp", far)
-            other[sz.top] = lax.ppermute(a, "fsdp", [(i, j ^ 1) for i, j in far])
         a, b = lax.ppermute(a, "fsdp", ahead), lax.ppermute(b, "fsdp", behind)
         if s <= len(beside):
             a, b = call_turn([a, b], [beside[s - 1]])
         same[sz.ring - s], same[s] = a, b
-    for d in same:
-        if d != sz.top:
-            other[d] = lax.ppermute(same[d], "fsdp", swap)
+    other = {d: lax.ppermute(same[d], "fsdp", swap) for d in same}
+    same[sz.top] = lax.ppermute(a, "fsdp", ahead)
+    other[sz.top] = lax.ppermute(a, "fsdp", [(i, j ^ 1) for i, j in ahead])
     return [side[d] for side in (same, other) for d in sz.order]
 
 
-def reduce_parts(sz, per, same, pair, beside=lambda s, a, b: (a, b)):
-    ahead, behind, far, _ = permutations(sz)
+def reduce_parts(sz, per, same, pair, beside=lambda a: a):
+    ahead, behind, _ = permutations(sz)
 
     def wide(d, *more):
         j = sz.order.index(d)
@@ -586,14 +582,13 @@
     def term(d, *more):
         return wide(d, *more).astype(jnp.bfloat16)
 
-    c, a, b = lax.optimization_barrier((term(sz.top), term(sz.top - 1), term(sz.top + 1)))
-    c = lax.ppermute(c, "fsdp", far)
+    a, b = lax.optimization_barrier((term(sz.top), term(sz.top + 1)))
     for s in range(1, sz.top):
-        if s > 1:
-            a = term(sz.top - s, a, c) if s == 2 else term(sz.top - s, a)
-            b = term(sz.top + s, b)
-            a, b = beside(s, *lax.optimization_barrier((a, b)))
         a, b = lax.ppermute(a, "fsdp", ahead), lax.ppermute(b, "fsdp", behind)
+        a = term(sz.top - s, a)
+        if s + 1 < sz.top:
+            a, b = lax.optimization_barrier((a, term(sz.top + 1 + s, b)))
+    a = lax.ppermute(beside(a), "fsdp", ahead)
     return wide(0), a, b
 
 
@@ -641,13 +636,11 @@
 
     late = idle
 
-    def beside(s, a, b):
+    def beside(a):
         nonlocal rests, late
-        if s != sz.top - 1:
-            return a, b
-        a, more = call_turn([a, extra], firsts[1:])
+        a, more = call_turn([a, extra], [])
         if sz.rest + sz.more == 0:
-            return a, b
+            return a
 
         def spill(rests, extra, idle):
             moved = exchange(rests)
@@ -659,7 +652,7 @@
             return moved, sum(t.astype(jnp.float32) for t in terms).astype(jnp.bfloat16)
 
         rests, late = lax.cond(flag[0, 0] > 0, spill, lambda r, e, i: (r, i), rests, more, idle)
-        return a, b
+        return a
 
     here, ahead, behind = reduce_parts(sz, sz.keep, same, pair, beside)
     outputs, input_grads = call_join(sz, plan, recv, firsts, rests)

time: 72 us -> 72.3 us (level)
  waiting for transfers between devices: 26.6 us -> 30 us
  starting transfers between devices: 25.3 us -> 22.1 us
    ppermute x6, waiting for transfers between devices: 3.4 us -> 12.6 us  [reduce_parts(): a, b = (lax.ppermute(a, 'fsdp', ahead), lax.ppermute(b, 'fsdp', behind))]
    ppermute x10, waiting for transfers between devices: 13.3 us -> 4.43 us  [the longest x1 2.79 us: gather_chunks(): same[sz.top] = lax.ppermute(a, 'fsdp', ahead)]
    ppermute x6, waiting for transfers between devices: 5.41 us -> 8.69 us  [gather_chunks(): a, b = (lax.ppermute(a, 'fsdp', ahead), lax.ppermute(b, 'fsdp', behind))]
    ppermute x10, starting transfers between devices: 7.63 us -> 6.01 us  [the longest x1 1.93 us: gather_chunks(): same[sz.top] = lax.ppermute(a, 'fsdp', ahead)]
    ppermute x1, starting transfers between devices: 1.5 us -> 0.08 us  [exchange(): lax.ppermute(arrays[s], 'tensor', [(i, (i + s) % T) for i in range(T)])]
  transfers between devices with their start and end apart: 26 -> 26, of which waited for: 13 -> 16; matrix products, arithmetic and copies ran while one was open for 2% -> 2% of each run, Pallas kernels for 5% -> 4%
where the time goes in v5:
time: 72.3 us; the launch traced here: 71.8 us
  waiting for transfers between devices  30 us (41%)
  starting transfers between devices  22.1 us (31%)
  Pallas kernels  16.3 us (23%)
  between operations  1.39 us (2%)
  other arithmetic  1.3 us (2%)
  local copies, waits for them, and re-layouts  0.79 us (1%)
    ppermute x6, waiting for transfers between devices, reduce_parts(): a, b = (lax.ppermute(a, 'fsdp', ahead), lax.ppermute(b, 'fsdp', behind))  12.6 us
    pallas_call x1, Pallas kernels, call_compute(): pl.pallas_call(functools.partial(compute_kernel, sz), out_shape=out_shape...  10.8 us
    ppermute x6, waiting for transfers between devices, gather_chunks(): a, b = (lax.ppermute(a, 'fsdp', ahead), lax.ppermute(b, 'fsdp', behind))  8.69 us
    ppermute x6, starting transfers between devices, gather_chunks(): a, b = (lax.ppermute(a, 'fsdp', ahead), lax.ppermute(b, 'fsdp', behind))  7.19 us
    ppermute x6, starting transfers between devices, reduce_parts(): a, b = (lax.ppermute(a, 'fsdp', ahead), lax.ppermute(b, 'fsdp', behind))  6.29 us
    ppermute x1, waiting for transfers between devices, gather_chunks(): same[sz.top] = lax.ppermute(a, 'fsdp', ahead)  2.79 us
    pallas_call x1, Pallas kernels, call_join(): pl.pallas_call(functools.partial(join_kernel, sz), out_shape=[half, half]...  2.65 us
    ppermute x1, starting transfers between devices, gather_chunks(): same[sz.top] = lax.ppermute(a, 'fsdp', ahead)  1.93 us
  transfers between devices with their start and end apart: 26, of which 16 were waited for; matrix products, arithmetic and copies ran while one was open for 2% of the time, Pallas kernels for 4%

profile of v5, /device:TPU:0, one launch (start us, length us, event | category | flops | bytes accessed | tf_op | source)
XLA Modules:
  0.0 71.8 jit_solution(16799056570375116873)
XLA Ops:
  0.6 0.9 %pad_maximum_fusion.refs_10_ = bf16[6,128,128]{2,1,0:T(8,128)(2,1)S(1)} fusion(bf16[2,128,128]{2,1,0:T(8,128)(2,1)} %bitcast.12, bf16[2,128,128]{2,1,0:T(8,128)(2,1)} %bitcast.13, bf16[2,128,128]{2,1,0:T(8,128)(2,1)} %bitcast.14), kind=kLoop, calls=%fused_computation.16 | loop fusion | flops 196608 | bytes 393216 | tf_op jit(solution)/shard_map/concatenate | solution.py:611
  1.6 3.0 %collective-permute-start.11 = (bf16[6,128,128]{2,1,0:T(8,128)(2,1)S(1)}, bf16[6,128,128]{2,1,0:T(8,128)(2,1)S(1)}, u32[]{:S(2)}, u32[]{:S(2)}) collective-permute-start(bf16[6,128,128]{2,1,0:T(8,128)(2,1)S(1)} %pad_maximum_fusion.refs_10_), channel_id=1, source_target_pairs={{0,4},{2,10},{8,0},{10,18},{16,8},{18,26},{24,16},{26,30},{28,24},... | collective-permute-start | bytes 589832 | tf_op jit(solution)/shard_map/ppermute | solution.py:562
  4.6 0.1 collective-permute-start.10
  4.7 0.8 %concatenate.6 = s32[101]{0:T(128)S(1)} concatenate(s32[32]{0:T(128)} %bitcast.15, s32[32]{0:T(128)} %bitcast.16, s32[32]{0:T(128)} %bitcast.17, s32[3]{0:T(128)} %bitcast.18, s32[1]{0:T(128)} %bitcast.4, s32[1]{0:T(128)} %bitcast.5), dimensions={0} | concatenate | bytes 808 | tf_op jit(solution)/shard_map/concatenate | solution.py:612
  5.5 0.5 plan.1.refs_1_.__2_.refs_0_
  5.9 3.9 %collective-permute-done.11.__1_ = bf16[6,128,128]{2,1,0:T(8,128)(2,1)S(1)} collective-permute-done((bf16[6,128,128]{2,1,0:T(8,128)(2,1)S(1)}, bf16[6,128,128]{2,1,0:T(8,128)(2,1)S(1)}, u32[]{:S(2)}, u32[]{:S(2)}) %collective-permute-start.11) | collective-permute-done | bytes 196640 | tf_op jit(solution)/shard_map/ppermute | solution.py:562
  9.8 0.4 collective-permute-done.10.__0_
  10.3 2.0 %collective-permute-start.12 = (bf16[6,128,128]{2,1,0:T(8,128)(2,1)S(1)}, bf16[6,128,128]{2,1,0:T(8,128)(2,1)S(1)}, u32[]{:S(2)}, u32[]{:S(2)}) collective-permute-start(bf16[6,128,128]{2,1,0:T(8,128)(2,1)S(1)} %get-tuple-element.52.refs_8_), channel_id=1, source_target_pairs={{0,8},{2,6},{8,16},{10,2},{16,24},{18,10},{24,28},{26,18},{28,20},... | collective-permute-start | bytes 589832 | tf_op jit(solution)/shard_map/ppermute | solution.py:562
  12.3 0.0 collective-permute-start.13
  12.3 0.0 collective-permute-start.24
  12.3 1.9 %collective-permute-start.9 = (s32[1,128]{1,0:T(1,128)S(1)}, s32[1,128]{1,0:T(1,128)S(1)}, u32[]{:S(2)}, u32[]{:S(2)}) collective-permute-start(s32[1,128]{1,0:T(1,128)S(1)} %pad_bitcast_fusion.own.refs_0_), channel_id=1, source_target_pairs={{0,1},{1,0},{2,3},{3,2},{4,5},{5,4},{6,7},{7,6},{8,9},{9,8},{10,11... | collective-permute-start | bytes 1544 | tf_op jit(solution)/shard_map/ppermute | solution.py:618
  14.2 1.6 %collective-permute-done.9.refs_2_ = s32[1,128]{1,0:T(1,128)S(1)} collective-permute-done((s32[1,128]{1,0:T(1,128)S(1)}, s32[1,128]{1,0:T(1,128)S(1)}, u32[]{:S(2)}, u32[]{:S(2)}) %collective-permute-start.9) | collective-permute-done | bytes 544 | tf_op jit(solution)/shard_map/ppermute | solution.py:618
  15.8 0.9 %recv.1 = (s32[8,128]{1,0:T(8,128)S(1)}, s32[1,1]{1,0:T(1,128)}) custom-call(s32[1,128]{1,0:T(1,128)S(1)} %pad_bitcast_fusion.own.refs_0_, s32[32,128]{1,0:T(8,128)S(1)} %plan.1.refs_1_.__2_.refs_0_, s32[1,128]{1,0:T(1,128)S(1)} %collective-permute-done.9.refs_2_), custom_call_target="tpu_custom_call" | custom-call | flops 1000000 | bytes 4000000 | tf_op jit(solution)/shard_map/recv/pallas_call | solution.py:458
  16.7 0.0 collective-permute-start.22
  16.7 0.5 collective-permute-done.12.__0_
  17.2 0.7 %collective-permute-done.13.__1_ = bf16[6,128,128]{2,1,0:T(8,128)(2,1)S(1)} collective-permute-done((bf16[6,128,128]{2,1,0:T(8,128)(2,1)S(1)}, bf16[6,128,128]{2,1,0:T(8,128)(2,1)S(1)}, u32[]{:S(2)}, u32[]{:S(2)}) %collective-permute-start.13) | collective-permute-done | bytes 196640 | tf_op jit(solution)/shard_map/ppermute | solution.py:562
  17.9 1.6 %collective-permute-start.14 = (bf16[6,128,128]{2,1,0:T(8,128)(2,1)S(1)}, bf16[6,128,128]{2,1,0:T(8,128)(2,1)S(1)}, u32[]{:S(2)}, u32[]{:S(2)}) collective-permute-start(bf16[6,128,128]{2,1,0:T(8,128)(2,1)S(1)} %get-tuple-element.54.refs_6_), channel_id=1, source_target_pairs={{0,8},{2,6},{8,16},{10,2},{16,24},{18,10},{24,28},{26,18},{28,20},... | collective-permute-start | bytes 589832 | tf_op jit(solution)/shard_map/ppermute | solution.py:562
  19.5 0.0 collective-permute-start.23
  19.5 0.5 collective-permute-start.20
  20.0 0.0 collective-permute-done.24.refs_18_
  20.0 0.4 collective-permute-start.16
  20.5 0.0 collective-permute-done.22.refs_16_
  20.5 0.9 %collective-permute-start.21 = (bf16[6,128,128]{2,1,0:T(8,128)(2,1)S(1)}, bf16[6,128,128]{2,1,0:T(8,128)(2,1)S(1)}, u32[]{:S(2)}, u32[]{:S(2)}) collective-permute-start(bf16[6,128,128]{2,1,0:T(8,128)(2,1)S(1)} %get-tuple-element.55.refs_7_), channel_id=1, source_target_pairs={{0,2},{2,0},{8,10},{10,8},{16,18},{18,16},{24,26},{26,24},{28,30},... | collective-permute-start | bytes 589832 | tf_op jit(solution)/shard_map/ppermute | solution.py:566
  21.4 3.2 %collective-permute-done.14.refs_4_ = bf16[6,128,128]{2,1,0:T(8,128)(2,1)S(1)} collective-permute-done((bf16[6,128,128]{2,1,0:T(8,128)(2,1)S(1)}, bf16[6,128,128]{2,1,0:T(8,128)(2,1)S(1)}, u32[]{:S(2)}, u32[]{:S(2)}) %collective-permute-start.14) | collective-permute-done | bytes 196640 | tf_op jit(solution)/shard_map/ppermute | solution.py:562
  24.6 0.0 collective-permute-start.18
  24.6 0.0 collective-permute-done.23.refs_17_
  24.6 1.6 %collective-permute-start.17 = (bf16[6,128,128]{2,1,0:T(8,128)(2,1)S(1)}, bf16[6,128,128]{2,1,0:T(8,128)(2,1)S(1)}, u32[]{:S(2)}, u32[]{:S(2)}) collective-permute-start(bf16[6,128,128]{2,1,0:T(8,128)(2,1)S(1)} %collective-permute-done.14.refs_4_), channel_id=1, source_target_pairs={{0,10},{2,4},{8,18},{10,0},{16,26},{18,8},{24,30},{26,16},{28,22},... | collective-permute-start | bytes 589832 | tf_op jit(solution)/shard_map/ppermute | solution.py:568
  26.2 0.0 collective-permute-done.20.refs_14_
  26.2 1.9 %collective-permute-start.15 = (bf16[6,128,128]{2,1,0:T(8,128)(2,1)S(1)}, bf16[6,128,128]{2,1,0:T(8,128)(2,1)S(1)}, u32[]{:S(2)}, u32[]{:S(2)}) collective-permute-start(bf16[6,128,128]{2,1,0:T(8,128)(2,1)S(1)} %collective-permute-done.14.refs_4_), channel_id=1, source_target_pairs={{0,8},{2,6},{8,16},{10,2},{16,24},{18,10},{24,28},{26,18},{28,20},... | collective-permute-start | bytes 589832 | tf_op jit(solution)/shard_map/ppermute | solution.py:567
  28.1 0.0 collective-permute-done.16.refs_5_
  28.1 0.0 collective-permute-start.19
  28.1 0.0 collective-permute-done.21.refs_15_
  28.1 0.0 collective-permute-done.18.refs_12_
  28.2 1.5 %collective-permute-done.17.refs_11_ = bf16[6,128,128]{2,1,0:T(8,128)(2,1)S(1)} collective-permute-done((bf16[6,128,128]{2,1,0:T(8,128)(2,1)S(1)}, bf16[6,128,128]{2,1,0:T(8,128)(2,1)S(1)}, u32[]{:S(2)}, u32[]{:S(2)}) %collective-permute-start.17) | collective-permute-done | bytes 196640 | tf_op jit(solution)/shard_map/ppermute | solution.py:568
  29.7 2.8 %collective-permute-done.15.refs_3_ = bf16[6,128,128]{2,1,0:T(8,128)(2,1)S(1)} collective-permute-done((bf16[6,128,128]{2,1,0:T(8,128)(2,1)S(1)}, bf16[6,128,128]{2,1,0:T(8,128)(2,1)S(1)}, u32[]{:S(2)}, u32[]{:S(2)}) %collective-permute-start.15) | collective-permute-done | bytes 196640 | tf_op jit(solution)/shard_map/ppermute | solution.py:567
  32.5 0.0 collective-permute-done.19.refs_13_
  32.5 10.8 %compute.1 = (bf16[32,128,128]{2,1,0:T(8,128)(2,1)S(1)}, bf16[16,128,128]{2,1,0:T(8,128)(2,1)S(1)}, bf16[16,128,128]{2,1,0:T(8,128)(2,1)S(1)}, bf16[32,128,128]{...) custom-call(s32[32,128]{1,0:T(8,128)S(1)} %plan.1.refs_1_.__2_.refs_, ...), custom_call_target="tpu_custom_call" | custom-call | flops 1000000000 | bytes 20000000 | tf_op jit(solution)/shard_map/compute/pallas_call | solution.py:514
  43.2 0.1 collective-permute-start.27
  43.3 0.5 collective-permute-start.26
  43.8 1.4 %collective-permute-done.27 = bf16[16,128,128]{2,1,0:T(8,128)(2,1)S(1)} collective-permute-done((bf16[16,128,128]{2,1,0:T(8,128)(2,1)S(1)}, bf16[16,128,128]{2,1,0:T(8,128)(2,1)S(1)}, u32[]{:S(2)}, u32[]{:S(2)}) %collective-permute-start.27) | collective-permute-done | bytes 524320 | tf_op jit(solution)/shard_map/ppermute | solution.py:630
  45.2 0.1 add_convert_fusion.13
  45.3 1.6 %collective-permute-start.28 = (bf16[4,128,128]{2,1,0:T(8,128)(2,1)S(1)}, bf16[4,128,128]{2,1,0:T(8,128)(2,1)S(1)}, u32[]{:S(2)}, u32[]{:S(2)}) collective-permute-start(bf16[4,128,128]{2,1,0:T(8,128)(2,1)S(1)} %get-tuple-element.65), channel_id=1, source_target_pairs={{0,8},{2,6},{8,16},{10,2},{16,24},{18,10},{24,28},{26,18},{28,20},... | collective-permute-start | bytes 393224 | tf_op jit(solution)/shard_map/ppermute | solution.py:587
  46.9 0.5 collective-permute-start.29
  47.4 4.3 %collective-permute-done.28 = bf16[4,128,128]{2,1,0:T(8,128)(2,1)S(1)} collective-permute-done((bf16[4,128,128]{2,1,0:T(8,128)(2,1)S(1)}, bf16[4,128,128]{2,1,0:T(8,128)(2,1)S(1)}, u32[]{:S(2)}, u32[]{:S(2)}) %collective-permute-start.28) | collective-permute-done | bytes 131104 | tf_op jit(solution)/shard_map/ppermute | solution.py:587
  51.7 0.1 collective-permute-done.29
  51.8 0.1 add_convert_fusion.11
  51.9 2.0 %collective-permute-start.30 = (bf16[4,128,128]{2,1,0:T(8,128)(2,1)S(1)}, bf16[4,128,128]{2,1,0:T(8,128)(2,1)S(1)}, u32[]{:S(2)}, u32[]{:S(2)}) collective-permute-start(bf16[4,128,128]{2,1,0:T(8,128)(2,1)S(1)} %get-tuple-element.67), channel_id=1, source_target_pairs={{0,8},{2,6},{8,16},{10,2},{16,24},{18,10},{24,28},{26,18},{28,20},... | collective-permute-start | bytes 393224 | tf_op jit(solution)/shard_map/ppermute | solution.py:587
  53.9 0.1 collective-permute-start.31
  54.0 0.1 collective-permute-start.25
  54.1 0.0 collective-permute-done.26
  54.1 3.9 %collective-permute-done.30 = bf16[4,128,128]{2,1,0:T(8,128)(2,1)S(1)} collective-permute-done((bf16[4,128,128]{2,1,0:T(8,128)(2,1)S(1)}, bf16[4,128,128]{2,1,0:T(8,128)(2,1)S(1)}, u32[]{:S(2)}, u32[]{:S(2)}) %collective-permute-start.30) | collective-permute-done | bytes 131104 | tf_op jit(solution)/shard_map/ppermute | solution.py:587
  58.0 0.9 %collective-permute-done.31 = bf16[4,128,128]{2,1,0:T(8,128)(2,1)S(1)} collective-permute-done((bf16[4,128,128]{2,1,0:T(8,128)(2,1)S(1)}, bf16[4,128,128]{2,1,0:T(8,128)(2,1)S(1)}, u32[]{:S(2)}, u32[]{:S(2)}) %collective-permute-start.31) | collective-permute-done | bytes 131104 | tf_op jit(solution)/shard_map/ppermute | solution.py:587
  58.9 0.1 convert_add_fusion
  59.0 1.6 %collective-permute-start.32 = (bf16[4,128,128]{2,1,0:T(8,128)(2,1)S(1)}, bf16[4,128,128]{2,1,0:T(8,128)(2,1)S(1)}, u32[]{:S(2)}, u32[]{:S(2)}) collective-permute-start(bf16[4,128,128]{2,1,0:T(8,128)(2,1)S(1)} %get-tuple-element.69), channel_id=1, source_target_pairs={{0,8},{2,6},{8,16},{10,2},{16,24},{18,10},{24,28},{26,18},{28,20},... | collective-permute-start | bytes 393224 | tf_op jit(solution)/shard_map/ppermute | solution.py:587
  61.3 0.5 collective-permute-start.34
  61.8 3.3 %collective-permute-done.32 = bf16[4,128,128]{2,1,0:T(8,128)(2,1)S(1)} collective-permute-done((bf16[4,128,128]{2,1,0:T(8,128)(2,1)S(1)}, bf16[4,128,128]{2,1,0:T(8,128)(2,1)S(1)}, u32[]{:S(2)}, u32[]{:S(2)}) %collective-permute-start.32) | collective-permute-done | bytes 131104 | tf_op jit(solution)/shard_map/ppermute | solution.py:587
  65.2 0.1 add_convert_fusion.8.__0_
  65.2 1.0 %collective-permute-start.33 = (bf16[4,128,128]{2,1,0:T(8,128)(2,1)S(1)}, bf16[4,128,128]{2,1,0:T(8,128)(2,1)S(1)}, u32[]{:S(2)}, u32[]{:S(2)}) collective-permute-start(bf16[4,128,128]{2,1,0:T(8,128)(2,1)S(1)} %get-tuple-element.75), channel_id=1, source_target_pairs={{0,8},{2,6},{8,16},{10,2},{16,24},{18,10},{24,28},{26,18},{28,20},... | collective-permute-start | bytes 393224 | tf_op jit(solution)/shard_map/ppermute | solution.py:591
  66.3 1.2 %collective-permute-done.25.refs_3_ = bf16[16,128,128]{2,1,0:T(8,128)(2,1)S(1)} collective-permute-done((bf16[16,128,128]{2,1,0:T(8,128)(2,1)}, bf16[16,128,128]{2,1,0:T(8,128)(2,1)S(1)}, u32[]{:S(2)}, u32[]{:S(2)}) %collective-permute-start.25) | collective-permute-done | bytes 524320 | tf_op jit(solution)/shard_map/ppermute | solution.py:628
  67.5 2.6 %join.1 = (bf16[128,4096]{1,0:T(8,128)(2,1)}, bf16[128,4096]{1,0:T(8,128)(2,1)}) custom-call(s32[32,128]{1,0:T(8,128)S(1)} %plan.1.refs_1_.__2_.refs_0_, s32[8,128]{1,0:T(8,128)S(1)} %get-tuple-element.51.__2_.refs_1_, bf16[16,128,128]{2,1,0:T(8,128)(2,1)S(1)} %get-tuple-element.56.refs_2_, bf16[16,128,128]{2,1,0:T(8,128)(2,1)S(1)} %collective-permute-done.25.refs_3_, ...), custom_call_target="tpu_custom_call" | custom-call | flops 1000000 | bytes 6000000 | tf_op jit(solution)/shard_map/join/pallas_call | solution.py:532
  70.1 0.0 collective-permute-done.34.behind
  70.1 0.1 collective-permute-done.33.ahead
  70.3 1.5 %finish.1 = (bf16[1,2,128,128]{3,2,1,0:T(8,128)(2,1)}, bf16[1,2,128,128]{3,2,1,0:T(8,128)(2,1)}, bf16[1,2,128,128]{3,2,1,0:T(8,128)(2,1)}) custom-call(s32[32,128]{1,0:T(8,128)S(1)} %plan.1.refs_1_.__2_.refs_0_, f32[4,128,128]{2,1,0:T(8,128)S(1)} %get-tuple-element.87.here, bf16[4,128,128]{2,1,0:T(8,128)(2,1)S(1)} %collective-permute-done.33.ahead, ...), custom_call_target="tpu_custom_call" | custom-call | flops 1000000 | bytes 1000000 | tf_op jit(solution)/shard_map/finish/pallas_call | solution.py:546
  (5 shorter events, 0.0 us)
Async XLA Ops:
  1.6 8.3 %collective-permute-start.11 = (bf16[6,128,128]{2,1,0:T(8,128)(2,1)S(1)}, bf16[6,128,128]{2,1,0:T(8,128)(2,1)S(1)}, u32[]{:S(2)}, u32[]{:S(2)}) collective-permute-start(bf16[6,128,128]{2,1,0:T(8,128)(2,1)S(1)} %pad_maximum_fusion.refs_10_), channel_id=1, source_target_pairs={{0,4},{2,10},{8,0},{10,18},{16,8},{18,26},{24,16},{26,30},{28,24},... | collective-permute-start | bytes 589832 | tf_op jit(solution)/shard_map/ppermute | solution.py:562
  4.6 5.7 %collective-permute-start.10 = (bf16[6,128,128]{2,1,0:T(8,128)(2,1)S(1)}, bf16[6,128,128]{2,1,0:T(8,128)(2,1)S(1)}, u32[]{:S(2)}, u32[]{:S(2)}) collective-permute-start(bf16[6,128,128]{2,1,0:T(8,128)(2,1)S(1)} %pad_maximum_fusion.refs_10_), channel_id=1, source_target_pairs={{0,8},{2,6},{8,16},{10,2},{16,24},{18,10},{24,28},{26,18},{28,20},... | collective-permute-start | bytes 589832 | tf_op jit(solution)/shard_map/ppermute | solution.py:562
  10.3 6.9 %collective-permute-start.12 = (bf16[6,128,128]{2,1,0:T(8,128)(2,1)S(1)}, bf16[6,128,128]{2,1,0:T(8,128)(2,1)S(1)}, u32[]{:S(2)}, u32[]{:S(2)}) collective-permute-start(bf16[6,128,128]{2,1,0:T(8,128)(2,1)S(1)} %get-tuple-element.52.refs_8_), channel_id=1, source_target_pairs={{0,8},{2,6},{8,16},{10,2},{16,24},{18,10},{24,28},{26,18},{28,20},... | collective-permute-start | bytes 589832 | tf_op jit(solution)/shard_map/ppermute | solution.py:562
  12.3 5.7 %collective-permute-start.13 = (bf16[6,128,128]{2,1,0:T(8,128)(2,1)S(1)}, bf16[6,128,128]{2,1,0:T(8,128)(2,1)S(1)}, u32[]{:S(2)}, u32[]{:S(2)}) collective-permute-start(bf16[6,128,128]{2,1,0:T(8,128)(2,1)S(1)} %get-tuple-element.53.refs_9_), channel_id=1, source_target_pairs={{0,4},{2,10},{8,0},{10,18},{16,8},{18,26},{24,16},{26,30},{28,24},... | collective-permute-start | bytes 589832 | tf_op jit(solution)/shard_map/ppermute | solution.py:562
  12.3 7.7 %collective-permute-start.24 = (bf16[6,128,128]{2,1,0:T(8,128)(2,1)S(1)}, bf16[6,128,128]{2,1,0:T(8,128)(2,1)S(1)}, u32[]{:S(2)}, u32[]{:S(2)}) collective-permute-start(bf16[6,128,128]{2,1,0:T(8,128)(2,1)S(1)} %pad_maximum_fusion.refs_10_), channel_id=1, source_target_pairs={{0,2},{2,0},{8,10},{10,8},{16,18},{18,16},{24,26},{26,24},{28,30},... | collective-permute-start | bytes 589832 | tf_op jit(solution)/shard_map/ppermute | solution.py:566
  12.3 3.5 %collective-permute-start.9 = (s32[1,128]{1,0:T(1,128)S(1)}, s32[1,128]{1,0:T(1,128)S(1)}, u32[]{:S(2)}, u32[]{:S(2)}) collective-permute-start(s32[1,128]{1,0:T(1,128)S(1)} %pad_bitcast_fusion.own.refs_0_), channel_id=1, source_target_pairs={{0,1},{1,0},{2,3},{3,2},{4,5},{5,4},{6,7},{7,6},{8,9},{9,8},{10,11... | collective-permute-start | bytes 1544 | tf_op jit(solution)/shard_map/ppermute | solution.py:618
  16.7 3.8 %collective-permute-start.22 = (bf16[6,128,128]{2,1,0:T(8,128)(2,1)S(1)}, bf16[6,128,128]{2,1,0:T(8,128)(2,1)S(1)}, u32[]{:S(2)}, u32[]{:S(2)}) collective-permute-start(bf16[6,128,128]{2,1,0:T(8,128)(2,1)S(1)} %get-tuple-element.52.refs_8_), channel_id=1, source_target_pairs={{0,2},{2,0},{8,10},{10,8},{16,18},{18,16},{24,26},{26,24},{28,30},... | collective-permute-start | bytes 589832 | tf_op jit(solution)/shard_map/ppermute | solution.py:566
  17.9 6.6 %collective-permute-start.14 = (bf16[6,128,128]{2,1,0:T(8,128)(2,1)S(1)}, bf16[6,128,128]{2,1,0:T(8,128)(2,1)S(1)}, u32[]{:S(2)}, u32[]{:S(2)}) collective-permute-start(bf16[6,128,128]{2,1,0:T(8,128)(2,1)S(1)} %get-tuple-element.54.refs_6_), channel_id=1, source_target_pairs={{0,8},{2,6},{8,16},{10,2},{16,24},{18,10},{24,28},{26,18},{28,20},... | collective-permute-start | bytes 589832 | tf_op jit(solution)/shard_map/ppermute | solution.py:562
  19.5 5.1 %collective-permute-start.23 = (bf16[6,128,128]{2,1,0:T(8,128)(2,1)S(1)}, bf16[6,128,128]{2,1,0:T(8,128)(2,1)S(1)}, u32[]{:S(2)}, u32[]{:S(2)}) collective-permute-start(bf16[6,128,128]{2,1,0:T(8,128)(2,1)S(1)} %get-tuple-element.53.refs_9_), channel_id=1, source_target_pairs={{0,2},{2,0},{8,10},{10,8},{16,18},{18,16},{24,26},{26,24},{28,30},... | collective-permute-start | bytes 589832 | tf_op jit(solution)/shard_map/ppermute | solution.py:566
  19.5 6.7 %collective-permute-start.20 = (bf16[6,128,128]{2,1,0:T(8,128)(2,1)S(1)}, bf16[6,128,128]{2,1,0:T(8,128)(2,1)S(1)}, u32[]{:S(2)}, u32[]{:S(2)}) collective-permute-start(bf16[6,128,128]{2,1,0:T(8,128)(2,1)S(1)} %get-tuple-element.54.refs_6_), channel_id=1, source_target_pairs={{0,2},{2,0},{8,10},{10,8},{16,18},{18,16},{24,26},{26,24},{28,30},... | collective-permute-start | bytes 589832 | tf_op jit(solution)/shard_map/ppermute | solution.py:566
  20.0 8.1 %collective-permute-start.16 = (bf16[6,128,128]{2,1,0:T(8,128)(2,1)S(1)}, bf16[6,128,128]{2,1,0:T(8,128)(2,1)S(1)}, u32[]{:S(2)}, u32[]{:S(2)}) collective-permute-start(bf16[6,128,128]{2,1,0:T(8,128)(2,1)S(1)} %get-tuple-element.55.refs_7_), channel_id=1, source_target_pairs={{0,4},{2,10},{8,0},{10,18},{16,8},{18,26},{24,16},{26,30},{28,24},... | collective-permute-start | bytes 589832 | tf_op jit(solution)/shard_map/ppermute | solution.py:562
  20.5 7.7 %collective-permute-start.21 = (bf16[6,128,128]{2,1,0:T(8,128)(2,1)S(1)}, bf16[6,128,128]{2,1,0:T(8,128)(2,1)S(1)}, u32[]{:S(2)}, u32[]{:S(2)}) collective-permute-start(bf16[6,128,128]{2,1,0:T(8,128)(2,1)S(1)} %get-tuple-element.55.refs_7_), channel_id=1, source_target_pairs={{0,2},{2,0},{8,10},{10,8},{16,18},{18,16},{24,26},{26,24},{28,30},... | collective-permute-start | bytes 589832 | tf_op jit(solution)/shard_map/ppermute | solution.py:566
  24.6 3.6 %collective-permute-start.18 = (bf16[6,128,128]{2,1,0:T(8,128)(2,1)S(1)}, bf16[6,128,128]{2,1,0:T(8,128)(2,1)S(1)}, u32[]{:S(2)}, u32[]{:S(2)}) collective-permute-start(bf16[6,128,128]{2,1,0:T(8,128)(2,1)S(1)} %collective-permute-done.14.refs_4_), channel_id=1, source_target_pairs={{0,2},{2,0},{8,10},{10,8},{16,18},{18,16},{24,26},{26,24},{28,30},... | collective-permute-start | bytes 589832 | tf_op jit(solution)/shard_map/ppermute | solution.py:566
  24.6 5.1 %collective-permute-start.17 = (bf16[6,128,128]{2,1,0:T(8,128)(2,1)S(1)}, bf16[6,128,128]{2,1,0:T(8,128)(2,1)S(1)}, u32[]{:S(2)}, u32[]{:S(2)}) collective-permute-start(bf16[6,128,128]{2,1,0:T(8,128)(2,1)S(1)} %collective-permute-done.14.refs_4_), channel_id=1, source_target_pairs={{0,10},{2,4},{8,18},{10,0},{16,26},{18,8},{24,30},{26,16},{28,22},... | collective-permute-start | bytes 589832 | tf_op jit(solution)/shard_map/ppermute | solution.py:568
  26.2 6.3 %collective-permute-start.15 = (bf16[6,128,128]{2,1,0:T(8,128)(2,1)S(1)}, bf16[6,128,128]{2,1,0:T(8,128)(2,1)S(1)}, u32[]{:S(2)}, u32[]{:S(2)}) collective-permute-start(bf16[6,128,128]{2,1,0:T(8,128)(2,1)S(1)} %collective-permute-done.14.refs_4_), channel_id=1, source_target_pairs={{0,8},{2,6},{8,16},{10,2},{16,24},{18,10},{24,28},{26,18},{28,20},... | collective-permute-start | bytes 589832 | tf_op jit(solution)/shard_map/ppermute | solution.py:567
  28.1 4.3 %collective-permute-start.19 = (bf16[6,128,128]{2,1,0:T(8,128)(2,1)S(1)}, bf16[6,128,128]{2,1,0:T(8,128)(2,1)S(1)}, u32[]{:S(2)}, u32[]{:S(2)}) collective-permute-start(bf16[6,128,128]{2,1,0:T(8,128)(2,1)S(1)} %collective-permute-done.16.refs_5_), channel_id=1, source_target_pairs={{0,2},{2,0},{8,10},{10,8},{16,18},{18,16},{24,26},{26,24},{28,30},... | collective-permute-start | bytes 589832 | tf_op jit(solution)/shard_map/ppermute | solution.py:566
  43.2 2.0 %collective-permute-start.27 = (bf16[16,128,128]{2,1,0:T(8,128)(2,1)S(1)}, bf16[16,128,128]{2,1,0:T(8,128)(2,1)S(1)}, u32[]{:S(2)}, u32[]{:S(2)}) collective-permute-start(bf16[16,128,128]{2,1,0:T(8,128)(2,1)S(1)} %get-tuple-element.64), channel_id=1, source_target_pairs={{0,2},{2,0},{8,10},{10,8},{16,18},{18,16},{24,26},{26,24},{28,30},... | collective-permute-start | bytes 1572872 | tf_op jit(solution)/shard_map/ppermute | solution.py:630
  43.3 10.8 %collective-permute-start.26 = (bf16[16,128,128]{2,1,0:T(8,128)(2,1)S(1)}, bf16[16,128,128]{2,1,0:T(8,128)(2,1)S(1)}, u32[]{:S(2)}, u32[]{:S(2)}) collective-permute-start(bf16[16,128,128]{2,1,0:T(8,128)(2,1)S(1)} %get-tuple-element.63), channel_id=1, source_target_pairs={{0,2},{2,0},{8,10},{10,8},{16,18},{18,16},{24,26},{26,24},{28,30},... | collective-permute-start | bytes 1572872 | tf_op jit(solution)/shard_map/ppermute | solution.py:630
  45.3 6.4 %collective-permute-start.28 = (bf16[4,128,128]{2,1,0:T(8,128)(2,1)S(1)}, bf16[4,128,128]{2,1,0:T(8,128)(2,1)S(1)}, u32[]{:S(2)}, u32[]{:S(2)}) collective-permute-start(bf16[4,128,128]{2,1,0:T(8,128)(2,1)S(1)} %get-tuple-element.65), channel_id=1, source_target_pairs={{0,8},{2,6},{8,16},{10,2},{16,24},{18,10},{24,28},{26,18},{28,20},... | collective-permute-start | bytes 393224 | tf_op jit(solution)/shard_map/ppermute | solution.py:587
  46.9 5.0 %collective-permute-start.29 = (bf16[4,128,128]{2,1,0:T(8,128)(2,1)S(1)}, bf16[4,128,128]{2,1,0:T(8,128)(2,1)S(1)}, u32[]{:S(2)}, u32[]{:S(2)}) collective-permute-start(bf16[4,128,128]{2,1,0:T(8,128)(2,1)S(1)} %get-tuple-element.66), channel_id=1, source_target_pairs={{0,4},{2,10},{8,0},{10,18},{16,8},{18,26},{24,16},{26,30},{28,24},... | collective-permute-start | bytes 393224 | tf_op jit(solution)/shard_map/ppermute | solution.py:587
  51.9 6.1 %collective-permute-start.30 = (bf16[4,128,128]{2,1,0:T(8,128)(2,1)S(1)}, bf16[4,128,128]{2,1,0:T(8,128)(2,1)S(1)}, u32[]{:S(2)}, u32[]{:S(2)}) collective-permute-start(bf16[4,128,128]{2,1,0:T(8,128)(2,1)S(1)} %get-tuple-element.67), channel_id=1, source_target_pairs={{0,8},{2,6},{8,16},{10,2},{16,24},{18,10},{24,28},{26,18},{28,20},... | collective-permute-start | bytes 393224 | tf_op jit(solution)/shard_map/ppermute | solution.py:587
  53.9 5.0 %collective-permute-start.31 = (bf16[4,128,128]{2,1,0:T(8,128)(2,1)S(1)}, bf16[4,128,128]{2,1,0:T(8,128)(2,1)S(1)}, u32[]{:S(2)}, u32[]{:S(2)}) collective-permute-start(bf16[4,128,128]{2,1,0:T(8,128)(2,1)S(1)} %get-tuple-element.68), channel_id=1, source_target_pairs={{0,4},{2,10},{8,0},{10,18},{16,8},{18,26},{24,16},{26,30},{28,24},... | collective-permute-start | bytes 393224 | tf_op jit(solution)/shard_map/ppermute | solution.py:587
  54.0 13.5 %collective-permute-start.25 = (bf16[16,128,128]{2,1,0:T(8,128)(2,1)}, bf16[16,128,128]{2,1,0:T(8,128)(2,1)S(1)}, u32[]{:S(2)}, u32[]{:S(2)}) collective-permute-start(bf16[16,128,128]{2,1,0:T(8,128)(2,1)} %get-tuple-element.57), channel_id=1, source_target_pairs={{0,1},{1,0},{2,3},{3,2},{4,5},{5,4},{6,7},{7,6},{8,9},{9,8},{10,11... | collective-permute-start | bytes 1572872 | tf_op jit(solution)/shard_map/ppermute | solution.py:628
  59.0 6.1 %collective-permute-start.32 = (bf16[4,128,128]{2,1,0:T(8,128)(2,1)S(1)}, bf16[4,128,128]{2,1,0:T(8,128)(2,1)S(1)}, u32[]{:S(2)}, u32[]{:S(2)}) collective-permute-start(bf16[4,128,128]{2,1,0:T(8,128)(2,1)S(1)} %get-tuple-element.69), channel_id=1, source_target_pairs={{0,8},{2,6},{8,16},{10,2},{16,24},{18,10},{24,28},{26,18},{28,20},... | collective-permute-start | bytes 393224 | tf_op jit(solution)/shard_map/ppermute | solution.py:587
  61.3 8.8 %collective-permute-start.34 = (bf16[4,128,128]{2,1,0:T(8,128)(2,1)S(1)}, bf16[4,128,128]{2,1,0:T(8,128)(2,1)S(1)}, u32[]{:S(2)}, u32[]{:S(2)}) collective-permute-start(bf16[4,128,128]{2,1,0:T(8,128)(2,1)S(1)} %get-tuple-element.76), channel_id=1, source_target_pairs={{0,4},{2,10},{8,0},{10,18},{16,8},{18,26},{24,16},{26,30},{28,24},... | collective-permute-start | bytes 393224 | tf_op jit(solution)/shard_map/ppermute | solution.py:587
  65.2 5.0 %collective-permute-start.33 = (bf16[4,128,128]{2,1,0:T(8,128)(2,1)S(1)}, bf16[4,128,128]{2,1,0:T(8,128)(2,1)S(1)}, u32[]{:S(2)}, u32[]{:S(2)}) collective-permute-start(bf16[4,128,128]{2,1,0:T(8,128)(2,1)S(1)} %get-tuple-element.75), channel_id=1, source_target_pairs={{0,8},{2,6},{8,16},{10,2},{16,24},{18,10},{24,28},{26,18},{28,20},... | collective-permute-start | bytes 393224 | tf_op jit(solution)/shard_map/ppermute | solution.py:591
